TPU v7x, 32 devices: a whole 2x2x4 slice. The times are simulated.
32 devices in a mesh: row: 2 (over y), col: 16 (over z, x, core).
Axes of the slice: x: 2, y: 2, z: 4, core: 2. Of those that a mesh axis runs over, the one named last changes fastest.
Arguments:
- feature_map: bfloat16 [128, 128, 64], P('row', 'col'), may hold values from -6 to 6
- first_conv_weight: bfloat16 [3, 3, 64, 64], replicated, may hold values from -0.25 to 0.25
- first_conv_bias: float32 [64], replicated, may hold values from -3 to 3
- second_conv_weight: bfloat16 [3, 3, 64, 64], replicated, may hold values from -0.25 to 0.25
- second_conv_bias: float32 [64], replicated, may hold values from -3 to 3
- cotangent: bfloat16 [128, 128, 64], P('row', 'col'), may hold values from -6 to 6
Outputs:
- output: bfloat16 [128, 128, 64], P('row', 'col')
- grad_input: bfloat16 [128, 128, 64], P('row', 'col')
All inputs are finite; a program needn't handle non-finite values.
Results may differ from a plain program's by a relative error of at most 0.0058.
Values may be sent and summed in bfloat16 or wider, within the bound.
No kernel may reach another device: no remote copies, remote signals or barrier semaphores. Data moves between devices by JAX's collectives and lax.ppermute only.
A program may use at most 64 MiB of HBM per device.

v0:
```python
import jax
import jax.numpy as jnp
from jax import lax
from jax.sharding import PartitionSpec as P

DILATION_STEP = 4


root_half = 0.7071067811865476
inv_root_tau = 0.3989422804014327


def with_halo(array, sides, width):
    for axis, dim in sides:
        size, length = (lax.axis_size(axis), array.shape[dim])
        up = [(i, (i + 1) % size) for i in range(size - 1)]
        down = [(j, i) for i, j in up]
        last = lax.slice_in_dim(array, length - width, length, axis=dim)
        first = lax.slice_in_dim(array, 0, width, axis=dim)
        before = lax.ppermute(last, axis, up)
        after = lax.ppermute(first, axis, down)
        array = jnp.concatenate([before, array, after], axis=dim)
    return array


def gelu_value(value_array):
    return 0.5 * value_array * (1.0 + lax.erf(value_array * root_half))


def gelu_slope(value_array):
    return (
        0.5 * (1.0 + lax.erf(value_array * root_half))
        + value_array * jnp.exp(-0.5 * value_array * value_array) * inv_root_tau
    )


def dilated_conv(padded_input, conv_kernel):
    return lax.conv_general_dilated(
        padded_input[None],
        conv_kernel,
        (1, 1),
        "VALID",
        rhs_dilation=(DILATION_STEP, DILATION_STEP),
        dimension_numbers=("NHWC", "HWIO", "NHWC"),
        preferred_element_type=jnp.float32,
    )[0]


def reversed_kernel(conv_kernel):
    return jnp.transpose(conv_kernel[::-1, ::-1], (0, 1, 3, 2))


def extend(value_array):
    return with_halo(value_array, (("row", 0), ("col", 1)), DILATION_STEP)


def mirror_rows(stack):
    row_count = lax.axis_size("row")
    col_count = lax.axis_size("col")
    count, tile_rows, tile_cols, channels = stack.shape
    unit_len = tile_rows // col_count
    col_ratio = col_count // row_count
    spread_parts = stack.reshape(count, 1, col_ratio, row_count, unit_len, tile_cols * channels)
    spread_parts = lax.all_to_all(spread_parts, "row", split_axis=3, concat_axis=1, tiled=True)
    across_parts = spread_parts.reshape(count, col_count, unit_len, 1, tile_cols * channels)
    across_parts = lax.all_to_all(across_parts, "col", split_axis=1, concat_axis=3, tiled=True)
    settle_parts = across_parts.reshape(count, 1, unit_len, row_count, tile_rows * channels)
    settle_parts = lax.all_to_all(settle_parts, "row", split_axis=3, concat_axis=1, tiled=True)
    turned = settle_parts.reshape(count, tile_cols, tile_rows, channels)
    return jnp.transpose(turned, (0, 2, 1, 3))


def mirror(stack):
    return mirror_rows(stack)


def branch(symmetric_padding, kernel_first, kernel_second, bias_first, bias_second):
    pre_first = dilated_conv(symmetric_padding, kernel_first) + bias_first
    hidden = gelu_value(pre_first).astype(jnp.bfloat16)
    second_preactivation = dilated_conv(extend(hidden), kernel_second) + bias_second
    return (pre_first, second_preactivation)


def backward(gradient, pre_first, second_preactivation, kernel_first, kernel_second):
    grad_second = (gradient.astype(jnp.float32) * gelu_slope(second_preactivation)).astype(
        jnp.bfloat16
    )
    hidden_gradient = dilated_conv(extend(grad_second), reversed_kernel(kernel_second))
    grad_first = (hidden_gradient * gelu_slope(pre_first)).astype(jnp.bfloat16)
    total_sum = gradient.astype(jnp.float32) + dilated_conv(
        extend(grad_first), reversed_kernel(kernel_first)
    )
    return total_sum.astype(jnp.bfloat16)


def per_device(
    feature_map, first_conv_weight, first_conv_bias, second_conv_weight, second_conv_bias, cotangent
):
    mirrored = mirror(feature_map[None])[0]
    symmetric = (feature_map.astype(jnp.float32) + mirrored.astype(jnp.float32)).astype(
        jnp.bfloat16
    )
    symmetric_padding = extend(symmetric)
    pre_first, second_preactivation = branch(
        symmetric_padding, first_conv_weight, second_conv_weight, first_conv_bias, second_conv_bias
    )
    output = (symmetric.astype(jnp.float32) + gelu_value(second_preactivation)).astype(jnp.bfloat16)
    grad_sym = backward(
        cotangent, pre_first, second_preactivation, first_conv_weight, second_conv_weight
    )
    grad_turned = mirror(grad_sym[None])[0]
    grad_input = (grad_sym.astype(jnp.float32) + grad_turned.astype(jnp.float32)).astype(
        jnp.bfloat16
    )
    return (output, grad_input)


def solution(mesh):
    in_specs = (P("row", "col", None), P(), P(), P(), P(), P("row", "col", None))
    out_specs = (P("row", "col", None), P("row", "col", None))
    return jax.shard_map(
        per_device, mesh=mesh, in_specs=in_specs, out_specs=out_specs, check_vma=False
    )
```

profile of v0, /device:TPU:0, one launch (start us, length us, event | category | flops | bytes accessed | tf_op | source)
XLA Modules:
  0.0 126.5 jit_solution(9464798538705142603)
XLA Ops:
  0.6 0.0 copy-start
  0.6 1.1 reshape_broadcast_in_dim.6
  1.8 8.2 %all_to_all.84 = bf16[1,1,8,2,4,512]{5,4,2,1,0,3:T(4,128)(2,1)S(1)} all-to-all(bf16[1,1,8,2,4,512]{5,4,2,1,0,3:T(4,128)(2,1)S(1)} %copy.32), channel_id=1, replica_groups=mesh['row'=2,'col'=16] {'row'}, dimensions={3} | all-to-all | bytes 131072 | tf_op jit(solution)/shard_map/all_to_all | solution.py:64
  9.9 0.1 copy.34
  10.0 12.6 %all_to_all.85 = bf16[1,16,4,1,512]{4,2,3,0,1:T(4,128)(2,1)S(1)} all-to-all(bf16[1,16,4,1,512]{4,2,3,0,1:T(4,128)(2,1)S(1)} %copy.34), channel_id=1, replica_groups=mesh['row'=2,'col'=16] {'col'}, dimensions={1} | all-to-all | bytes 131072 | tf_op jit(solution)/shard_map/all_to_all | solution.py:66
  22.7 0.1 copy.36
  22.7 6.5 %all_to_all.86 = bf16[1,1,4,2,4096]{4,2,1,0,3:T(4,128)(2,1)S(1)} all-to-all(bf16[1,1,4,2,4096]{4,2,1,0,3:T(4,128)(2,1)S(1)} %copy.36), channel_id=1, replica_groups=mesh['row'=2,'col'=16] {'row'}, dimensions={3} | all-to-all | bytes 131072 | tf_op jit(solution)/shard_map/all_to_all | solution.py:68
  29.2 0.0 copy-start.1
  29.2 0.2 reshape.40
  29.4 0.7 copy-done.1
  30.1 0.2 fusion.21
  30.3 1.9 %collective-permute-start = (bf16[4,8,64]{2,1,0:T(8,128)(2,1)S(1)}, bf16[4,8,64]{2,1,0:T(8,128)(2,1)S(1)}, u32[]{:S(2)}, u32[]{:S(2)}) collective-permute-start(bf16[4,8,64]{2,1,0:T(8,128)(2,1)S(1)} %get-tuple-element.18), channel_id=1, source_target_pairs={{0,16},{1,17},{2,18},{3,19},{4,20},{5,21},{6,22},{7,23},{8,24},{9,... | collective-permute-start | bytes 12296 | tf_op jit(solution)/shard_map/ppermute | solution.py:20
  32.2 1.3 %collective-permute-start.1 = (bf16[4,8,64]{2,1,0:T(8,128)(2,1)S(1)}, bf16[4,8,64]{2,1,0:T(8,128)(2,1)S(1)}, u32[]{:S(2)}, u32[]{:S(2)}) collective-permute-start(bf16[4,8,64]{2,1,0:T(8,128)(2,1)S(1)} %get-tuple-element.19), channel_id=1, source_target_pairs={{16,0},{17,1},{18,2},{19,3},{20,4},{21,5},{22,6},{23,7},{24,8},{25... | collective-permute-start | bytes 12296 | tf_op jit(solution)/shard_map/ppermute | solution.py:21
  33.5 0.0 collective-permute-done
  33.6 4.2 %collective-permute-done.1 = bf16[4,8,64]{2,1,0:T(8,128)(2,1)S(1)} collective-permute-done((bf16[4,8,64]{2,1,0:T(8,128)(2,1)S(1)}, bf16[4,8,64]{2,1,0:T(8,128)(2,1)S(1)}, u32[]{:S(2)}, u32[]{:S(2)}) %collective-permute-start.1) | collective-permute-done | bytes 4128 | tf_op jit(solution)/shard_map/ppermute | solution.py:21
  37.8 0.1 fusion.25
  37.9 1.3 %collective-permute-start.2 = (bf16[72,4,64]{2,1,0:T(4,128)(2,1)S(1)}, bf16[72,4,64]{2,1,0:T(4,128)(2,1)S(1)}, u32[]{:S(2)}, u32[]{:S(2)}) collective-permute-start(bf16[72,4,64]{2,1,0:T(4,128)(2,1)S(1)} %get-tuple-element.10), channel_id=1, source_target_pairs={{0,1},{1,2},{2,3},{3,4},{4,5},{5,6},{6,7},{7,8},{8,9},{9,10},{10,1... | collective-permute-start | bytes 110600 | tf_op jit(solution)/shard_map/ppermute | solution.py:20
  39.2 1.4 %collective-permute-start.3 = (bf16[72,4,64]{2,1,0:T(4,128)(2,1)S(1)}, bf16[72,4,64]{2,1,0:T(4,128)(2,1)S(1)}, u32[]{:S(2)}, u32[]{:S(2)}) collective-permute-start(bf16[72,4,64]{2,1,0:T(4,128)(2,1)S(1)} %get-tuple-element.11), channel_id=1, source_target_pairs={{1,0},{2,1},{3,2},{4,3},{5,4},{6,5},{7,6},{8,7},{9,8},{10,9},{11,1... | collective-permute-start | bytes 110600 | tf_op jit(solution)/shard_map/ppermute | solution.py:21
  40.6 2.2 %collective-permute-done.3 = bf16[72,4,64]{2,1,0:T(4,128)(2,1)S(1)} collective-permute-done((bf16[72,4,64]{2,1,0:T(4,128)(2,1)S(1)}, bf16[72,4,64]{2,1,0:T(4,128)(2,1)S(1)}, u32[]{:S(2)}, u32[]{:S(2)}) %collective-permute-start.3) | collective-permute-done | bytes 36896 | tf_op jit(solution)/shard_map/ppermute | solution.py:21
  42.8 0.2 maximum_bitcast_fusion
  43.0 1.0 fusion
  44.1 0.6 copy-done.3
  44.7 0.1 multiply_convert_fusion
  44.8 1.6 %collective-permute-start.4 = (bf16[4,8,64]{2,1,0:T(8,128)(2,1)S(1)}, bf16[4,8,64]{2,1,0:T(8,128)(2,1)S(1)}, u32[]{:S(2)}, u32[]{:S(2)}) collective-permute-start(bf16[4,8,64]{2,1,0:T(8,128)(2,1)S(1)} %get-tuple-element.16), channel_id=1, source_target_pairs={{0,16},{1,17},{2,18},{3,19},{4,20},{5,21},{6,22},{7,23},{8,24},{9,... | collective-permute-start | bytes 12296 | tf_op jit(solution)/shard_map/ppermute | solution.py:20
  46.5 1.3 %collective-permute-start.5 = (bf16[4,8,64]{2,1,0:T(8,128)(2,1)S(1)}, bf16[4,8,64]{2,1,0:T(8,128)(2,1)S(1)}, u32[]{:S(2)}, u32[]{:S(2)}) collective-permute-start(bf16[4,8,64]{2,1,0:T(8,128)(2,1)S(1)} %get-tuple-element.17), channel_id=1, source_target_pairs={{16,0},{17,1},{18,2},{19,3},{20,4},{21,5},{22,6},{23,7},{24,8},{25... | collective-permute-start | bytes 12296 | tf_op jit(solution)/shard_map/ppermute | solution.py:21
  47.8 0.0 collective-permute-done.4
  47.8 4.2 %collective-permute-done.5 = bf16[4,8,64]{2,1,0:T(8,128)(2,1)S(1)} collective-permute-done((bf16[4,8,64]{2,1,0:T(8,128)(2,1)S(1)}, bf16[4,8,64]{2,1,0:T(8,128)(2,1)S(1)}, u32[]{:S(2)}, u32[]{:S(2)}) %collective-permute-start.5) | collective-permute-done | bytes 4128 | tf_op jit(solution)/shard_map/ppermute | solution.py:21
  52.1 0.1 fusion.24
  52.1 3.5 %collective-permute-start.6 = (bf16[72,4,64]{2,1,0:T(4,128)(2,1)S(1)}, bf16[72,4,64]{2,1,0:T(4,128)(2,1)S(1)}, u32[]{:S(2)}, u32[]{:S(2)}) collective-permute-start(bf16[72,4,64]{2,1,0:T(4,128)(2,1)S(1)} %get-tuple-element.8), channel_id=1, source_target_pairs={{0,1},{1,2},{2,3},{3,4},{4,5},{5,6},{6,7},{7,8},{8,9},{9,10},{10,1... | collective-permute-start | bytes 110600 | tf_op jit(solution)/shard_map/ppermute | solution.py:20
  55.6 1.3 %collective-permute-start.7 = (bf16[72,4,64]{2,1,0:T(4,128)(2,1)S(1)}, bf16[72,4,64]{2,1,0:T(4,128)(2,1)S(1)}, u32[]{:S(2)}, u32[]{:S(2)}) collective-permute-start(bf16[72,4,64]{2,1,0:T(4,128)(2,1)S(1)} %get-tuple-element.9), channel_id=1, source_target_pairs={{1,0},{2,1},{3,2},{4,3},{5,4},{6,5},{7,6},{8,7},{9,8},{10,9},{11,1... | collective-permute-start | bytes 110600 | tf_op jit(solution)/shard_map/ppermute | solution.py:21
  56.9 2.7 %collective-permute-done.7 = bf16[72,4,64]{2,1,0:T(4,128)(2,1)S(1)} collective-permute-done((bf16[72,4,64]{2,1,0:T(4,128)(2,1)S(1)}, bf16[72,4,64]{2,1,0:T(4,128)(2,1)S(1)}, u32[]{:S(2)}, u32[]{:S(2)}) %collective-permute-start.7) | collective-permute-done | bytes 36896 | tf_op jit(solution)/shard_map/ppermute | solution.py:21
  59.7 0.2 maximum_bitcast_fusion.1
  59.9 1.0 fusion.6
  60.9 0.6 copy-done.4
  61.6 0.8 fusion.8
  62.4 1.6 %collective-permute-start.8 = (bf16[4,8,64]{2,1,0:T(8,128)(2,1)S(1)}, bf16[4,8,64]{2,1,0:T(8,128)(2,1)S(1)}, u32[]{:S(2)}, u32[]{:S(2)}) collective-permute-start(bf16[4,8,64]{2,1,0:T(8,128)(2,1)S(1)} %get-tuple-element.14), channel_id=1, source_target_pairs={{0,16},{1,17},{2,18},{3,19},{4,20},{5,21},{6,22},{7,23},{8,24},{9,... | collective-permute-start | bytes 12296 | tf_op jit(solution)/shard_map/ppermute | solution.py:20
  64.0 1.3 %collective-permute-start.9 = (bf16[4,8,64]{2,1,0:T(8,128)(2,1)S(1)}, bf16[4,8,64]{2,1,0:T(8,128)(2,1)S(1)}, u32[]{:S(2)}, u32[]{:S(2)}) collective-permute-start(bf16[4,8,64]{2,1,0:T(8,128)(2,1)S(1)} %get-tuple-element.15), channel_id=1, source_target_pairs={{16,0},{17,1},{18,2},{19,3},{20,4},{21,5},{22,6},{23,7},{24,8},{25... | collective-permute-start | bytes 12296 | tf_op jit(solution)/shard_map/ppermute | solution.py:21
  65.3 0.0 collective-permute-done.8
  65.4 4.2 %collective-permute-done.9 = bf16[4,8,64]{2,1,0:T(8,128)(2,1)S(1)} collective-permute-done((bf16[4,8,64]{2,1,0:T(8,128)(2,1)S(1)}, bf16[4,8,64]{2,1,0:T(8,128)(2,1)S(1)}, u32[]{:S(2)}, u32[]{:S(2)}) %collective-permute-start.9) | collective-permute-done | bytes 4128 | tf_op jit(solution)/shard_map/ppermute | solution.py:21
  69.6 0.1 fusion.23
  69.7 3.5 %collective-permute-start.10 = (bf16[72,4,64]{2,1,0:T(4,128)(2,1)S(1)}, bf16[72,4,64]{2,1,0:T(4,128)(2,1)S(1)}, u32[]{:S(2)}, u32[]{:S(2)}) collective-permute-start(bf16[72,4,64]{2,1,0:T(4,128)(2,1)S(1)} %get-tuple-element.6), channel_id=1, source_target_pairs={{0,1},{1,2},{2,3},{3,4},{4,5},{5,6},{6,7},{7,8},{8,9},{9,10},{10,1... | collective-permute-start | bytes 110600 | tf_op jit(solution)/shard_map/ppermute | solution.py:20
  73.2 1.3 %collective-permute-start.11 = (bf16[72,4,64]{2,1,0:T(4,128)(2,1)S(1)}, bf16[72,4,64]{2,1,0:T(4,128)(2,1)S(1)}, u32[]{:S(2)}, u32[]{:S(2)}) collective-permute-start(bf16[72,4,64]{2,1,0:T(4,128)(2,1)S(1)} %get-tuple-element.7), channel_id=1, source_target_pairs={{1,0},{2,1},{3,2},{4,3},{5,4},{6,5},{7,6},{8,7},{9,8},{10,9},{11,1... | collective-permute-start | bytes 110600 | tf_op jit(solution)/shard_map/ppermute | solution.py:21
  74.5 2.7 %collective-permute-done.11 = bf16[72,4,64]{2,1,0:T(4,128)(2,1)S(1)} collective-permute-done((bf16[72,4,64]{2,1,0:T(4,128)(2,1)S(1)}, bf16[72,4,64]{2,1,0:T(4,128)(2,1)S(1)}, u32[]{:S(2)}, u32[]{:S(2)}) %collective-permute-start.11) | collective-permute-done | bytes 36896 | tf_op jit(solution)/shard_map/ppermute | solution.py:21
  77.2 0.2 maximum_bitcast_fusion.2
  77.4 2.3 %fusion.4 = f32[1,64,8,64]{3,0,2,1:T(1,128)S(1)} fusion(bf16[3,3,64,64]{3,2,1,0:T(8,128)(2,1)S(1)} %copy-done, bf16[1,72,16,64]{3,2,1,0:T(8,128)(2,1)S(1)} %maximum_bitcast_fusion.2), kind=kOutput, calls=%fused_computation.4 | convolution fusion | flops 37748736 | bytes 352256 | tf_op jit(solution)/shard_map/conv_general_dilated | solution.py:38
  79.7 0.1 fusion.19
  79.8 1.6 %collective-permute-start.12 = (bf16[4,8,64]{2,1,0:T(8,128)(2,1)S(1)}, bf16[4,8,64]{2,1,0:T(8,128)(2,1)S(1)}, u32[]{:S(2)}, u32[]{:S(2)}) collective-permute-start(bf16[4,8,64]{2,1,0:T(8,128)(2,1)S(1)} %get-tuple-element.12), channel_id=1, source_target_pairs={{0,16},{1,17},{2,18},{3,19},{4,20},{5,21},{6,22},{7,23},{8,24},{9,... | collective-permute-start | bytes 12296 | tf_op jit(solution)/shard_map/ppermute | solution.py:20
  81.5 1.3 %collective-permute-start.13 = (bf16[4,8,64]{2,1,0:T(8,128)(2,1)S(1)}, bf16[4,8,64]{2,1,0:T(8,128)(2,1)S(1)}, u32[]{:S(2)}, u32[]{:S(2)}) collective-permute-start(bf16[4,8,64]{2,1,0:T(8,128)(2,1)S(1)} %get-tuple-element.13), channel_id=1, source_target_pairs={{16,0},{17,1},{18,2},{19,3},{20,4},{21,5},{22,6},{23,7},{24,8},{25... | collective-permute-start | bytes 12296 | tf_op jit(solution)/shard_map/ppermute | solution.py:21
  82.8 0.0 collective-permute-done.12
  82.8 4.2 %collective-permute-done.13 = bf16[4,8,64]{2,1,0:T(8,128)(2,1)S(1)} collective-permute-done((bf16[4,8,64]{2,1,0:T(8,128)(2,1)S(1)}, bf16[4,8,64]{2,1,0:T(8,128)(2,1)S(1)}, u32[]{:S(2)}, u32[]{:S(2)}) %collective-permute-start.13) | collective-permute-done | bytes 4128 | tf_op jit(solution)/shard_map/ppermute | solution.py:21
  87.1 0.1 fusion.22
  87.1 4.0 %collective-permute-start.14 = (bf16[72,4,64]{2,1,0:T(4,128)(2,1)S(1)}, bf16[72,4,64]{2,1,0:T(4,128)(2,1)S(1)}, u32[]{:S(2)}, u32[]{:S(2)}) collective-permute-start(bf16[72,4,64]{2,1,0:T(4,128)(2,1)S(1)} %get-tuple-element.4), channel_id=1, source_target_pairs={{0,1},{1,2},{2,3},{3,4},{4,5},{5,6},{6,7},{7,8},{8,9},{9,10},{10,1... | collective-permute-start | bytes 110600 | tf_op jit(solution)/shard_map/ppermute | solution.py:20
  91.2 1.3 %collective-permute-start.15 = (bf16[72,4,64]{2,1,0:T(4,128)(2,1)S(1)}, bf16[72,4,64]{2,1,0:T(4,128)(2,1)S(1)}, u32[]{:S(2)}, u32[]{:S(2)}) collective-permute-start(bf16[72,4,64]{2,1,0:T(4,128)(2,1)S(1)} %get-tuple-element.5), channel_id=1, source_target_pairs={{1,0},{2,1},{3,2},{4,3},{5,4},{6,5},{7,6},{8,7},{9,8},{10,9},{11,1... | collective-permute-start | bytes 110600 | tf_op jit(solution)/shard_map/ppermute | solution.py:21
  92.5 2.7 %collective-permute-done.15 = bf16[72,4,64]{2,1,0:T(4,128)(2,1)S(1)} collective-permute-done((bf16[72,4,64]{2,1,0:T(4,128)(2,1)S(1)}, bf16[72,4,64]{2,1,0:T(4,128)(2,1)S(1)}, u32[]{:S(2)}, u32[]{:S(2)}) %collective-permute-start.15) | collective-permute-done | bytes 36896 | tf_op jit(solution)/shard_map/ppermute | solution.py:21
  95.2 0.2 maximum_bitcast_fusion.3
  95.4 2.3 %fusion.2 = f32[1,64,8,64]{3,0,2,1:T(1,128)S(1)} fusion(bf16[3,3,64,64]{3,2,1,0:T(8,128)(2,1)S(1)} %copy-done.5, bf16[1,72,16,64]{3,2,1,0:T(8,128)(2,1)S(1)} %maximum_bitcast_fusion.3), kind=kOutput, calls=%fused_computation.2 | convolution fusion | flops 37748736 | bytes 352256 | tf_op jit(solution)/shard_map/conv_general_dilated | solution.py:38
  97.7 0.1 reshape_broadcast_in_dim.7
  97.9 6.5 %all_to_all.87 = bf16[1,1,8,2,4,512]{5,2,4,1,0,3:T(8,128)(2,1)S(1)} all-to-all(bf16[1,1,8,2,4,512]{5,2,4,1,0,3:T(8,128)(2,1)S(1)} %copy.43), channel_id=1, replica_groups=mesh['row'=2,'col'=16] {'row'}, dimensions={3} | all-to-all | bytes 131072 | tf_op jit(solution)/shard_map/all_to_all | solution.py:64
  104.4 0.1 copy.45
  104.4 14.5 %all_to_all.88 = bf16[1,16,4,1,512]{4,2,3,0,1:T(4,128)(2,1)S(1)} all-to-all(bf16[1,16,4,1,512]{4,2,3,0,1:T(4,128)(2,1)S(1)} %copy.45), channel_id=1, replica_groups=mesh['row'=2,'col'=16] {'col'}, dimensions={1} | all-to-all | bytes 131072 | tf_op jit(solution)/shard_map/all_to_all | solution.py:66
  119.0 0.1 copy.47
  119.0 6.5 %all_to_all.89 = bf16[1,1,4,2,4096]{4,2,1,0,3:T(4,128)(2,1)S(1)} all-to-all(bf16[1,1,4,2,4096]{4,2,1,0,3:T(4,128)(2,1)S(1)} %copy.47), channel_id=1, replica_groups=mesh['row'=2,'col'=16] {'row'}, dimensions={3} | all-to-all | bytes 131072 | tf_op jit(solution)/shard_map/all_to_all | solution.py:68
  125.5 0.2 reshape.41
  125.7 0.8 fusion.20
  (30 shorter events, 0.4 us)
Async XLA Ops:
  0.6 59.2 %copy-start = (bf16[3,3,64,64]{3,2,1,0:T(8,128)(2,1)S(1)}, bf16[3,3,64,64]{3,2,1,0:T(8,128)(2,1)}, u32[]{:S(2)}) copy-start(bf16[3,3,64,64]{3,2,1,0:T(8,128)(2,1)} %param.9) | copy-start | bytes 221188
  29.2 0.9 copy-start.1
  30.3 3.3 %collective-permute-start = (bf16[4,8,64]{2,1,0:T(8,128)(2,1)S(1)}, bf16[4,8,64]{2,1,0:T(8,128)(2,1)S(1)}, u32[]{:S(2)}, u32[]{:S(2)}) collective-permute-start(bf16[4,8,64]{2,1,0:T(8,128)(2,1)S(1)} %get-tuple-element.18), channel_id=1, source_target_pairs={{0,16},{1,17},{2,18},{3,19},{4,20},{5,21},{6,22},{7,23},{8,24},{9,... | collective-permute-start | bytes 12296 | tf_op jit(solution)/shard_map/ppermute | solution.py:20
  32.2 5.5 %collective-permute-start.1 = (bf16[4,8,64]{2,1,0:T(8,128)(2,1)S(1)}, bf16[4,8,64]{2,1,0:T(8,128)(2,1)S(1)}, u32[]{:S(2)}, u32[]{:S(2)}) collective-permute-start(bf16[4,8,64]{2,1,0:T(8,128)(2,1)S(1)} %get-tuple-element.19), channel_id=1, source_target_pairs={{16,0},{17,1},{18,2},{19,3},{20,4},{21,5},{22,6},{23,7},{24,8},{25... | collective-permute-start | bytes 12296 | tf_op jit(solution)/shard_map/ppermute | solution.py:21
  37.9 2.7 %collective-permute-start.2 = (bf16[72,4,64]{2,1,0:T(4,128)(2,1)S(1)}, bf16[72,4,64]{2,1,0:T(4,128)(2,1)S(1)}, u32[]{:S(2)}, u32[]{:S(2)}) collective-permute-start(bf16[72,4,64]{2,1,0:T(4,128)(2,1)S(1)} %get-tuple-element.10), channel_id=1, source_target_pairs={{0,1},{1,2},{2,3},{3,4},{4,5},{5,6},{6,7},{7,8},{8,9},{9,10},{10,1... | collective-permute-start | bytes 110600 | tf_op jit(solution)/shard_map/ppermute | solution.py:20
  39.2 3.8 %copy-start.5 = (bf16[3,3,64,64]{3,2,1,0:T(8,128)(2,1)S(1)}, bf16[3,3,64,64]{3,2,1,0:T(8,128)(2,1)}, u32[]{:S(2)}) copy-start(bf16[3,3,64,64]{3,2,1,0:T(8,128)(2,1)} %param.7) | copy-start | bytes 221188
  39.2 3.6 %collective-permute-start.3 = (bf16[72,4,64]{2,1,0:T(4,128)(2,1)S(1)}, bf16[72,4,64]{2,1,0:T(4,128)(2,1)S(1)}, u32[]{:S(2)}, u32[]{:S(2)}) collective-permute-start(bf16[72,4,64]{2,1,0:T(4,128)(2,1)S(1)} %get-tuple-element.11), channel_id=1, source_target_pairs={{1,0},{2,1},{3,2},{4,3},{5,4},{6,5},{7,6},{8,7},{9,8},{10,9},{11,1... | collective-permute-start | bytes 110600 | tf_op jit(solution)/shard_map/ppermute | solution.py:21
  44.1 0.7 copy-start.3
  44.8 3.0 %collective-permute-start.4 = (bf16[4,8,64]{2,1,0:T(8,128)(2,1)S(1)}, bf16[4,8,64]{2,1,0:T(8,128)(2,1)S(1)}, u32[]{:S(2)}, u32[]{:S(2)}) collective-permute-start(bf16[4,8,64]{2,1,0:T(8,128)(2,1)S(1)} %get-tuple-element.16), channel_id=1, source_target_pairs={{0,16},{1,17},{2,18},{3,19},{4,20},{5,21},{6,22},{7,23},{8,24},{9,... | collective-permute-start | bytes 12296 | tf_op jit(solution)/shard_map/ppermute | solution.py:20
  46.5 5.5 %collective-permute-start.5 = (bf16[4,8,64]{2,1,0:T(8,128)(2,1)S(1)}, bf16[4,8,64]{2,1,0:T(8,128)(2,1)S(1)}, u32[]{:S(2)}, u32[]{:S(2)}) collective-permute-start(bf16[4,8,64]{2,1,0:T(8,128)(2,1)S(1)} %get-tuple-element.17), channel_id=1, source_target_pairs={{16,0},{17,1},{18,2},{19,3},{20,4},{21,5},{22,6},{23,7},{24,8},{25... | collective-permute-start | bytes 12296 | tf_op jit(solution)/shard_map/ppermute | solution.py:21
  52.1 4.8 %collective-permute-start.6 = (bf16[72,4,64]{2,1,0:T(4,128)(2,1)S(1)}, bf16[72,4,64]{2,1,0:T(4,128)(2,1)S(1)}, u32[]{:S(2)}, u32[]{:S(2)}) collective-permute-start(bf16[72,4,64]{2,1,0:T(4,128)(2,1)S(1)} %get-tuple-element.8), channel_id=1, source_target_pairs={{0,1},{1,2},{2,3},{3,4},{4,5},{5,6},{6,7},{7,8},{8,9},{9,10},{10,1... | collective-permute-start | bytes 110600 | tf_op jit(solution)/shard_map/ppermute | solution.py:20
  55.6 4.0 %collective-permute-start.7 = (bf16[72,4,64]{2,1,0:T(4,128)(2,1)S(1)}, bf16[72,4,64]{2,1,0:T(4,128)(2,1)S(1)}, u32[]{:S(2)}, u32[]{:S(2)}) collective-permute-start(bf16[72,4,64]{2,1,0:T(4,128)(2,1)S(1)} %get-tuple-element.9), channel_id=1, source_target_pairs={{1,0},{2,1},{3,2},{4,3},{5,4},{6,5},{7,6},{8,7},{9,8},{10,9},{11,1... | collective-permute-start | bytes 110600 | tf_op jit(solution)/shard_map/ppermute | solution.py:21
  59.9 1.1 copy-start.2
  60.9 0.7 copy-start.4
  62.4 3.0 %collective-permute-start.8 = (bf16[4,8,64]{2,1,0:T(8,128)(2,1)S(1)}, bf16[4,8,64]{2,1,0:T(8,128)(2,1)S(1)}, u32[]{:S(2)}, u32[]{:S(2)}) collective-permute-start(bf16[4,8,64]{2,1,0:T(8,128)(2,1)S(1)} %get-tuple-element.14), channel_id=1, source_target_pairs={{0,16},{1,17},{2,18},{3,19},{4,20},{5,21},{6,22},{7,23},{8,24},{9,... | collective-permute-start | bytes 12296 | tf_op jit(solution)/shard_map/ppermute | solution.py:20
  64.0 5.5 %collective-permute-start.9 = (bf16[4,8,64]{2,1,0:T(8,128)(2,1)S(1)}, bf16[4,8,64]{2,1,0:T(8,128)(2,1)S(1)}, u32[]{:S(2)}, u32[]{:S(2)}) collective-permute-start(bf16[4,8,64]{2,1,0:T(8,128)(2,1)S(1)} %get-tuple-element.15), channel_id=1, source_target_pairs={{16,0},{17,1},{18,2},{19,3},{20,4},{21,5},{22,6},{23,7},{24,8},{25... | collective-permute-start | bytes 12296 | tf_op jit(solution)/shard_map/ppermute | solution.py:21
  69.7 4.8 %collective-permute-start.10 = (bf16[72,4,64]{2,1,0:T(4,128)(2,1)S(1)}, bf16[72,4,64]{2,1,0:T(4,128)(2,1)S(1)}, u32[]{:S(2)}, u32[]{:S(2)}) collective-permute-start(bf16[72,4,64]{2,1,0:T(4,128)(2,1)S(1)} %get-tuple-element.6), channel_id=1, source_target_pairs={{0,1},{1,2},{2,3},{3,4},{4,5},{5,6},{6,7},{7,8},{8,9},{9,10},{10,1... | collective-permute-start | bytes 110600 | tf_op jit(solution)/shard_map/ppermute | solution.py:20
  73.2 4.0 %collective-permute-start.11 = (bf16[72,4,64]{2,1,0:T(4,128)(2,1)S(1)}, bf16[72,4,64]{2,1,0:T(4,128)(2,1)S(1)}, u32[]{:S(2)}, u32[]{:S(2)}) collective-permute-start(bf16[72,4,64]{2,1,0:T(4,128)(2,1)S(1)} %get-tuple-element.7), channel_id=1, source_target_pairs={{1,0},{2,1},{3,2},{4,3},{5,4},{6,5},{7,6},{8,7},{9,8},{10,9},{11,1... | collective-permute-start | bytes 110600 | tf_op jit(solution)/shard_map/ppermute | solution.py:21
  79.8 3.0 %collective-permute-start.12 = (bf16[4,8,64]{2,1,0:T(8,128)(2,1)S(1)}, bf16[4,8,64]{2,1,0:T(8,128)(2,1)S(1)}, u32[]{:S(2)}, u32[]{:S(2)}) collective-permute-start(bf16[4,8,64]{2,1,0:T(8,128)(2,1)S(1)} %get-tuple-element.12), channel_id=1, source_target_pairs={{0,16},{1,17},{2,18},{3,19},{4,20},{5,21},{6,22},{7,23},{8,24},{9,... | collective-permute-start | bytes 12296 | tf_op jit(solution)/shard_map/ppermute | solution.py:20
  81.5 5.5 %collective-permute-start.13 = (bf16[4,8,64]{2,1,0:T(8,128)(2,1)S(1)}, bf16[4,8,64]{2,1,0:T(8,128)(2,1)S(1)}, u32[]{:S(2)}, u32[]{:S(2)}) collective-permute-start(bf16[4,8,64]{2,1,0:T(8,128)(2,1)S(1)} %get-tuple-element.13), channel_id=1, source_target_pairs={{16,0},{17,1},{18,2},{19,3},{20,4},{21,5},{22,6},{23,7},{24,8},{25... | collective-permute-start | bytes 12296 | tf_op jit(solution)/shard_map/ppermute | solution.py:21
  87.1 5.4 %collective-permute-start.14 = (bf16[72,4,64]{2,1,0:T(4,128)(2,1)S(1)}, bf16[72,4,64]{2,1,0:T(4,128)(2,1)S(1)}, u32[]{:S(2)}, u32[]{:S(2)}) collective-permute-start(bf16[72,4,64]{2,1,0:T(4,128)(2,1)S(1)} %get-tuple-element.4), channel_id=1, source_target_pairs={{0,1},{1,2},{2,3},{3,4},{4,5},{5,6},{6,7},{7,8},{8,9},{9,10},{10,1... | collective-permute-start | bytes 110600 | tf_op jit(solution)/shard_map/ppermute | solution.py:20
  91.2 4.0 %collective-permute-start.15 = (bf16[72,4,64]{2,1,0:T(4,128)(2,1)S(1)}, bf16[72,4,64]{2,1,0:T(4,128)(2,1)S(1)}, u32[]{:S(2)}, u32[]{:S(2)}) collective-permute-start(bf16[72,4,64]{2,1,0:T(4,128)(2,1)S(1)} %get-tuple-element.5), channel_id=1, source_target_pairs={{1,0},{2,1},{3,2},{4,3},{5,4},{6,5},{7,6},{8,7},{9,8},{10,9},{11,1... | collective-permute-start | bytes 110600 | tf_op jit(solution)/shard_map/ppermute | solution.py:21
where the time goes:
time: 127 us
  blocking collectives  54.7 us (43%)
  starting transfers between devices  29.6 us (23%)
  waiting for transfers between devices  27.4 us (22%)
  matrix products  6.59 us (5%)
  local copies, waits for them, and re-layouts  4.21 us (3%)
  other arithmetic  2.91 us (2%)
    ppermute x8, waiting for transfers between devices, with_halo(): after = lax.ppermute(first, axis, down)  27.2 us
    all_to_all x2, blocking collectives, mirror_rows(): lax.all_to_all(across_parts, 'col', split_axis=1, concat_axis=3, tiled=True)  27.1 us
    ppermute x8, starting transfers between devices, with_halo(): before = lax.ppermute(last, axis, up)  19.2 us
    all_to_all x2, blocking collectives, mirror_rows(): lax.all_to_all(spread_parts, 'row', split_axis=3, concat_axis=1, tiled=True)  14.7 us
    all_to_all x2, blocking collectives, mirror_rows(): lax.all_to_all(settle_parts, 'row', split_axis=3, concat_axis=1, tiled=True)  13 us
    ppermute x8, starting transfers between devices, with_halo(): after = lax.ppermute(first, axis, down)  10.5 us
    conv_general_dilated x4, matrix products, dilated_conv(): lax.conv_general_dilated(padded_input[None], conv_kernel, (1, 1), 'VALID'...  6.59 us
  transfers between devices with their start and end apart: 16, of which 8 were waited for; matrix products, arithmetic and copies ran while one was open for 0% of the time, Pallas kernels for 0%

commit v1 on v0

v1 whole, which is shorter than its diff:
```python
import jax
import jax.numpy as jnp
from jax import lax
from jax.sharding import PartitionSpec as P

DILATION_STEP = 4
CORES = 2
CONVS = 4


root_half = 0.7071067811865476
inv_root_tau = 0.3989422804014327
both = ("row", "col")


def with_halo(array, sides, width):
    for axis, dim in sides:
        size, length = (lax.axis_size(axis), array.shape[dim])
        up = [(i, (i + 1) % size) for i in range(size - 1)]
        down = [(j, i) for i, j in up]
        last = lax.slice_in_dim(array, length - width, length, axis=dim)
        first = lax.slice_in_dim(array, 0, width, axis=dim)
        before = lax.ppermute(last, axis, up)
        after = lax.ppermute(first, axis, down)
        array = jnp.concatenate([before, array, after], axis=dim)
    return array


def gelu_value(value_array):
    return 0.5 * value_array * (1.0 + lax.erf(value_array * root_half))


def gelu_slope(value_array):
    return (
        0.5 * (1.0 + lax.erf(value_array * root_half))
        + value_array * jnp.exp(-0.5 * value_array * value_array) * inv_root_tau
    )


def conv(padded_input, conv_kernel, step):
    return lax.conv_general_dilated(
        padded_input[None],
        conv_kernel,
        (1, 1),
        "VALID",
        rhs_dilation=(step, step),
        dimension_numbers=("NHWC", "HWIO", "NHWC"),
        preferred_element_type=jnp.float32,
    )[0]


def dilated_conv(padded_input, conv_kernel):
    return conv(padded_input, conv_kernel, DILATION_STEP)


def reversed_kernel(conv_kernel):
    return jnp.transpose(conv_kernel[::-1, ::-1], (0, 1, 3, 2))


def extend(value_array):
    return with_halo(value_array, (("row", 0), ("col", 1)), DILATION_STEP)


def mirror(tile):
    row_count = lax.axis_size("row")
    col_count = lax.axis_size("col")
    tile_rows, tile_cols, channels = tile.shape
    unit_len = tile_rows // col_count
    col_ratio = col_count // row_count
    spread_parts = tile.reshape(1, 1, col_ratio, row_count, unit_len, tile_cols * channels)
    spread_parts = lax.all_to_all(spread_parts, "row", split_axis=3, concat_axis=1, tiled=True)
    across_parts = spread_parts.reshape(1, col_count, unit_len, 1, tile_cols * channels)
    across_parts = lax.all_to_all(across_parts, "col", split_axis=1, concat_axis=3, tiled=True)
    settle_parts = across_parts.reshape(1, 1, unit_len, row_count, tile_rows * channels)
    settle_parts = lax.all_to_all(settle_parts, "row", split_axis=3, concat_axis=1, tiled=True)
    turned = settle_parts.reshape(tile_cols, tile_rows, channels)
    return jnp.transpose(turned, (1, 0, 2))


def add_rounded(first, second):
    return (first.astype(jnp.float32) + second.astype(jnp.float32)).astype(jnp.bfloat16)


def by_tiles(feature_map, kernel_first, bias_first, kernel_second, bias_second, cotangent):
    symmetric = add_rounded(feature_map, mirror(feature_map))
    pre_first = dilated_conv(extend(symmetric), kernel_first) + bias_first
    hidden = gelu_value(pre_first).astype(jnp.bfloat16)
    pre_second = dilated_conv(extend(hidden), kernel_second) + bias_second
    output = (symmetric.astype(jnp.float32) + gelu_value(pre_second)).astype(jnp.bfloat16)
    grad_second = (cotangent.astype(jnp.float32) * gelu_slope(pre_second)).astype(jnp.bfloat16)
    hidden_gradient = dilated_conv(extend(grad_second), reversed_kernel(kernel_second))
    grad_first = (hidden_gradient * gelu_slope(pre_first)).astype(jnp.bfloat16)
    total_sum = cotangent.astype(jnp.float32) + dilated_conv(
        extend(grad_first), reversed_kernel(kernel_first)
    )
    grad_sym = total_sum.astype(jnp.bfloat16)
    return output, add_rounded(grad_sym, mirror(grad_sym))


def flipped_pair(conv_kernel):
    return jnp.transpose(conv_kernel, (1, 0, 2, 3)), conv_kernel


def block_diagonal(first, second):
    zeros = jnp.zeros_like(first)
    return jnp.concatenate(
        [jnp.concatenate([first, zeros], 3), jnp.concatenate([zeros, second], 3)], 2
    )


def dense_conv(image, conv_kernel):
    return conv(jnp.pad(image, ((1, 1), (1, 1), (0, 0))), conv_kernel, 1)


def by_classes(feature_map, kernel_first, bias_first, kernel_second, bias_second, cotangent):
    row_count, col_count = lax.axis_size("row"), lax.axis_size("col")
    device_count = row_count * col_count
    tile_rows, tile_cols, channels = feature_map.shape
    step = DILATION_STEP
    part_rows, part_cols = tile_rows // step, tile_cols // step
    class_rows, class_cols = part_rows * row_count, part_cols * col_count
    core = lax.axis_index("col") % CORES

    tile = jnp.concatenate([feature_map, cotangent], -1)
    parts = tile.reshape(part_rows, step, part_cols, step, 2 * channels)
    parts = jnp.transpose(parts, (1, 3, 2, 0, 4))
    parts = jnp.stack([parts, jnp.swapaxes(parts, 0, 1)], 2)
    parts = parts.reshape(device_count, part_cols * part_rows, 2 * channels)
    own = lax.all_to_all(parts, both, 0, 0, tiled=True)
    other = lax.ppermute(own, "col", [(i, i ^ 1) for i in range(col_count)])
    straight = jnp.where(core == 0, own, other)
    turned = jnp.where(core == 0, other, own)

    def image(pieces):
        pieces = pieces.reshape(row_count, col_count, part_cols, part_rows, 2 * channels)
        return jnp.transpose(pieces, (1, 2, 0, 3, 4)).reshape(class_cols, class_rows, 2 * channels)

    straight, turned = image(straight), jnp.swapaxes(image(turned), 0, 1)
    share = class_cols // CORES
    straight, turned = (
        lax.dynamic_slice_in_dim(v, core * (share - CONVS), share + CONVS, 0)
        for v in (straight, turned)
    )
    symmetric = add_rounded(straight[..., :channels], turned[..., :channels])
    gradient = jnp.concatenate([straight[..., channels:], turned[..., channels:]], -1)

    pre_first = dense_conv(symmetric, jnp.concatenate(flipped_pair(kernel_first), 3)) + jnp.tile(
        bias_first, 2
    )
    hidden = gelu_value(pre_first).astype(jnp.bfloat16)
    pre_second = dense_conv(hidden, block_diagonal(*flipped_pair(kernel_second))) + jnp.tile(
        bias_second, 2
    )
    output = (
        symmetric.astype(jnp.float32) + gelu_value(pre_second[..., :channels])
    ).astype(jnp.bfloat16)
    grad_second = (gradient.astype(jnp.float32) * gelu_slope(pre_second)).astype(jnp.bfloat16)
    hidden_gradient = dense_conv(
        grad_second, block_diagonal(*flipped_pair(reversed_kernel(kernel_second)))
    )
    grad_first = (hidden_gradient * gelu_slope(pre_first)).astype(jnp.bfloat16)
    total_sum = gradient.astype(jnp.float32) + dense_conv(
        grad_first, block_diagonal(*flipped_pair(reversed_kernel(kernel_first)))
    )
    grad_sym = total_sum.astype(jnp.bfloat16)
    grad_input = add_rounded(grad_sym[..., :channels], grad_sym[..., channels:])
    result = jnp.concatenate([output, grad_input], -1)
    result = lax.dynamic_slice_in_dim(result, core * CONVS, share, 0)

    half = col_count // CORES
    result = result.reshape(half, part_cols, row_count, part_rows, 2 * channels)
    result = jnp.transpose(result, (2, 0, 1, 3, 4))[:, None]
    result = jnp.broadcast_to(result, (row_count, CORES) + result.shape[2:])
    result = result.reshape(device_count, part_cols * part_rows, 2 * channels)
    back = lax.all_to_all(result, both, 0, 0, tiled=True)
    back = back.reshape(step, step, CORES, part_cols, part_rows, 2 * channels)
    back = lax.dynamic_index_in_dim(back, lax.axis_index("col") // half, 2, keepdims=False)
    back = jnp.transpose(back, (3, 0, 2, 1, 4)).reshape(tile_rows, tile_cols, 2 * channels)
    return back[..., :channels], back[..., channels:]


def solution(mesh):
    row_count, col_count = mesh.shape["row"], mesh.shape["col"]
    classes = DILATION_STEP * DILATION_STEP
    paired = row_count * col_count == CORES * classes and col_count % CORES == 0
    in_specs = (P("row", "col", None), P(), P(), P(), P(), P("row", "col", None))
    out_specs = (P("row", "col", None), P("row", "col", None))

    def whole(feature_map, *others):
        size = feature_map.shape[0]
        fits = size % (DILATION_STEP * row_count) == 0 and size % (DILATION_STEP * col_count) == 0
        per_device = by_classes if paired and fits else by_tiles
        return jax.shard_map(
            per_device, mesh=mesh, in_specs=in_specs, out_specs=out_specs, check_vma=False
        )(feature_map, *others)

    return whole
```

time: 127 us -> 43.7 us (0.34)
  blocking collectives: 54.7 us -> 17.4 us
  starting transfers between devices: 29.6 us -> 2.89 us
  waiting for transfers between devices: 27.4 us -> 10.3 us
  matrix products: 6.59 us -> 2.7 us
  local copies, waits for them, and re-layouts: 4.21 us -> 6.63 us
    all_to_all x6 -> x1, blocking collectives: 54.7 us -> 17.4 us  [by_classes(): own = lax.all_to_all(parts, both, 0, 0, tiled=True)]
    ppermute x16 -> x1, starting transfers between devices: 29.6 us -> 0.3 us  [by_classes(): other = lax.ppermute(own, 'col', [(i, i ^ 1) for i in range(col_count)])]
    ppermute x16 -> x1, waiting for transfers between devices: 27.4 us -> 0.01 us  [by_classes(): other = lax.ppermute(own, 'col', [(i, i ^ 1) for i in range(col_count)])]
    all_to_all x0 -> x1, waiting for transfers between devices: none -> 10.3 us  [by_classes(): back = lax.all_to_all(result, both, 0, 0, tiled=True)]
    conv_general_dilated x4, matrix products: 6.59 us -> 2.7 us  [conv(): lax.conv_general_dilated(padded_input[None], conv_kernel, (1, 1), 'VALID'...]
    all_to_all x0 -> x1, starting transfers between devices: none -> 2.58 us  [by_classes(): back = lax.all_to_all(result, both, 0, 0, tiled=True)]
    unnamed x12 -> x19, local copies, waits for them, and re-layouts: 2.03 us -> 3.22 us
  transfers between devices with their start and end apart: 16 -> 2, of which waited for: 8 -> 1; matrix products, arithmetic and copies ran while one was open for 0% -> 1% of each run, Pallas kernels for 0% -> 0%
where the time goes in v1:
time: 43.7 us; the launch traced here: 43.4 us
  blocking collectives  17.4 us (40%)
  waiting for transfers between devices  10.3 us (24%)
  local copies, waits for them, and re-layouts  6.63 us (15%)
  starting transfers between devices  2.89 us (7%)
  matrix products  2.7 us (6%)
  other arithmetic  2.35 us (5%)
  between operations  1.14 us (3%)
    all_to_all x1, blocking collectives, by_classes(): own = lax.all_to_all(parts, both, 0, 0, tiled=True)  17.4 us
    all_to_all x1, waiting for transfers between devices, by_classes(): back = lax.all_to_all(result, both, 0, 0, tiled=True)  10.3 us
    unnamed x19, local copies, waits for them, and re-layouts  3.22 us
    conv_general_dilated x4, matrix products, conv(): lax.conv_general_dilated(padded_input[None], conv_kernel, (1, 1), 'VALID'...  2.7 us
    all_to_all x1, starting transfers between devices, by_classes(): back = lax.all_to_all(result, both, 0, 0, tiled=True)  2.58 us
    concatenate x1, other arithmetic, by_classes(): tile = jnp.concatenate([feature_map, cotangent], -1)  1.08 us
  transfers between devices with their start and end apart: 2, of which 1 were waited for; matrix products, arithmetic and copies ran while one was open for 1% of the time, Pallas kernels for 0%

profile of v1, /device:TPU:0, one launch (start us, length us, event | category | flops | bytes accessed | tf_op | source)
XLA Modules:
  0.0 43.4 jit_solution(8771346491393635662)
XLA Ops:
  0.6 1.1 %pad_maximum_fusion.2 = bf16[64,8,128]{2,1,0:T(8,128)(2,1)S(1)} fusion(bf16[64,8,64]{2,1,0:T(8,128)(2,1)} %param.11, bf16[64,8,64]{2,1,0:T(8,128)(2,1)} %param.6), kind=kLoop, calls=%fused_computation.101 | loop fusion | flops 262144 | bytes 262144 | tf_op jit(solution)/shard_map/concatenate | solution.py:124
  1.7 0.1 copy.158
  1.8 0.2 pad_maximum_fusion
  2.0 0.1 copy.79
  2.1 0.0 copy-start.1
  2.1 17.4 %all_to_all.10 = bf16[32,32,128]{2,1,0:T(8,128)(2,1)S(1)} all-to-all(bf16[32,32,128]{2,1,0:T(8,128)(2,1)S(1)} %bitcast.112), channel_id=1, replica_groups=mesh['row'=2,'col'=16] {'row','col'}, dimensions={0} | all-to-all | bytes 524288 | tf_op jit(solution)/shard_map/all_to_all | solution.py:129
  19.5 0.3 collective-permute-start
  19.8 0.0 copy-done.1
  19.8 0.0 copy-start
  19.8 0.1 copy.98
  20.0 0.8 %copy-done = bf16[3,3,64,64]{3,2,1,0:T(8,128)(2,1)S(1)} copy-done((bf16[3,3,64,64]{3,2,1,0:T(8,128)(2,1)S(1)}, bf16[3,3,64,64]{3,2,1,0:T(8,128)(2,1)}, u32[]{:S(2)}) %copy-start) | copy-done | bytes 73752
  20.7 0.1 copy.105
  20.9 0.0 copy-start.2
  20.9 0.6 %copy-done.2 = f32[64]{0:T(128)S(1)} copy-done((f32[64]{0:T(128)S(1)}, f32[64]{0:T(128)}, u32[]{:S(2)}) %copy-start.2) | copy-done | bytes 280
  21.6 0.1 add.90
  21.6 0.0 copy-start.3
  21.7 0.7 %copy-done.3 = f32[64]{0:T(128)S(1)} copy-done((f32[64]{0:T(128)S(1)}, f32[64]{0:T(128)}, u32[]{:S(2)}) %copy-start.3) | copy-done | bytes 280
  22.3 0.1 add.94
  22.4 0.1 reverse_bitcast_fusion.3
  22.5 0.0 collective-permute-done
  22.6 0.1 constant_dynamic-slice_fusion
  22.7 0.1 slice.50
  22.8 0.1 add_convert_fusion.2
  22.9 0.1 pad_bitcast_fusion.3
  23.0 0.1 pad.24.clone
  23.2 0.0 copy-start.4
  23.2 0.7 %copy-done.4 = pred[8,5]{0,1:T(8,128)(4,1)S(1)} copy-done((pred[8,5]{0,1:T(8,128)(4,1)S(1)}, pred[8,5]{0,1:T(8,128)(4,1)}, u32[]{:S(2)}) %copy-start.4) | copy-done | bytes 64
  23.8 0.5 %convolution_select_fusion.3 = f32[20,8,5,128]{3,1,2,0:T(8,128)S(1)} fusion(bf16[22,1,7,2,64]{4,2,3,0,1:T(8,128)(2,1)S(1)} %slice.45, bf16[22,1,8,5,64]{4,2,3,0,1:T(8,128)(2,1)S(1)} %copy.85, pred[8,5]{0,1:T(8,128)(4,1)S(1)} %copy-done.4, bf16[3,3,64,64]{3,2,1,0:T(8,128)(2,1)S(1)} %copy-done, bf16[3,3,64,64]{3,2,1,0:T(8,128)(2,1)S(1)} %bitcast.124), kind=kOutput, calls=%fused_computation.3 | convolution fusion | flops 118835200 | bytes 709160 | tf_op jit(solution)/shard_map/conv_general_dilated | solution.py:41
  24.4 0.1 copy.87
  24.5 0.1 multiply_convert_fusion
  24.6 0.1 pad_bitcast_fusion.2
  24.8 0.7 %convolution_select_fusion.2 = f32[20,8,5,128]{3,1,2,0:T(8,128)S(1)} fusion(bf16[22,1,7,2,128]{4,2,3,0,1:T(8,128)(2,1)S(1)} %slice.47, bf16[22,1,8,5,128]{4,2,3,0,1:T(8,128)(2,1)S(1)} %copy.91, bf16[3,3,64,64]{3,2,1,0:T(8,128)(2,1)S(1)} %copy-done.1, bf16[3,3,64,64]{3,2,1,0:T(8,128)(2,1)S(1)} %bitcast.123, pred[8,5]{0,1:T(8,128)(4,1)S(1)} %copy-done.4), kind=kOutput, calls=%fused_computation.2 | convolution fusion | flops 238157824 | bytes 861224 | tf_op jit(solution)/shard_map/conv_general_dilated | solution.py:41
  25.6 0.1 copy.93
  25.7 0.1 constant_dynamic-slice_fusion.1
  25.8 0.2 fusion.10
  26.1 0.1 pad_bitcast_fusion.1
  26.3 0.7 %convolution_select_fusion.1 = f32[20,8,5,128]{3,1,2,0:T(8,128)S(1)} fusion(bf16[22,1,7,2,128]{4,2,3,0,1:T(8,128)(2,1)S(1)} %slice.51, bf16[22,1,8,5,128]{4,2,3,0,1:T(8,128)(2,1)S(1)} %copy.97, bf16[3,3,64,64]{3,2,1,0:T(8,128)(2,1)S(1)} %get-tuple-element.9, pred[8,5]{0,1:T(8,128)(4,1)S(1)} %copy-done.4, bf16[3,3,64,64]{3,2,0,1:T(8,128)(2,1)S(1)} %get-tuple-element.8), kind=kOutput, calls=%fused_computation.1 | convolution fusion | flops 238157824 | bytes 861224 | tf_op jit(solution)/shard_map/conv_general_dilated | solution.py:41
  27.0 0.1 copy.100
  27.1 0.2 fusion.21
  27.3 0.1 pad_bitcast_fusion
  27.6 0.7 %convolution_select_fusion = f32[20,8,5,128]{3,1,2,0:T(8,128)S(1)} fusion(bf16[22,1,7,2,128]{4,2,3,0,1:T(8,128)(2,1)S(1)} %slice.53, bf16[22,1,8,5,128]{4,2,3,0,1:T(8,128)(2,1)S(1)} %copy.104, bf16[3,3,64,64]{3,2,1,0:T(8,128)(2,1)S(1)} %get-tuple-element.7, pred[8,5]{0,1:T(8,128)(4,1)S(1)} %copy-done.4, bf16[3,3,64,64]{3,2,0,1:T(8,128)(2,1)S(1)} %get-tuple-element.6), kind=kOutput, calls=%fused_computation | convolution fusion | flops 238157824 | bytes 861224 | tf_op jit(solution)/shard_map/conv_general_dilated | solution.py:41
  28.3 0.1 copy.107
  28.4 0.2 fusion.11
  28.6 0.2 add_convert_fusion
  28.8 0.1 fusion.76
  28.9 0.7 %broadcast_in_dim.22 = bf16[2,2,8,2,16,128]{5,4,3,2,1,0:T(8,128)(2,1)} broadcast(bf16[2,8,2,16,128]{4,3,2,1,0:T(8,128)(2,1)S(1)} %copy.109), dimensions={0,2,3,4,5} | broadcast | bytes 393216 | tf_op jit(solution)/shard_map/broadcast_in_dim | solution.py:173
  29.6 2.6 %all-to-all-start.1 = ((bf16[32,32,128]{2,1,0:T(8,128)(2,1)}), bf16[32,32,128]{2,1,0:T(8,128)(2,1)S(1)}, u32[]{:S(2)}, u32[]{:S(2)}) async-start(bf16[32,32,128]{2,1,0:T(8,128)(2,1)} %bitcast.41), calls=%async_computation.1 | async-start | bytes 524288 | tf_op jit(solution)/shard_map/all_to_all | solution.py:175
  32.3 10.3 %all-to-all-done.1 = bf16[32,32,128]{2,1,0:T(8,128)(2,1)S(1)} async-done(((bf16[32,32,128]{2,1,0:T(8,128)(2,1)}), bf16[32,32,128]{2,1,0:T(8,128)(2,1)S(1)}, u32[]{:S(2)}, u32[]{:S(2)}) %all-to-all-start.1) | async-done | bytes 262176 | tf_op jit(solution)/shard_map/all_to_all | solution.py:175
  42.5 0.1 copy.110
  42.6 0.8 %fusion.93 = (bf16[64,8,64]{2,1,0:T(8,128)(2,1)}, bf16[64,8,64]{2,1,0:T(8,128)(2,1)}) fusion(bf16[64,8,128]{2,1,0:T(8,128)(2,1)S(1)} %bitcast.109), kind=kLoop, calls=%fused_computation.125 | loop fusion | bytes 262144 | tf_op jit(solution)/shard_map/slice | solution.py:179
  (30 shorter events, 0.8 us)
Async XLA Ops:
  2.1 17.7 %copy-start.1 = (bf16[3,3,64,64]{3,2,1,0:T(8,128)(2,1)S(1)}, bf16[3,3,64,64]{3,2,1,0:T(8,128)(2,1)}, u32[]{:S(2)}) copy-start(bf16[3,3,64,64]{3,2,1,0:T(8,128)(2,1)} %param.9) | copy-start | bytes 221188
  19.5 3.0 %collective-permute-start = (bf16[32,32,128]{2,1,0:T(8,128)(2,1)S(1)}, bf16[32,32,128]{2,1,0:T(8,128)(2,1)S(1)}, u32[]{:S(2)}, u32[]{:S(2)}) collective-permute-start(bf16[32,32,128]{2,1,0:T(8,128)(2,1)S(1)} %all_to_all.10), channel_id=1, source_target_pairs={{0,1},{1,0},{2,3},{3,2},{4,5},{5,4},{6,7},{7,6},{8,9},{9,8},{10,11... | collective-permute-start | bytes 786440 | tf_op jit(solution)/shard_map/ppermute | solution.py:130
  19.8 0.9 %copy-start = (bf16[3,3,64,64]{3,2,1,0:T(8,128)(2,1)S(1)}, bf16[3,3,64,64]{3,2,1,0:T(8,128)(2,1)}, u32[]{:S(2)}) copy-start(bf16[3,3,64,64]{3,2,1,0:T(8,128)(2,1)} %param.7) | copy-start | bytes 221188
  20.9 0.7 %copy-start.2 = (f32[64]{0:T(128)S(1)}, f32[64]{0:T(128)}, u32[]{:S(2)}) copy-start(f32[64]{0:T(128)} %param.8) | copy-start | bytes 772
  21.6 0.7 %copy-start.3 = (f32[64]{0:T(128)S(1)}, f32[64]{0:T(128)}, u32[]{:S(2)}) copy-start(f32[64]{0:T(128)} %param.10) | copy-start | bytes 772
  23.2 0.7 %copy-start.4 = (pred[8,5]{0,1:T(8,128)(4,1)S(1)}, pred[8,5]{0,1:T(8,128)(4,1)}, u32[]{:S(2)}) copy-start(pred[8,5]{0,1:T(8,128)(4,1)} %constant.98) | copy-start | bytes 124
  29.6 12.9 %all-to-all-start.1 = ((bf16[32,32,128]{2,1,0:T(8,128)(2,1)}), bf16[32,32,128]{2,1,0:T(8,128)(2,1)S(1)}, u32[]{:S(2)}, u32[]{:S(2)}) async-start(bf16[32,32,128]{2,1,0:T(8,128)(2,1)} %bitcast.41), calls=%async_computation.1 | async-start | bytes 524288 | tf_op jit(solution)/shard_map/all_to_all | solution.py:175

commit v2 on v1

--- a/solution.py
+++ b/solution.py
@@ -1,6 +1,10 @@
+import functools
+
 import jax
 import jax.numpy as jnp
 from jax import lax
+from jax.experimental import pallas as pl
+from jax.experimental.pallas import tpu as pltpu
 from jax.sharding import PartitionSpec as P
 
 DILATION_STEP = 4
@@ -108,8 +112,110 @@
     )
 
 
-def dense_conv(image, conv_kernel):
-    return conv(jnp.pad(image, ((1, 1), (1, 1), (0, 0))), conv_kernel, 1)
+def tap_matrix(first, second):
+    taps = jnp.transpose(block_diagonal(first, second), (0, 2, 1, 3))
+    return taps.reshape(taps.shape[0] * taps.shape[1], -1)
+
+
+def class_kernel(
+    row_count,
+    part_cols,
+    own,
+    other,
+    weight_first,
+    weight_second,
+    weight_third,
+    weight_fourth,
+    bias_first,
+    bias_second,
+    result,
+    turning,
+    window,
+):
+    blocks, part, width = own.shape
+    channels = width // 2
+    part_rows = part // part_cols
+    col_count = blocks // row_count
+    class_cols, class_rows = col_count * part_cols, row_count * part_rows
+    share = class_cols // CORES
+    count = share + CONVS
+    core = lax.rem(lax.axis_index("col"), CORES)
+    begin = core * (share - CONVS)
+    low = lax.broadcasted_iota(jnp.int32, (count * class_rows, width), 1) < channels
+    place = lax.rem(lax.broadcasted_iota(jnp.int32, (count * class_rows, width), 0), class_rows)
+
+    pieces = []
+    for r in range(row_count):
+        reach = pl.ds(r * col_count + core * ((share - CONVS) // part_cols), count // part_cols)
+        piece = jnp.where(core == 0, own[reach], other[reach])
+        pieces.append(piece.reshape(count, part_rows, width))
+    straight = jnp.concatenate(pieces, 1).astype(jnp.float32)
+    straight = straight.reshape(count * class_rows, width)
+
+    for r in range(row_count):
+        reach = pl.ds(r * col_count, col_count)
+        piece = jnp.where(core == 0, other[reach], own[reach]).astype(jnp.float32)
+        piece = piece.reshape(class_cols, part_rows, width)
+        for k in range(class_cols):
+            turning[pl.ds(k * class_rows + r * part_rows, part_rows), :] = piece[k]
+    turned = jnp.concatenate(
+        [turning[pl.ds(begin + i, class_cols, stride=class_rows), :] for i in range(count)], 0
+    )
+
+    def swapped(value):
+        return pltpu.roll(value, channels, 1)
+
+    def tap_sum(image, matrix):
+        gap = jnp.zeros((class_rows, width), image.dtype)
+        before = jnp.concatenate([gap, image[:-class_rows]], 0)
+        after = jnp.concatenate([image[class_rows:], gap], 0)
+        taps = jnp.dot(
+            jnp.concatenate([before, image, after], 1),
+            matrix[...],
+            preferred_element_type=jnp.float32,
+        )
+        above = jnp.where(place == 0, 0.0, pltpu.roll(taps[:, :width], 1, 0))
+        below = pltpu.roll(taps[:, 2 * width :], count * class_rows - 1, 0)
+        below = jnp.where(place == class_rows - 1, 0.0, below)
+        return above + taps[:, width : 2 * width] + below
+
+    symmetric = straight + turned
+    symmetric = jnp.where(low, symmetric, swapped(symmetric)).astype(jnp.bfloat16)
+    gradient = jnp.where(low, swapped(straight), turned)
+
+    pre_first = tap_sum(symmetric, weight_first) + bias_first[...]
+    hidden = gelu_value(pre_first).astype(jnp.bfloat16)
+    slope_first = gelu_slope(pre_first)
+    pre_second = tap_sum(hidden, weight_second) + bias_second[...]
+    output = symmetric.astype(jnp.float32) + gelu_value(pre_second)
+    grad_second = (gradient * gelu_slope(pre_second)).astype(jnp.bfloat16)
+    grad_first = (tap_sum(grad_second, weight_third) * slope_first).astype(jnp.bfloat16)
+    grad_sym = (gradient + tap_sum(grad_first, weight_fourth)).astype(jnp.bfloat16)
+    grad_sym = grad_sym.astype(jnp.float32)
+    both_results = jnp.where(low, output, grad_sym + swapped(grad_sym)).astype(jnp.bfloat16)
+    window[...] = both_results.reshape(count, class_rows, width)
+    kept = window[pl.ds(core * CONVS, share)]
+    half = share // part_cols
+    for r in range(row_count):
+        piece = kept[:, r * part_rows : (r + 1) * part_rows]
+        result[r * half : (r + 1) * half] = piece.reshape(half, part, width)
+
+
+def class_chains(row_count, part_cols, own, other, *parameters):
+    blocks, part, width = own.shape
+    class_cols, class_rows = blocks // row_count * part_cols, row_count * (part // part_cols)
+    share = class_cols // CORES
+    return pl.pallas_call(
+        functools.partial(class_kernel, row_count, part_cols),
+        out_shape=jax.ShapeDtypeStruct((blocks // CORES, part, width), jnp.bfloat16),
+        in_specs=[pl.BlockSpec(memory_space=pltpu.VMEM)] * 8,
+        out_specs=pl.BlockSpec(memory_space=pltpu.VMEM),
+        scratch_shapes=[
+            pltpu.VMEM((class_cols * class_rows, width), jnp.float32),
+            pltpu.VMEM((share + CONVS, class_rows, width), jnp.bfloat16),
+        ],
+        compiler_params=pltpu.CompilerParams(vmem_limit_bytes=32 * 2**20),
+    )(own, other, *parameters)
 
 
 def by_classes(feature_map, kernel_first, bias_first, kernel_second, bias_second, cotangent):
@@ -118,8 +224,6 @@
     tile_rows, tile_cols, channels = feature_map.shape
     step = DILATION_STEP
     part_rows, part_cols = tile_rows // step, tile_cols // step
-    class_rows, class_cols = part_rows * row_count, part_cols * col_count
-    core = lax.axis_index("col") % CORES
 
     tile = jnp.concatenate([feature_map, cotangent], -1)
     parts = tile.reshape(part_rows, step, part_cols, step, 2 * channels)
@@ -128,48 +232,21 @@
     parts = parts.reshape(device_count, part_cols * part_rows, 2 * channels)
     own = lax.all_to_all(parts, both, 0, 0, tiled=True)
     other = lax.ppermute(own, "col", [(i, i ^ 1) for i in range(col_count)])
-    straight = jnp.where(core == 0, own, other)
-    turned = jnp.where(core == 0, other, own)
-
-    def image(pieces):
-        pieces = pieces.reshape(row_count, col_count, part_cols, part_rows, 2 * channels)
-        return jnp.transpose(pieces, (1, 2, 0, 3, 4)).reshape(class_cols, class_rows, 2 * channels)
-
-    straight, turned = image(straight), jnp.swapaxes(image(turned), 0, 1)
-    share = class_cols // CORES
-    straight, turned = (
-        lax.dynamic_slice_in_dim(v, core * (share - CONVS), share + CONVS, 0)
-        for v in (straight, turned)
-    )
-    symmetric = add_rounded(straight[..., :channels], turned[..., :channels])
-    gradient = jnp.concatenate([straight[..., channels:], turned[..., channels:]], -1)
-
-    pre_first = dense_conv(symmetric, jnp.concatenate(flipped_pair(kernel_first), 3)) + jnp.tile(
-        bias_first, 2
-    )
-    hidden = gelu_value(pre_first).astype(jnp.bfloat16)
-    pre_second = dense_conv(hidden, block_diagonal(*flipped_pair(kernel_second))) + jnp.tile(
-        bias_second, 2
-    )
-    output = (
-        symmetric.astype(jnp.float32) + gelu_value(pre_second[..., :channels])
-    ).astype(jnp.bfloat16)
-    grad_second = (gradient.astype(jnp.float32) * gelu_slope(pre_second)).astype(jnp.bfloat16)
-    hidden_gradient = dense_conv(
-        grad_second, block_diagonal(*flipped_pair(reversed_kernel(kernel_second)))
-    )
-    grad_first = (hidden_gradient * gelu_slope(pre_first)).astype(jnp.bfloat16)
-    total_sum = gradient.astype(jnp.float32) + dense_conv(
-        grad_first, block_diagonal(*flipped_pair(reversed_kernel(kernel_first)))
-    )
-    grad_sym = total_sum.astype(jnp.bfloat16)
-    grad_input = add_rounded(grad_sym[..., :channels], grad_sym[..., channels:])
-    result = jnp.concatenate([output, grad_input], -1)
-    result = lax.dynamic_slice_in_dim(result, core * CONVS, share, 0)
+    result = class_chains(
+        row_count,
+        part_cols,
+        own,
+        other,
+        tap_matrix(*flipped_pair(kernel_first)),
+        tap_matrix(*flipped_pair(kernel_second)),
+        tap_matrix(*flipped_pair(reversed_kernel(kernel_second))),
+        tap_matrix(*flipped_pair(reversed_kernel(kernel_first))),
+        jnp.tile(bias_first, 2)[None],
+        jnp.tile(bias_second, 2)[None],
+    )
 
     half = col_count // CORES
-    result = result.reshape(half, part_cols, row_count, part_rows, 2 * channels)
-    result = jnp.transpose(result, (2, 0, 1, 3, 4))[:, None]
+    result = result.reshape(row_count, 1, half, part_cols * part_rows, 2 * channels)
     result = jnp.broadcast_to(result, (row_count, CORES) + result.shape[2:])
     result = result.reshape(device_count, part_cols * part_rows, 2 * channels)
     back = lax.all_to_all(result, both, 0, 0, tiled=True)

time: 43.7 us -> 39.5 us (0.904)
  blocking collectives: 17.4 us -> 0 us
  waiting for transfers between devices: 10.3 us -> 18.6 us
  starting transfers between devices: 2.89 us -> 10.2 us
  matrix products: 2.7 us -> 0 us
  Pallas kernels: 0 us -> 2.35 us
  local copies, waits for them, and re-layouts: 6.63 us -> 4.96 us
    all_to_all x1 -> x0, blocking collectives: 17.4 us -> none  [by_classes(): own = lax.all_to_all(parts, both, 0, 0, tiled=True)]
    all_to_all x0 -> x1, waiting for transfers between devices: none -> 8.32 us  [by_classes(): own = lax.all_to_all(parts, both, 0, 0, tiled=True)]
    all_to_all x0 -> x1, starting transfers between devices: none -> 7.3 us  [by_classes(): own = lax.all_to_all(parts, both, 0, 0, tiled=True)]
    conv_general_dilated x4 -> x0, matrix products: 2.7 us -> none  [conv(): lax.conv_general_dilated(padded_input[None], conv_kernel, (1, 1), 'VALID'...]
    pallas_call x0 -> x1, Pallas kernels: none -> 2.35 us  [class_chains(): pl.pallas_call(functools.partial(class_kernel, row_count, part_cols), out...]
    unnamed x19 -> x8, local copies, waits for them, and re-layouts: 3.22 us -> 1.86 us
    transpose x1 -> x6, local copies, waits for them, and re-layouts: 0.01 us -> 1.02 us  [the longest x4 1 us: tap_matrix(): taps = jnp.transpose(block_diagonal(first, second), (0, 2, 1, 3))]
    convert_element_type x6 -> x0, other arithmetic: 0.93 us -> none  [the longest x1 0.25 us: by_classes(): (gradient.astype(jnp.float32) * gelu_slope(pre_second)).astype(jnp.bfloat16)]
  transfers between devices with their start and end apart: 2 -> 3, of which waited for: 1 -> 2; matrix products, arithmetic and copies ran while one was open for 1% -> 5% of each run, Pallas kernels for 0% -> 0%
where the time goes in v2:
time: 39.5 us; the launch traced here: 39.2 us
  waiting for transfers between devices  18.6 us (47%)
  starting transfers between devices  10.2 us (26%)
  local copies, waits for them, and re-layouts  4.96 us (13%)
  Pallas kernels  2.35 us (6%)
  other arithmetic  2.29 us (6%)
  between operations  0.83 us (2%)
    all_to_all x1, waiting for transfers between devices, by_classes(): back = lax.all_to_all(result, both, 0, 0, tiled=True)  10.3 us
    all_to_all x1, waiting for transfers between devices, by_classes(): own = lax.all_to_all(parts, both, 0, 0, tiled=True)  8.32 us
    all_to_all x1, starting transfers between devices, by_classes(): own = lax.all_to_all(parts, both, 0, 0, tiled=True)  7.3 us
    all_to_all x1, starting transfers between devices, by_classes(): back = lax.all_to_all(result, both, 0, 0, tiled=True)  2.58 us
    pallas_call x1, Pallas kernels, class_chains(): pl.pallas_call(functools.partial(class_kernel, row_count, part_cols), out...  2.35 us
    unnamed x8, local copies, waits for them, and re-layouts  1.86 us
    concatenate x1, other arithmetic, by_classes(): tile = jnp.concatenate([feature_map, cotangent], -1)  1.08 us
    transpose x4, local copies, waits for them, and re-layouts, tap_matrix(): taps = jnp.transpose(block_diagonal(first, second), (0, 2, 1, 3))  1 us
  transfers between devices with their start and end apart: 3, of which 2 were waited for; matrix products, arithmetic and copies ran while one was open for 5% of the time, Pallas kernels for 0%

profile of v2, /device:TPU:0, one launch (start us, length us, event | category | flops | bytes accessed | tf_op | source)
XLA Modules:
  0.0 39.2 jit_solution(11884964243394596738)
XLA Ops:
  0.6 1.1 %pad_maximum_fusion.1 = bf16[64,8,128]{2,1,0:T(8,128)(2,1)S(1)} fusion(bf16[64,8,64]{2,1,0:T(8,128)(2,1)} %param.11, bf16[64,8,64]{2,1,0:T(8,128)(2,1)} %param.6), kind=kLoop, calls=%fused_computation.27 | loop fusion | flops 262144 | bytes 262144 | tf_op jit(solution)/shard_map/concatenate | solution.py:228
  1.7 0.1 copy.65
  1.8 0.1 copy.66
  1.8 0.7 %pad_maximum_fusion = bf16[4,4,2,2,16,128]{5,4,3,2,1,0:T(8,128)(2,1)} fusion(bf16[4,4,1,2,16,128]{5,4,3,2,1,0:T(8,128)(2,1)S(1)} %bitcast.65, bf16[4,4,1,2,16,128]{5,4,3,2,1,0:T(8,128)(2,1)S(1)} %bitcast.66), kind=kLoop, calls=%fused_computation.24 | loop fusion | flops 131072 | bytes 524288 | tf_op jit(solution)/shard_map/stack | solution.py:231
  2.6 0.0 copy-start
  2.6 7.3 %all-to-all-start = ((bf16[32,32,128]{2,1,0:T(8,128)(2,1)}), bf16[32,32,128]{2,1,0:T(8,128)(2,1)S(1)}, u32[]{:S(2)}, u32[]{:S(2)}) async-start(bf16[32,32,128]{2,1,0:T(8,128)(2,1)} %bitcast.5), calls=%async_computation | async-start | bytes 524288 | tf_op jit(solution)/shard_map/all_to_all | solution.py:233
  9.9 0.0 copy-done
  9.9 0.0 copy-start.1
  9.9 0.9 %copy-done.1 = bf16[3,3,64,64]{3,2,1,0:T(8,128)(2,1)S(1)} copy-done((bf16[3,3,64,64]{3,2,1,0:T(8,128)(2,1)S(1)}, bf16[3,3,64,64]{3,2,1,0:T(8,128)(2,1)}, u32[]{:S(2)}) %copy-start.1) | copy-done | bytes 73752
  10.8 0.1 fusion.11
  10.9 0.1 fusion.9
  11.1 0.3 copy.43
  11.3 0.3 copy.41
  11.6 0.1 fusion.15
  11.8 0.1 copy_bitcast_fusion.2
  11.8 8.3 %all-to-all-done.own = bf16[32,32,128]{2,1,0:T(8,128)(2,1)S(1)} async-done(((bf16[32,32,128]{2,1,0:T(8,128)(2,1)}), bf16[32,32,128]{2,1,0:T(8,128)(2,1)S(1)}, u32[]{:S(2)}, u32[]{:S(2)}) %all-to-all-start) | async-done | bytes 262176 | tf_op jit(solution)/shard_map/all_to_all | solution.py:233
  20.2 0.3 collective-permute-start
  20.5 0.1 fusion.13
  20.6 0.2 copy.47
  20.9 0.0 copy-start.2
  20.9 0.2 copy.45
  21.1 0.4 %copy-done.2 = f32[64]{0:T(128)S(1)} copy-done((f32[64]{0:T(128)S(1)}, f32[64]{0:T(128)}, u32[]{:S(2)}) %copy-start.2) | copy-done | bytes 280
  21.5 0.0 copy-start.3
  21.5 0.1 broadcast_in_dim_tile.6.bias_first
  21.6 0.6 %copy-done.3 = f32[64]{0:T(128)S(1)} copy-done((f32[64]{0:T(128)S(1)}, f32[64]{0:T(128)}, u32[]{:S(2)}) %copy-start.3) | copy-done | bytes 280
  22.2 0.1 broadcast_in_dim_tile.7.bias_second
  22.3 0.1 copy_bitcast_fusion
  22.3 0.0 collective-permute-done.other
  22.4 2.3 %shard_map.77 = bf16[16,32,128]{2,1,0:T(8,128)(2,1)S(1)} custom-call(bf16[32,32,128]{2,1,0:T(8,128)(2,1)S(1)} %all-to-all-done.own, bf16[32,32,128]{2,1,0:T(8,128)(2,1)S(1)} %collective-permute-done.other, bf16[384,384]{1,0:T(8,128)(2,1)S(1)} %get-tuple-element.7.weight_first, bf16[384,384]{1,0:T(8,128)(2,1)S(1)} %get-tuple-element.6.weight_second, ...), custom_call_target="tpu_custom_call" | custom-call | tf_op jit(solution)/shard_map/pallas_call | solution.py:208
  24.7 0.8 %broadcast_in_dim.8 = bf16[2,2,8,32,128]{4,3,2,1,0:T(8,128)(2,1)} broadcast(bf16[2,8,32,128]{3,2,1,0:T(8,128)(2,1)S(1)} %bitcast.54), dimensions={0,2,3,4} | broadcast | bytes 393216 | tf_op jit(solution)/shard_map/broadcast_in_dim | solution.py:250
  25.5 2.6 %all-to-all-start.1 = ((bf16[32,32,128]{2,1,0:T(8,128)(2,1)}), bf16[32,32,128]{2,1,0:T(8,128)(2,1)S(1)}, u32[]{:S(2)}, u32[]{:S(2)}) async-start(bf16[32,32,128]{2,1,0:T(8,128)(2,1)} %bitcast.17), calls=%async_computation.1 | async-start | bytes 524288 | tf_op jit(solution)/shard_map/all_to_all | solution.py:252
  28.1 10.3 %all-to-all-done.1 = bf16[32,32,128]{2,1,0:T(8,128)(2,1)S(1)} async-done(((bf16[32,32,128]{2,1,0:T(8,128)(2,1)}), bf16[32,32,128]{2,1,0:T(8,128)(2,1)S(1)}, u32[]{:S(2)}, u32[]{:S(2)}) %all-to-all-start.1) | async-done | bytes 262176 | tf_op jit(solution)/shard_map/all_to_all | solution.py:252
  38.4 0.1 copy.48
  38.4 0.8 %fusion.16 = (bf16[64,8,64]{2,1,0:T(8,128)(2,1)}, bf16[64,8,64]{2,1,0:T(8,128)(2,1)}) fusion(bf16[64,8,128]{2,1,0:T(8,128)(2,1)S(1)} %bitcast.63), kind=kLoop, calls=%fused_computation.33 | loop fusion | bytes 262144 | tf_op jit(solution)/shard_map/slice | solution.py:256
  (7 shorter events, 0.1 us)
Async XLA Ops:
  2.6 7.3 %copy-start = (bf16[3,3,64,64]{3,2,1,0:T(8,128)(2,1)S(1)}, bf16[3,3,64,64]{3,2,1,0:T(8,128)(2,1)}, u32[]{:S(2)}) copy-start(bf16[3,3,64,64]{3,2,1,0:T(8,128)(2,1)} %param.7) | copy-start | bytes 221188
  2.6 17.6 %all-to-all-start = ((bf16[32,32,128]{2,1,0:T(8,128)(2,1)}), bf16[32,32,128]{2,1,0:T(8,128)(2,1)S(1)}, u32[]{:S(2)}, u32[]{:S(2)}) async-start(bf16[32,32,128]{2,1,0:T(8,128)(2,1)} %bitcast.5), calls=%async_computation | async-start | bytes 524288 | tf_op jit(solution)/shard_map/all_to_all | solution.py:233
  9.9 0.9 %copy-start.1 = (bf16[3,3,64,64]{3,2,1,0:T(8,128)(2,1)S(1)}, bf16[3,3,64,64]{3,2,1,0:T(8,128)(2,1)}, u32[]{:S(2)}) copy-start(bf16[3,3,64,64]{3,2,1,0:T(8,128)(2,1)} %param.9) | copy-start | bytes 221188
  20.2 2.2 %collective-permute-start = (bf16[32,32,128]{2,1,0:T(8,128)(2,1)S(1)}, bf16[32,32,128]{2,1,0:T(8,128)(2,1)S(1)}, u32[]{:S(2)}, u32[]{:S(2)}) collective-permute-start(bf16[32,32,128]{2,1,0:T(8,128)(2,1)S(1)} %all-to-all-done.own), channel_id=1, source_target_pairs={{0,1},{1,0},{2,3},{3,2},{4,5},{5,4},{6,7},{7,6},{8,9},{9,8},{10,11... | collective-permute-start | bytes 786440 | tf_op jit(solution)/shard_map/ppermute | solution.py:234
  20.9 0.7 %copy-start.2 = (f32[64]{0:T(128)S(1)}, f32[64]{0:T(128)}, u32[]{:S(2)}) copy-start(f32[64]{0:T(128)} %param.8) | copy-start | bytes 772
  21.5 0.7 %copy-start.3 = (f32[64]{0:T(128)S(1)}, f32[64]{0:T(128)}, u32[]{:S(2)}) copy-start(f32[64]{0:T(128)} %param.10) | copy-start | bytes 772
  25.5 12.9 %all-to-all-start.1 = ((bf16[32,32,128]{2,1,0:T(8,128)(2,1)}), bf16[32,32,128]{2,1,0:T(8,128)(2,1)S(1)}, u32[]{:S(2)}, u32[]{:S(2)}) async-start(bf16[32,32,128]{2,1,0:T(8,128)(2,1)} %bitcast.17), calls=%async_computation.1 | async-start | bytes 524288 | tf_op jit(solution)/shard_map/all_to_all | solution.py:252

commit v3 on v2

--- a/solution.py
+++ b/solution.py
@@ -8,7 +8,7 @@
 from jax.sharding import PartitionSpec as P
 
 DILATION_STEP = 4
-CORES = 2
+HALVES = 2
 CONVS = 4
 
 
@@ -115,6 +115,42 @@
 def tap_matrix(first, second):
     taps = jnp.transpose(block_diagonal(first, second), (0, 2, 1, 3))
     return taps.reshape(taps.shape[0] * taps.shape[1], -1)
+
+
+def class_order():
+    step = range(DILATION_STEP)
+    uneven = [[(a, b), (b, a)] for a in step for b in step if a < b]
+    return sum(uneven, []) + [(a, a) for a in step]
+
+
+def part_kernel(tile_cols, tile, parts):
+    step = DILATION_STEP
+    part_cols = tile_cols // step
+    part_rows = tile.shape[0] // (tile_cols * step)
+    for index, (a, b) in enumerate(class_order()):
+        columns = [
+            tile[pl.ds(a * tile_cols + k * step + b, part_rows, stride=step * tile_cols), :]
+            for k in range(part_cols)
+        ]
+        part = jnp.concatenate(columns, 0).astype(jnp.bfloat16)
+        r, c = divmod(index, parts.shape[2])
+        for half in range(HALVES):
+            parts[r, half, c] = part
+
+
+def class_parts(row_count, feature_map, cotangent):
+    tile_rows, tile_cols, channels = feature_map.shape
+    classes = DILATION_STEP * DILATION_STEP
+    cells = tile_rows * tile_cols
+    shape = (row_count, HALVES, classes // row_count, cells // classes, 2 * channels)
+    tile = jnp.concatenate([feature_map, cotangent], 2).astype(jnp.float32)
+    return pl.pallas_call(
+        functools.partial(part_kernel, tile_cols),
+        out_shape=jax.ShapeDtypeStruct(shape, jnp.bfloat16),
+        in_specs=[pl.BlockSpec(memory_space=pltpu.VMEM)],
+        out_specs=pl.BlockSpec(memory_space=pltpu.VMEM),
+        compiler_params=pltpu.CompilerParams(vmem_limit_bytes=16 * 2**20),
+    )(tile.reshape(cells, 2 * channels))
 
 
 def class_kernel(
@@ -136,25 +172,28 @@
     channels = width // 2
     part_rows = part // part_cols
     col_count = blocks // row_count
+    half_count = col_count // HALVES
     class_cols, class_rows = col_count * part_cols, row_count * part_rows
-    share = class_cols // CORES
+    share = class_cols // HALVES
     count = share + CONVS
-    core = lax.rem(lax.axis_index("col"), CORES)
-    begin = core * (share - CONVS)
-    low = lax.broadcasted_iota(jnp.int32, (count * class_rows, width), 1) < channels
-    place = lax.rem(lax.broadcasted_iota(jnp.int32, (count * class_rows, width), 0), class_rows)
+    column = lax.axis_index("col")
+    half = lax.div(column, half_count)
+    place = lax.axis_index("row") * half_count + lax.rem(column, half_count)
+    even = place >= len(class_order()) - DILATION_STEP
+    begin = half * (share - CONVS)
+    cells = count * class_rows
+    low = lax.broadcasted_iota(jnp.int32, (cells, width), 1) < channels
+    row = lax.rem(lax.broadcasted_iota(jnp.int32, (cells, width), 0), class_rows)
 
     pieces = []
     for r in range(row_count):
-        reach = pl.ds(r * col_count + core * ((share - CONVS) // part_cols), count // part_cols)
-        piece = jnp.where(core == 0, own[reach], other[reach])
-        pieces.append(piece.reshape(count, part_rows, width))
-    straight = jnp.concatenate(pieces, 1).astype(jnp.float32)
-    straight = straight.reshape(count * class_rows, width)
+        reach = pl.ds(r * col_count + half * ((share - CONVS) // part_cols), count // part_cols)
+        pieces.append(own[reach].reshape(count, part_rows, width))
+    straight = jnp.concatenate(pieces, 1).astype(jnp.float32).reshape(cells, width)
 
     for r in range(row_count):
-        reach = pl.ds(r * col_count, col_count)
-        piece = jnp.where(core == 0, other[reach], own[reach]).astype(jnp.float32)
+        reach = slice(r * col_count, (r + 1) * col_count)
+        piece = jnp.where(even, own[reach], other[reach]).astype(jnp.float32)
         piece = piece.reshape(class_cols, part_rows, width)
         for k in range(class_cols):
             turning[pl.ds(k * class_rows + r * part_rows, part_rows), :] = piece[k]
@@ -174,9 +213,9 @@
             matrix[...],
             preferred_element_type=jnp.float32,
         )
-        above = jnp.where(place == 0, 0.0, pltpu.roll(taps[:, :width], 1, 0))
-        below = pltpu.roll(taps[:, 2 * width :], count * class_rows - 1, 0)
-        below = jnp.where(place == class_rows - 1, 0.0, below)
+        above = jnp.where(row == 0, 0.0, pltpu.roll(taps[:, :width], 1, 0))
+        below = pltpu.roll(taps[:, 2 * width :], cells - 1, 0)
+        below = jnp.where(row == class_rows - 1, 0.0, below)
         return above + taps[:, width : 2 * width] + below
 
     symmetric = straight + turned
@@ -192,27 +231,28 @@
     grad_first = (tap_sum(grad_second, weight_third) * slope_first).astype(jnp.bfloat16)
     grad_sym = (gradient + tap_sum(grad_first, weight_fourth)).astype(jnp.bfloat16)
     grad_sym = grad_sym.astype(jnp.float32)
-    both_results = jnp.where(low, output, grad_sym + swapped(grad_sym)).astype(jnp.bfloat16)
-    window[...] = both_results.reshape(count, class_rows, width)
-    kept = window[pl.ds(core * CONVS, share)]
-    half = share // part_cols
-    for r in range(row_count):
-        piece = kept[:, r * part_rows : (r + 1) * part_rows]
-        result[r * half : (r + 1) * half] = piece.reshape(half, part, width)
+    finished = jnp.where(low, output, grad_sym + swapped(grad_sym)).astype(jnp.bfloat16)
+    window[...] = finished.reshape(count, class_rows, width)
+
+    for index, (a, b) in enumerate(class_order()):
+        r, c = divmod(index, half_count)
+        kept = window[pl.ds(half * CONVS + c * part_cols, part_cols)]
+        kept = kept[:, r * part_rows : (r + 1) * part_rows]
+        result[a * DILATION_STEP + b] = kept.reshape(part, width)
 
 
 def class_chains(row_count, part_cols, own, other, *parameters):
     blocks, part, width = own.shape
     class_cols, class_rows = blocks // row_count * part_cols, row_count * (part // part_cols)
-    share = class_cols // CORES
+    count = class_cols // HALVES + CONVS
     return pl.pallas_call(
         functools.partial(class_kernel, row_count, part_cols),
-        out_shape=jax.ShapeDtypeStruct((blocks // CORES, part, width), jnp.bfloat16),
+        out_shape=jax.ShapeDtypeStruct((blocks // HALVES, part, width), jnp.bfloat16),
         in_specs=[pl.BlockSpec(memory_space=pltpu.VMEM)] * 8,
         out_specs=pl.BlockSpec(memory_space=pltpu.VMEM),
         scratch_shapes=[
             pltpu.VMEM((class_cols * class_rows, width), jnp.float32),
-            pltpu.VMEM((share + CONVS, class_rows, width), jnp.bfloat16),
+            pltpu.VMEM((count, class_rows, width), jnp.bfloat16),
         ],
         compiler_params=pltpu.CompilerParams(vmem_limit_bytes=32 * 2**20),
     )(own, other, *parameters)
@@ -220,23 +260,14 @@
 
 def by_classes(feature_map, kernel_first, bias_first, kernel_second, bias_second, cotangent):
     row_count, col_count = lax.axis_size("row"), lax.axis_size("col")
-    device_count = row_count * col_count
     tile_rows, tile_cols, channels = feature_map.shape
     step = DILATION_STEP
     part_rows, part_cols = tile_rows // step, tile_cols // step
 
-    tile = jnp.concatenate([feature_map, cotangent], -1)
-    parts = tile.reshape(part_rows, step, part_cols, step, 2 * channels)
-    parts = jnp.transpose(parts, (1, 3, 2, 0, 4))
-    parts = jnp.stack([parts, jnp.swapaxes(parts, 0, 1)], 2)
-    parts = parts.reshape(device_count, part_cols * part_rows, 2 * channels)
+    parts = class_parts(row_count, feature_map, cotangent)
+    parts = parts.reshape(row_count * col_count, part_cols * part_rows, 2 * channels)
     own = lax.all_to_all(parts, both, 0, 0, tiled=True)
-    other = lax.ppermute(own, "col", [(i, i ^ 1) for i in range(col_count)])
-    result = class_chains(
-        row_count,
-        part_cols,
-        own,
-        other,
+    parameters = (
         tap_matrix(*flipped_pair(kernel_first)),
         tap_matrix(*flipped_pair(kernel_second)),
         tap_matrix(*flipped_pair(reversed_kernel(kernel_second))),
@@ -244,14 +275,18 @@
         jnp.tile(bias_first, 2)[None],
         jnp.tile(bias_second, 2)[None],
     )
-
-    half = col_count // CORES
-    result = result.reshape(row_count, 1, half, part_cols * part_rows, 2 * channels)
-    result = jnp.broadcast_to(result, (row_count, CORES) + result.shape[2:])
-    result = result.reshape(device_count, part_cols * part_rows, 2 * channels)
-    back = lax.all_to_all(result, both, 0, 0, tiled=True)
-    back = back.reshape(step, step, CORES, part_cols, part_rows, 2 * channels)
-    back = lax.dynamic_index_in_dim(back, lax.axis_index("col") // half, 2, keepdims=False)
+    own, *parameters = lax.optimization_barrier((own,) + parameters)
+    other = lax.ppermute(own, "col", [(i, i ^ 1) for i in range(col_count)])
+    result = class_chains(row_count, part_cols, own, other, *parameters)
+
+    half_count = col_count // HALVES
+    order = sorted(range(step * step), key=lambda index: class_order()[index])
+    halves = [
+        [i // half_count * col_count + h * half_count + i % half_count for i in order]
+        for h in range(HALVES)
+    ]
+    back = lax.all_to_all(result, both, 0, 0, axis_index_groups=halves, tiled=True)
+    back = back.reshape(step, step, part_cols, part_rows, 2 * channels)
     back = jnp.transpose(back, (3, 0, 2, 1, 4)).reshape(tile_rows, tile_cols, 2 * channels)
     return back[..., :channels], back[..., channels:]
 
@@ -259,13 +294,15 @@
 def solution(mesh):
     row_count, col_count = mesh.shape["row"], mesh.shape["col"]
     classes = DILATION_STEP * DILATION_STEP
-    paired = row_count * col_count == CORES * classes and col_count % CORES == 0
+    paired = row_count * col_count == HALVES * classes and col_count % (2 * HALVES) == 0
     in_specs = (P("row", "col", None), P(), P(), P(), P(), P("row", "col", None))
     out_specs = (P("row", "col", None), P("row", "col", None))
 
     def whole(feature_map, *others):
         size = feature_map.shape[0]
+        part_rows, part_cols = size // row_count // DILATION_STEP, size // col_count // DILATION_STEP
         fits = size % (DILATION_STEP * row_count) == 0 and size % (DILATION_STEP * col_count) == 0
+        fits = fits and part_rows % 16 == 0 and CONVS % part_cols == 0
         per_device = by_classes if paired and fits else by_tiles
         return jax.shard_map(
             per_device, mesh=mesh, in_specs=in_specs, out_specs=out_specs, check_vma=False

time: 39.5 us -> 34.1 us (0.86)
  waiting for transfers between devices: 18.6 us -> 7.68 us
  blocking collectives: 0 us -> 8.91 us
  starting transfers between devices: 10.2 us -> 7.6 us
  local copies, waits for them, and re-layouts: 4.96 us -> 4.09 us
  Pallas kernels: 2.35 us -> 3.19 us
  other arithmetic: 2.29 us -> 1.56 us
    all_to_all x1 -> x0, waiting for transfers between devices: 10.3 us -> none  [by_classes(): back = lax.all_to_all(result, both, 0, 0, tiled=True)]
    all_to_all x0 -> x1, blocking collectives: none -> 8.91 us  [by_classes(): lax.all_to_all(result, both, 0, 0, axis_index_groups=halves, tiled=True)]
    all_to_all x1 -> x0, starting transfers between devices: 2.58 us -> none  [by_classes(): back = lax.all_to_all(result, both, 0, 0, tiled=True)]
    all_to_all x1, waiting for transfers between devices: 8.32 us -> 6.45 us  [by_classes(): own = lax.all_to_all(parts, both, 0, 0, tiled=True)]
    ppermute x1, waiting for transfers between devices: 0.01 us -> 1.23 us  [by_classes(): other = lax.ppermute(own, 'col', [(i, i ^ 1) for i in range(col_count)])]
    concatenate x1 -> x0, other arithmetic: 1.08 us -> none  [by_classes(): tile = jnp.concatenate([feature_map, cotangent], -1)]
    convert_element_type x0 -> x1, other arithmetic: none -> 1.08 us  [class_parts(): tile = jnp.concatenate([feature_map, cotangent], 2).astype(jnp.float32)]
    pallas_call x0 -> x1, Pallas kernels: none -> 0.85 us  [class_parts(): pl.pallas_call(functools.partial(part_kernel, tile_cols), out_shape=jax.S...]
  transfers between devices with their start and end apart: 3 -> 2, of which waited for: 2 -> 2; matrix products, arithmetic and copies ran while one was open for 5% -> 6% of each run, Pallas kernels for 0% -> 0%
where the time goes in v3:
time: 34.1 us; the launch traced here: 33.8 us
  blocking collectives  8.91 us (26%)
  waiting for transfers between devices  7.68 us (23%)
  starting transfers between devices  7.6 us (22%)
  local copies, waits for them, and re-layouts  4.09 us (12%)
  Pallas kernels  3.19 us (9%)
  other arithmetic  1.56 us (5%)
  between operations  0.77 us (2%)
    all_to_all x1, blocking collectives, by_classes(): lax.all_to_all(result, both, 0, 0, axis_index_groups=halves, tiled=True)  8.91 us
    all_to_all x1, starting transfers between devices, by_classes(): own = lax.all_to_all(parts, both, 0, 0, tiled=True)  7.3 us
    all_to_all x1, waiting for transfers between devices, by_classes(): own = lax.all_to_all(parts, both, 0, 0, tiled=True)  6.45 us
    pallas_call x1, Pallas kernels, class_chains(): pl.pallas_call(functools.partial(class_kernel, row_count, part_cols), out...  2.34 us
    unnamed x8, local copies, waits for them, and re-layouts  1.85 us
    ppermute x1, waiting for transfers between devices, by_classes(): other = lax.ppermute(own, 'col', [(i, i ^ 1) for i in range(col_count)])  1.23 us
    convert_element_type x1, other arithmetic, class_parts(): tile = jnp.concatenate([feature_map, cotangent], 2).astype(jnp.float32)  1.08 us
    transpose x4, local copies, waits for them, and re-layouts, tap_matrix(): taps = jnp.transpose(block_diagonal(first, second), (0, 2, 1, 3))  1 us
  transfers between devices with their start and end apart: 2, of which 2 were waited for; matrix products, arithmetic and copies ran while one was open for 6% of the time, Pallas kernels for 0%

profile of v3, /device:TPU:0, one launch (start us, length us, event | category | flops | bytes accessed | tf_op | source)
XLA Modules:
  0.0 33.8 jit_solution(6352760322610072016)
XLA Ops:
  0.6 1.1 %maximum_convert_fusion.tile = f32[512,128]{1,0:T(8,128)S(1)} fusion(bf16[512,64]{1,0:T(8,128)(2,1)} %bitcast.49, bf16[512,64]{1,0:T(8,128)(2,1)} %bitcast.50), kind=kLoop, calls=%fused_computation.26 | loop fusion | flops 262144 | bytes 393216 | tf_op jit(solution)/shard_map/convert_element_type | solution.py:146
  1.7 0.8 %shard_map.77 = bf16[2,2,8,32,128]{4,3,2,1,0:T(8,128)(2,1)} custom-call(f32[512,128]{1,0:T(8,128)S(1)} %maximum_convert_fusion.tile), custom_call_target="tpu_custom_call" | custom-call | tf_op jit(solution)/shard_map/pallas_call | solution.py:147
  2.6 0.0 copy-start.1
  2.6 7.3 %all-to-all-start = ((bf16[32,32,128]{2,1,0:T(8,128)(2,1)}), bf16[32,32,128]{2,1,0:T(8,128)(2,1)S(1)}, u32[]{:S(2)}, u32[]{:S(2)}) async-start(bf16[32,32,128]{2,1,0:T(8,128)(2,1)} %bitcast.2), calls=%async_computation | async-start | bytes 524288 | tf_op jit(solution)/shard_map/all_to_all | solution.py:269
  9.9 0.0 copy-done.1
  9.9 0.0 copy-start
  9.9 0.9 %copy-done = bf16[3,3,64,64]{3,2,1,0:T(8,128)(2,1)S(1)} copy-done((bf16[3,3,64,64]{3,2,1,0:T(8,128)(2,1)S(1)}, bf16[3,3,64,64]{3,2,1,0:T(8,128)(2,1)}, u32[]{:S(2)}) %copy-start) | copy-done | bytes 73752
  10.8 0.1 fusion.13
  11.0 0.2 copy.22
  11.2 0.1 fusion.15
  11.4 0.2 copy.24
  11.6 0.1 fusion.9
  11.7 0.3 copy.18
  12.0 0.1 fusion.11
  12.1 0.0 copy-start.2
  12.1 0.3 copy.20
  12.4 0.4 %copy-done.2 = f32[64]{0:T(128)S(1)} copy-done((f32[64]{0:T(128)S(1)}, f32[64]{0:T(128)}, u32[]{:S(2)}) %copy-start.2) | copy-done | bytes 280
  12.8 0.0 copy-start.3
  12.8 0.1 broadcast_in_dim_tile.6.bias_first
  12.9 0.6 %copy-done.3 = f32[64]{0:T(128)S(1)} copy-done((f32[64]{0:T(128)S(1)}, f32[64]{0:T(128)}, u32[]{:S(2)}) %copy-start.3) | copy-done | bytes 280
  13.4 0.1 broadcast_in_dim_tile.7.bias_second
  13.5 0.1 copy_bitcast_fusion
  13.6 0.1 copy_bitcast_fusion.2
  13.7 6.4 %all-to-all-done.own = bf16[32,32,128]{2,1,0:T(8,128)(2,1)S(1)} async-done(((bf16[32,32,128]{2,1,0:T(8,128)(2,1)}), bf16[32,32,128]{2,1,0:T(8,128)(2,1)S(1)}, u32[]{:S(2)}, u32[]{:S(2)}) %all-to-all-start) | async-done | bytes 262176 | tf_op jit(solution)/shard_map/all_to_all | solution.py:269
  20.2 0.3 collective-permute-start
  20.5 1.2 %collective-permute-done.other = bf16[32,32,128]{2,1,0:T(8,128)(2,1)S(1)} collective-permute-done((bf16[32,32,128]{2,1,0:T(8,128)(2,1)S(1)}, bf16[32,32,128]{2,1,0:T(8,128)(2,1)S(1)}, u32[]{:S(2)}, u32[]{:S(2)}) %collective-permute-start) | collective-permute-done | bytes 262176 | tf_op jit(solution)/shard_map/ppermute | solution.py:279
  21.7 2.3 %shard_map.78 = bf16[16,32,128]{2,1,0:T(8,128)(2,1)S(1)} custom-call(bf16[32,32,128]{2,1,0:T(8,128)(2,1)S(1)} %all-to-all-done.own, bf16[32,32,128]{2,1,0:T(8,128)(2,1)S(1)} %collective-permute-done.other, bf16[384,384]{1,0:T(8,128)(2,1)S(1)} %get-tuple-element.10.weight_first, bf16[384,384]{1,0:T(8,128)(2,1)S(1)} %get-tuple-element.11.weight_second, ...), custom_call_target="tpu_custom_call" | custom-call | tf_op jit(solution)/shard_map/pallas_call | solution.py:248
  24.0 8.9 %all_to_all.10 = bf16[16,32,128]{2,1,0:T(8,128)(2,1)S(1)} all-to-all(bf16[16,32,128]{2,1,0:T(8,128)(2,1)S(1)} %shard_map.78), channel_id=1, replica_groups={{20,0,2,4,1,21,6,16,3,7,22,18,5,17,19,23},{28,8,10,12,9,29,14,24,11,15,..., dimensions={0} | all-to-all | bytes 262144 | tf_op jit(solution)/shard_map/all_to_all | solution.py:288
  33.0 0.1 copy.25
  33.0 0.8 %fusion.16 = (bf16[64,8,64]{2,1,0:T(8,128)(2,1)}, bf16[64,8,64]{2,1,0:T(8,128)(2,1)}) fusion(bf16[64,8,128]{2,1,0:T(8,128)(2,1)S(1)} %bitcast.47), kind=kLoop, calls=%fused_computation.29 | loop fusion | bytes 262144 | tf_op jit(solution)/shard_map/slice | solution.py:291
  (6 shorter events, 0.0 us)
Async XLA Ops:
  2.6 7.3 %copy-start.1 = (bf16[3,3,64,64]{3,2,1,0:T(8,128)(2,1)S(1)}, bf16[3,3,64,64]{3,2,1,0:T(8,128)(2,1)}, u32[]{:S(2)}) copy-start(bf16[3,3,64,64]{3,2,1,0:T(8,128)(2,1)} %param.9) | copy-start | bytes 221188
  2.6 17.6 %all-to-all-start = ((bf16[32,32,128]{2,1,0:T(8,128)(2,1)}), bf16[32,32,128]{2,1,0:T(8,128)(2,1)S(1)}, u32[]{:S(2)}, u32[]{:S(2)}) async-start(bf16[32,32,128]{2,1,0:T(8,128)(2,1)} %bitcast.2), calls=%async_computation | async-start | bytes 524288 | tf_op jit(solution)/shard_map/all_to_all | solution.py:269
  9.9 0.9 %copy-start = (bf16[3,3,64,64]{3,2,1,0:T(8,128)(2,1)S(1)}, bf16[3,3,64,64]{3,2,1,0:T(8,128)(2,1)}, u32[]{:S(2)}) copy-start(bf16[3,3,64,64]{3,2,1,0:T(8,128)(2,1)} %param.7) | copy-start | bytes 221188
  12.1 0.7 %copy-start.2 = (f32[64]{0:T(128)S(1)}, f32[64]{0:T(128)}, u32[]{:S(2)}) copy-start(f32[64]{0:T(128)} %param.8) | copy-start | bytes 772
  12.8 0.7 %copy-start.3 = (f32[64]{0:T(128)S(1)}, f32[64]{0:T(128)}, u32[]{:S(2)}) copy-start(f32[64]{0:T(128)} %param.10) | copy-start | bytes 772
  20.2 1.5 %collective-permute-start = (bf16[32,32,128]{2,1,0:T(8,128)(2,1)S(1)}, bf16[32,32,128]{2,1,0:T(8,128)(2,1)S(1)}, u32[]{:S(2)}, u32[]{:S(2)}) collective-permute-start(bf16[32,32,128]{2,1,0:T(8,128)(2,1)S(1)} %all-to-all-done.own), channel_id=1, source_target_pairs={{0,1},{1,0},{2,3},{3,2},{4,5},{5,4},{6,7},{7,6},{8,9},{9,8},{10,11... | collective-permute-start | bytes 786440 | tf_op jit(solution)/shard_map/ppermute | solution.py:279

commit v4 on v3

--- a/solution.py
+++ b/solution.py
@@ -101,20 +101,41 @@
     return output, add_rounded(grad_sym, mirror(grad_sym))
 
 
-def flipped_pair(conv_kernel):
-    return jnp.transpose(conv_kernel, (1, 0, 2, 3)), conv_kernel
-
-
-def block_diagonal(first, second):
-    zeros = jnp.zeros_like(first)
-    return jnp.concatenate(
-        [jnp.concatenate([first, zeros], 3), jnp.concatenate([zeros, second], 3)], 2
-    )
-
-
-def tap_matrix(first, second):
-    taps = jnp.transpose(block_diagonal(first, second), (0, 2, 1, 3))
-    return taps.reshape(taps.shape[0] * taps.shape[1], -1)
+def matrix_kernel(weight_first, weight_second, bias_first, bias_second, *outputs):
+    first, second, third, fourth, first_bias, second_bias = outputs
+    taps, channels = weight_first.shape[0], weight_first.shape[2]
+    gap = jnp.zeros(weight_first.shape[2:], weight_first.dtype)
+    for weight, ahead, behind in (
+        (weight_first, first, fourth),
+        (weight_second, second, third),
+    ):
+        for p in range(taps):
+            for q in range(taps):
+                upper = jnp.concatenate([weight[q, p], gap], 1)
+                lower = jnp.concatenate([gap, weight[p, q]], 1)
+                block = jnp.concatenate([upper, lower], 0)
+                ahead[pl.ds(2 * channels * p, 2 * channels), pl.ds(2 * channels * q, 2 * channels)] = block
+                p_back, q_back = taps - 1 - p, taps - 1 - q
+                behind[
+                    pl.ds(2 * channels * q_back, 2 * channels),
+                    pl.ds(2 * channels * p_back, 2 * channels),
+                ] = block
+    for bias, wide in ((bias_first, first_bias), (bias_second, second_bias)):
+        wide[...] = jnp.concatenate([bias[...], bias[...]], 1)
+
+
+def chain_matrices(weight_first, weight_second, bias_first, bias_second):
+    taps, channels = weight_first.shape[0], weight_first.shape[2]
+    size = taps * 2 * channels
+    vmem = pl.BlockSpec(memory_space=pltpu.VMEM)
+    return pl.pallas_call(
+        matrix_kernel,
+        out_shape=[jax.ShapeDtypeStruct((size, size), jnp.bfloat16)] * 4
+        + [jax.ShapeDtypeStruct((1, 2 * channels), jnp.float32)] * 2,
+        in_specs=[vmem] * 4,
+        out_specs=[vmem] * 6,
+        compiler_params=pltpu.CompilerParams(vmem_limit_bytes=16 * 2**20),
+    )(weight_first, weight_second, bias_first[None], bias_second[None])
 
 
 def class_order():
@@ -204,13 +225,14 @@
     def swapped(value):
         return pltpu.roll(value, channels, 1)
 
-    def tap_sum(image, matrix):
+    def tap_sum(image, matrix, dimension):
         gap = jnp.zeros((class_rows, width), image.dtype)
         before = jnp.concatenate([gap, image[:-class_rows]], 0)
         after = jnp.concatenate([image[class_rows:], gap], 0)
-        taps = jnp.dot(
+        taps = lax.dot_general(
             jnp.concatenate([before, image, after], 1),
             matrix[...],
+            (((1,), (dimension,)), ((), ())),
             preferred_element_type=jnp.float32,
         )
         above = jnp.where(row == 0, 0.0, pltpu.roll(taps[:, :width], 1, 0))
@@ -222,14 +244,14 @@
     symmetric = jnp.where(low, symmetric, swapped(symmetric)).astype(jnp.bfloat16)
     gradient = jnp.where(low, swapped(straight), turned)
 
-    pre_first = tap_sum(symmetric, weight_first) + bias_first[...]
+    pre_first = tap_sum(symmetric, weight_first, 0) + bias_first[...]
     hidden = gelu_value(pre_first).astype(jnp.bfloat16)
     slope_first = gelu_slope(pre_first)
-    pre_second = tap_sum(hidden, weight_second) + bias_second[...]
+    pre_second = tap_sum(hidden, weight_second, 0) + bias_second[...]
     output = symmetric.astype(jnp.float32) + gelu_value(pre_second)
     grad_second = (gradient * gelu_slope(pre_second)).astype(jnp.bfloat16)
-    grad_first = (tap_sum(grad_second, weight_third) * slope_first).astype(jnp.bfloat16)
-    grad_sym = (gradient + tap_sum(grad_first, weight_fourth)).astype(jnp.bfloat16)
+    grad_first = (tap_sum(grad_second, weight_third, 1) * slope_first).astype(jnp.bfloat16)
+    grad_sym = (gradient + tap_sum(grad_first, weight_fourth, 1)).astype(jnp.bfloat16)
     grad_sym = grad_sym.astype(jnp.float32)
     finished = jnp.where(low, output, grad_sym + swapped(grad_sym)).astype(jnp.bfloat16)
     window[...] = finished.reshape(count, class_rows, width)
@@ -267,17 +289,10 @@
     parts = class_parts(row_count, feature_map, cotangent)
     parts = parts.reshape(row_count * col_count, part_cols * part_rows, 2 * channels)
     own = lax.all_to_all(parts, both, 0, 0, tiled=True)
-    parameters = (
-        tap_matrix(*flipped_pair(kernel_first)),
-        tap_matrix(*flipped_pair(kernel_second)),
-        tap_matrix(*flipped_pair(reversed_kernel(kernel_second))),
-        tap_matrix(*flipped_pair(reversed_kernel(kernel_first))),
-        jnp.tile(bias_first, 2)[None],
-        jnp.tile(bias_second, 2)[None],
-    )
-    own, *parameters = lax.optimization_barrier((own,) + parameters)
+    raw = (kernel_first, kernel_second, bias_first, bias_second)
+    own, *raw = lax.optimization_barrier((own,) + raw)
     other = lax.ppermute(own, "col", [(i, i ^ 1) for i in range(col_count)])
-    result = class_chains(row_count, part_cols, own, other, *parameters)
+    result = class_chains(row_count, part_cols, own, other, *chain_matrices(*raw))
 
     half_count = col_count // HALVES
     order = sorted(range(step * step), key=lambda index: class_order()[index])

time: 34.1 us -> 33.2 us (0.974)
  blocking collectives: 8.91 us -> 26.3 us
  waiting for transfers between devices: 7.68 us -> 0.36 us
  starting transfers between devices: 7.6 us -> 0.3 us
  local copies, waits for them, and re-layouts: 4.09 us -> 1.51 us
  Pallas kernels: 3.19 us -> 2.69 us
  other arithmetic: 1.56 us -> 1.08 us
    all_to_all x0 -> x1, blocking collectives: none -> 17.4 us  [by_classes(): own = lax.all_to_all(parts, both, 0, 0, tiled=True)]
    all_to_all x1 -> x0, starting transfers between devices: 7.3 us -> none  [by_classes(): own = lax.all_to_all(parts, both, 0, 0, tiled=True)]
    all_to_all x1 -> x0, waiting for transfers between devices: 6.45 us -> none  [by_classes(): own = lax.all_to_all(parts, both, 0, 0, tiled=True)]
    unnamed x8, local copies, waits for them, and re-layouts: 1.85 us -> 0.67 us
    transpose x6 -> x0, local copies, waits for them, and re-layouts: 1.03 us -> none  [the longest x4 1 us: tap_matrix(): taps = jnp.transpose(block_diagonal(first, second), (0, 2, 1, 3))]
    ppermute x1, waiting for transfers between devices: 1.23 us -> 0.36 us  [by_classes(): other = lax.ppermute(own, 'col', [(i, i ^ 1) for i in range(col_count)])]
    pallas_call x1, Pallas kernels: 0.85 us -> 0.15 us  [class_parts(): pl.pallas_call(functools.partial(part_kernel, tile_cols), out_shape=jax.S...]
    transpose x4 -> x0, other arithmetic: 0.48 us -> none  [tap_matrix(): taps = jnp.transpose(block_diagonal(first, second), (0, 2, 1, 3))]
  transfers between devices with their start and end apart: 2 -> 1, of which waited for: 2 -> 1; matrix products, arithmetic and copies ran while one was open for 6% -> 0% of each run, Pallas kernels for 0% -> 1%
where the time goes in v4:
time: 33.2 us; the launch traced here: 32.9 us
  blocking collectives  26.3 us (79%)
  Pallas kernels  2.69 us (8%)
  local copies, waits for them, and re-layouts  1.51 us (5%)
  other arithmetic  1.08 us (3%)
  between operations  0.68 us (2%)
  waiting for transfers between devices  0.36 us (1%)
    all_to_all x1, blocking collectives, by_classes(): own = lax.all_to_all(parts, both, 0, 0, tiled=True)  17.4 us
    all_to_all x1, blocking collectives, by_classes(): lax.all_to_all(result, both, 0, 0, axis_index_groups=halves, tiled=True)  8.92 us
    pallas_call x1, Pallas kernels, class_chains(): pl.pallas_call(functools.partial(class_kernel, row_count, part_cols), out...  2.35 us
    convert_element_type x1, other arithmetic, class_parts(): tile = jnp.concatenate([feature_map, cotangent], 2).astype(jnp.float32)  1.08 us
    slice x1, local copies, waits for them, and re-layouts, by_classes(): return (back[..., :channels], back[..., channels:])  0.77 us
    unnamed x8, local copies, waits for them, and re-layouts  0.67 us
  transfers between devices with their start and end apart: 1, of which 1 were waited for; matrix products, arithmetic and copies ran while one was open for 0% of the time, Pallas kernels for 1%

profile of v4, /device:TPU:0, one launch (start us, length us, event | category | flops | bytes accessed | tf_op | source)
XLA Modules:
  0.0 32.9 jit_solution(369993801921557255)
XLA Ops:
  0.6 1.1 %maximum_convert_fusion.tile = f32[512,128]{1,0:T(8,128)S(1)} fusion(bf16[512,64]{1,0:T(8,128)(2,1)} %bitcast.14, bf16[512,64]{1,0:T(8,128)(2,1)} %bitcast.15), kind=kLoop, calls=%fused_computation | loop fusion | flops 262144 | bytes 393216 | tf_op jit(solution)/shard_map/convert_element_type | solution.py:167
  1.7 0.1 shard_map.77
  1.9 0.0 copy-start
  1.9 0.0 copy-start.1
  1.9 17.4 %all_to_all.10.own = bf16[32,32,128]{2,1,0:T(8,128)(2,1)S(1)} all-to-all(bf16[32,32,128]{2,1,0:T(8,128)(2,1)S(1)} %bitcast.9), channel_id=1, replica_groups=mesh['row'=2,'col'=16] {'row','col'}, dimensions={0} | all-to-all | bytes 524288 | tf_op jit(solution)/shard_map/all_to_all | solution.py:291
  19.3 0.3 collective-permute-start
  19.6 0.0 copy-start.2
  19.6 0.0 copy-start.3
  19.6 0.0 copy-done
  19.6 0.0 copy-done.1
  19.6 0.6 %copy-done.2 = f32[64]{0:T(128)S(1)} copy-done((f32[64]{0:T(128)S(1)}, f32[64]{0:T(128)}, u32[]{:S(2)}) %copy-start.2) | copy-done | bytes 280
  20.3 0.0 copy-done.3
  20.3 0.2 shard_map.78
  20.5 0.4 %collective-permute-done.other = bf16[32,32,128]{2,1,0:T(8,128)(2,1)S(1)} collective-permute-done((bf16[32,32,128]{2,1,0:T(8,128)(2,1)S(1)}, bf16[32,32,128]{2,1,0:T(8,128)(2,1)S(1)}, u32[]{:S(2)}, u32[]{:S(2)}) %collective-permute-start) | collective-permute-done | bytes 262176 | tf_op jit(solution)/shard_map/ppermute | solution.py:294
  20.8 2.4 %shard_map.79 = bf16[16,32,128]{2,1,0:T(8,128)(2,1)S(1)} custom-call(bf16[32,32,128]{2,1,0:T(8,128)(2,1)S(1)} %all_to_all.10.own, bf16[32,32,128]{2,1,0:T(8,128)(2,1)S(1)} %collective-permute-done.other, bf16[384,384]{1,0:T(8,128)(2,1)S(1)} %get-tuple-element.18.weight_first, bf16[384,384]{1,0:T(8,128)(2,1)S(1)} %get-tuple-element.19.weight_second, ...), custom_call_target="tpu_custom_call" | custom-call | tf_op jit(solution)/shard_map/pallas_call | solution.py:270
  23.2 8.9 %all_to_all.11 = bf16[16,32,128]{2,1,0:T(8,128)(2,1)S(1)} all-to-all(bf16[16,32,128]{2,1,0:T(8,128)(2,1)S(1)} %shard_map.79), channel_id=1, replica_groups={{20,0,2,4,1,21,6,16,3,7,22,18,5,17,19,23},{28,8,10,12,9,29,14,24,11,15,..., dimensions={0} | all-to-all | bytes 262144 | tf_op jit(solution)/shard_map/all_to_all | solution.py:303
  32.1 0.1 copy.8
  32.2 0.8 %fusion = (bf16[64,8,64]{2,1,0:T(8,128)(2,1)}, bf16[64,8,64]{2,1,0:T(8,128)(2,1)}) fusion(bf16[64,8,128]{2,1,0:T(8,128)(2,1)S(1)} %bitcast.12), kind=kLoop, calls=%fused_computation.1 | loop fusion | bytes 262144 | tf_op jit(solution)/shard_map/slice | solution.py:306
Async XLA Ops:
  1.9 17.7 %copy-start = (bf16[3,3,64,64]{3,2,1,0:T(8,128)(2,1)S(1)}, bf16[3,3,64,64]{3,2,1,0:T(8,128)(2,1)}, u32[]{:S(2)}) copy-start(bf16[3,3,64,64]{3,2,1,0:T(8,128)(2,1)} %weight_first) | copy-start | bytes 221188
  1.9 17.7 %copy-start.1 = (bf16[3,3,64,64]{3,2,1,0:T(8,128)(2,1)S(1)}, bf16[3,3,64,64]{3,2,1,0:T(8,128)(2,1)}, u32[]{:S(2)}) copy-start(bf16[3,3,64,64]{3,2,1,0:T(8,128)(2,1)} %weight_second) | copy-start | bytes 221188
  19.3 1.5 %collective-permute-start = (bf16[32,32,128]{2,1,0:T(8,128)(2,1)S(1)}, bf16[32,32,128]{2,1,0:T(8,128)(2,1)S(1)}, u32[]{:S(2)}, u32[]{:S(2)}) collective-permute-start(bf16[32,32,128]{2,1,0:T(8,128)(2,1)S(1)} %all_to_all.10.own), channel_id=1, source_target_pairs={{0,1},{1,0},{2,3},{3,2},{4,5},{5,4},{6,7},{7,6},{8,9},{9,8},{10,11... | collective-permute-start | bytes 786440 | tf_op jit(solution)/shard_map/ppermute | solution.py:294
  19.6 0.7 %copy-start.2 = (f32[64]{0:T(128)S(1)}, f32[64]{0:T(128)}, u32[]{:S(2)}) copy-start(f32[64]{0:T(128)} %param.8) | copy-start | bytes 772
  19.6 0.7 %copy-start.3 = (f32[64]{0:T(128)S(1)}, f32[64]{0:T(128)}, u32[]{:S(2)}) copy-start(f32[64]{0:T(128)} %param.10) | copy-start | bytes 772

commit v5 on v4

--- a/solution.py
+++ b/solution.py
@@ -39,6 +39,12 @@
         0.5 * (1.0 + lax.erf(value_array * root_half))
         + value_array * jnp.exp(-0.5 * value_array * value_array) * inv_root_tau
     )
+
+
+def gelu_pair(value_array):
+    share = 0.5 + 0.5 * lax.erf(value_array * root_half)
+    bell = jnp.exp(-0.5 * value_array * value_array) * inv_root_tau
+    return value_array * share, share + value_array * bell
 
 
 def conv(padded_input, conv_kernel, step):
@@ -114,12 +120,19 @@
                 upper = jnp.concatenate([weight[q, p], gap], 1)
                 lower = jnp.concatenate([gap, weight[p, q]], 1)
                 block = jnp.concatenate([upper, lower], 0)
-                ahead[pl.ds(2 * channels * p, 2 * channels), pl.ds(2 * channels * q, 2 * channels)] = block
+                columns = pl.ds(2 * channels * q, 2 * channels)
+                if ahead is second:
+                    ahead[pl.ds(2 * channels * p, 2 * channels), columns] = block
+                else:
+                    joint = jnp.concatenate([weight[q, p], weight[p, q]], 1)
+                    ahead[pl.ds(channels * p, channels), columns] = joint
                 p_back, q_back = taps - 1 - p, taps - 1 - q
                 behind[
                     pl.ds(2 * channels * q_back, 2 * channels),
                     pl.ds(2 * channels * p_back, 2 * channels),
                 ] = block
+    rest = slice(taps * channels, first.shape[0])
+    first[rest] = jnp.zeros_like(first[rest])
     for bias, wide in ((bias_first, first_bias), (bias_second, second_bias)):
         wide[...] = jnp.concatenate([bias[...], bias[...]], 1)
 
@@ -130,7 +143,10 @@
     vmem = pl.BlockSpec(memory_space=pltpu.VMEM)
     return pl.pallas_call(
         matrix_kernel,
-        out_shape=[jax.ShapeDtypeStruct((size, size), jnp.bfloat16)] * 4
+        out_shape=[
+            jax.ShapeDtypeStruct(((taps + 1) * channels, size), jnp.bfloat16),
+            *[jax.ShapeDtypeStruct((size, size), jnp.bfloat16)] * 3,
+        ]
         + [jax.ShapeDtypeStruct((1, 2 * channels), jnp.float32)] * 2,
         in_specs=[vmem] * 4,
         out_specs=[vmem] * 6,
@@ -204,7 +220,7 @@
     begin = half * (share - CONVS)
     cells = count * class_rows
     low = lax.broadcasted_iota(jnp.int32, (cells, width), 1) < channels
-    row = lax.rem(lax.broadcasted_iota(jnp.int32, (cells, width), 0), class_rows)
+    row = lax.broadcasted_iota(jnp.int32, (1, class_rows, width), 1)
 
     pieces = []
     for r in range(row_count):
@@ -225,36 +241,59 @@
     def swapped(value):
         return pltpu.roll(value, channels, 1)
 
-    def tap_sum(image, matrix, dimension):
-        gap = jnp.zeros((class_rows, width), image.dtype)
-        before = jnp.concatenate([gap, image[:-class_rows]], 0)
-        after = jnp.concatenate([image[class_rows:], gap], 0)
+    chunks = 2
+    size = cells // chunks
+    rows = [slice(k * size, (k + 1) * size) for k in range(chunks)]
+    low = low[:size]
+
+    def tap_sum(images, k, matrix, dimension, doubled=False):
+        gap = jnp.zeros((class_rows, width), jnp.bfloat16)
+        image = images[k]
+        before = images[k - 1][-class_rows:] if k else gap
+        before = jnp.concatenate([before, image[:-class_rows]], 0)
+        after = images[k + 1][:class_rows] if k + 1 < chunks else gap
+        after = jnp.concatenate([image[class_rows:], after], 0)
+        columns = [jnp.where(low, before, image), after] if doubled else [before, image, after]
         taps = lax.dot_general(
-            jnp.concatenate([before, image, after], 1),
+            jnp.concatenate(columns, 1),
             matrix[...],
             (((1,), (dimension,)), ((), ())),
             preferred_element_type=jnp.float32,
         )
-        above = jnp.where(row == 0, 0.0, pltpu.roll(taps[:, :width], 1, 0))
-        below = pltpu.roll(taps[:, 2 * width :], cells - 1, 0)
+        taps = taps.reshape(count // chunks, class_rows, 3 * width)
+        above = jnp.where(row == 0, 0.0, pltpu.roll(taps[:, :, :width], 1, 1))
+        below = pltpu.roll(taps[:, :, 2 * width :], class_rows - 1, 1)
         below = jnp.where(row == class_rows - 1, 0.0, below)
-        return above + taps[:, width : 2 * width] + below
-
-    symmetric = straight + turned
-    symmetric = jnp.where(low, symmetric, swapped(symmetric)).astype(jnp.bfloat16)
-    gradient = jnp.where(low, swapped(straight), turned)
-
-    pre_first = tap_sum(symmetric, weight_first, 0) + bias_first[...]
-    hidden = gelu_value(pre_first).astype(jnp.bfloat16)
-    slope_first = gelu_slope(pre_first)
-    pre_second = tap_sum(hidden, weight_second, 0) + bias_second[...]
-    output = symmetric.astype(jnp.float32) + gelu_value(pre_second)
-    grad_second = (gradient * gelu_slope(pre_second)).astype(jnp.bfloat16)
-    grad_first = (tap_sum(grad_second, weight_third, 1) * slope_first).astype(jnp.bfloat16)
-    grad_sym = (gradient + tap_sum(grad_first, weight_fourth, 1)).astype(jnp.bfloat16)
-    grad_sym = grad_sym.astype(jnp.float32)
-    finished = jnp.where(low, output, grad_sym + swapped(grad_sym)).astype(jnp.bfloat16)
-    window[...] = finished.reshape(count, class_rows, width)
+        return (above + taps[:, :, width : 2 * width] + below).reshape(size, width)
+
+    symmetric, gradient = [], []
+    for k in range(chunks):
+        total = straight[rows[k]] + turned[rows[k]]
+        symmetric.append(jnp.where(low, total, swapped(total)).astype(jnp.bfloat16))
+        gradient.append(jnp.where(low, swapped(straight[rows[k]]), turned[rows[k]]))
+
+    hidden, slope_first = [], []
+    for k in range(chunks):
+        pre_first = tap_sum(symmetric, k, weight_first, 0, True) + bias_first[...]
+        value, slope = gelu_pair(pre_first)
+        hidden.append(value.astype(jnp.bfloat16))
+        slope_first.append(slope)
+    output, grad_second = [], []
+    for k in range(chunks):
+        pre_second = tap_sum(hidden, k, weight_second, 0) + bias_second[...]
+        value, slope = gelu_pair(pre_second)
+        output.append(symmetric[k].astype(jnp.float32) + value)
+        grad_second.append((gradient[k] * slope).astype(jnp.bfloat16))
+    grad_first = [
+        (tap_sum(grad_second, k, weight_third, 1) * slope_first[k]).astype(jnp.bfloat16)
+        for k in range(chunks)
+    ]
+    for k in range(chunks):
+        grad_sym = (gradient[k] + tap_sum(grad_first, k, weight_fourth, 1)).astype(jnp.bfloat16)
+        grad_sym = grad_sym.astype(jnp.float32)
+        finished = jnp.where(low, output[k], grad_sym + swapped(grad_sym)).astype(jnp.bfloat16)
+        share_cols = count // chunks
+        window[k * share_cols : (k + 1) * share_cols] = finished.reshape(share_cols, class_rows, width)
 
     for index, (a, b) in enumerate(class_order()):
         r, c = divmod(index, half_count)

time: 33.2 us -> 32.5 us (0.979)
  Pallas kernels: 2.69 us -> 1.98 us
    pallas_call x1, Pallas kernels: 2.35 us -> 1.65 us  [class_chains(): pl.pallas_call(functools.partial(class_kernel, row_count, part_cols), out...]
where the time goes in v5:
time: 32.5 us; the launch traced here: 32.3 us
  blocking collectives  26.3 us (81%)
  Pallas kernels  1.98 us (6%)
  local copies, waits for them, and re-layouts  1.51 us (5%)
  other arithmetic  1.08 us (3%)
  between operations  0.68 us (2%)
  waiting for transfers between devices  0.38 us (1%)
    all_to_all x1, blocking collectives, by_classes(): own = lax.all_to_all(parts, both, 0, 0, tiled=True)  17.4 us
    all_to_all x1, blocking collectives, by_classes(): lax.all_to_all(result, both, 0, 0, axis_index_groups=halves, tiled=True)  8.92 us
    pallas_call x1, Pallas kernels, class_chains(): pl.pallas_call(functools.partial(class_kernel, row_count, part_cols), out...  1.65 us
    convert_element_type x1, other arithmetic, class_parts(): tile = jnp.concatenate([feature_map, cotangent], 2).astype(jnp.float32)  1.08 us
    slice x1, local copies, waits for them, and re-layouts, by_classes(): return (back[..., :channels], back[..., channels:])  0.77 us
    unnamed x8, local copies, waits for them, and re-layouts  0.67 us
  transfers between devices with their start and end apart: 1, of which 1 were waited for; matrix products, arithmetic and copies ran while one was open for 0% of the time, Pallas kernels for 1%

profile of v5, /device:TPU:0, one launch (start us, length us, event | category | flops | bytes accessed | tf_op | source)
XLA Modules:
  0.0 32.3 jit_solution(7750334784005861646)
XLA Ops:
  0.6 1.1 %maximum_convert_fusion.tile = f32[512,128]{1,0:T(8,128)S(1)} fusion(bf16[512,64]{1,0:T(8,128)(2,1)} %bitcast.14, bf16[512,64]{1,0:T(8,128)(2,1)} %bitcast.15), kind=kLoop, calls=%fused_computation | loop fusion | flops 262144 | bytes 393216 | tf_op jit(solution)/shard_map/convert_element_type | solution.py:183
  1.7 0.1 shard_map.77
  1.9 0.0 copy-start
  1.9 0.0 copy-start.1
  1.9 17.4 %all_to_all.10.own = bf16[32,32,128]{2,1,0:T(8,128)(2,1)S(1)} all-to-all(bf16[32,32,128]{2,1,0:T(8,128)(2,1)S(1)} %bitcast.9), channel_id=1, replica_groups=mesh['row'=2,'col'=16] {'row','col'}, dimensions={0} | all-to-all | bytes 524288 | tf_op jit(solution)/shard_map/all_to_all | solution.py:330
  19.3 0.3 collective-permute-start
  19.6 0.0 copy-start.2
  19.6 0.0 copy-start.3
  19.6 0.0 copy-done
  19.6 0.0 copy-done.1
  19.6 0.6 %copy-done.2 = f32[64]{0:T(128)S(1)} copy-done((f32[64]{0:T(128)S(1)}, f32[64]{0:T(128)}, u32[]{:S(2)}) %copy-start.2) | copy-done | bytes 280
  20.3 0.0 copy-done.3
  20.3 0.2 shard_map.78
  20.4 0.4 %collective-permute-done.other = bf16[32,32,128]{2,1,0:T(8,128)(2,1)S(1)} collective-permute-done((bf16[32,32,128]{2,1,0:T(8,128)(2,1)S(1)}, bf16[32,32,128]{2,1,0:T(8,128)(2,1)S(1)}, u32[]{:S(2)}, u32[]{:S(2)}) %collective-permute-start) | collective-permute-done | bytes 262176 | tf_op jit(solution)/shard_map/ppermute | solution.py:333
  20.8 1.7 %shard_map.79 = bf16[16,32,128]{2,1,0:T(8,128)(2,1)S(1)} custom-call(bf16[32,32,128]{2,1,0:T(8,128)(2,1)S(1)} %all_to_all.10.own, bf16[32,32,128]{2,1,0:T(8,128)(2,1)S(1)} %collective-permute-done.other, bf16[256,384]{1,0:T(8,128)(2,1)S(1)} %get-tuple-element.18.weight_first, bf16[384,384]{1,0:T(8,128)(2,1)S(1)} %get-tuple-element.19.weight_second, ...), custom_call_target="tpu_custom_call" | custom-call | tf_op jit(solution)/shard_map/pallas_call | solution.py:309
  22.5 8.9 %all_to_all.11 = bf16[16,32,128]{2,1,0:T(8,128)(2,1)S(1)} all-to-all(bf16[16,32,128]{2,1,0:T(8,128)(2,1)S(1)} %shard_map.79), channel_id=1, replica_groups={{20,0,2,4,1,21,6,16,3,7,22,18,5,17,19,23},{28,8,10,12,9,29,14,24,11,15,..., dimensions={0} | all-to-all | bytes 262144 | tf_op jit(solution)/shard_map/all_to_all | solution.py:342
  31.4 0.1 copy.8
  31.5 0.8 %fusion = (bf16[64,8,64]{2,1,0:T(8,128)(2,1)}, bf16[64,8,64]{2,1,0:T(8,128)(2,1)}) fusion(bf16[64,8,128]{2,1,0:T(8,128)(2,1)S(1)} %bitcast.12), kind=kLoop, calls=%fused_computation.1 | loop fusion | bytes 262144 | tf_op jit(solution)/shard_map/slice | solution.py:345
Async XLA Ops:
  1.9 17.7 %copy-start = (bf16[3,3,64,64]{3,2,1,0:T(8,128)(2,1)S(1)}, bf16[3,3,64,64]{3,2,1,0:T(8,128)(2,1)}, u32[]{:S(2)}) copy-start(bf16[3,3,64,64]{3,2,1,0:T(8,128)(2,1)} %weight_first) | copy-start | bytes 221188
  1.9 17.7 %copy-start.1 = (bf16[3,3,64,64]{3,2,1,0:T(8,128)(2,1)S(1)}, bf16[3,3,64,64]{3,2,1,0:T(8,128)(2,1)}, u32[]{:S(2)}) copy-start(bf16[3,3,64,64]{3,2,1,0:T(8,128)(2,1)} %weight_second) | copy-start | bytes 221188
  19.3 1.5 %collective-permute-start = (bf16[32,32,128]{2,1,0:T(8,128)(2,1)S(1)}, bf16[32,32,128]{2,1,0:T(8,128)(2,1)S(1)}, u32[]{:S(2)}, u32[]{:S(2)}) collective-permute-start(bf16[32,32,128]{2,1,0:T(8,128)(2,1)S(1)} %all_to_all.10.own), channel_id=1, source_target_pairs={{0,1},{1,0},{2,3},{3,2},{4,5},{5,4},{6,7},{7,6},{8,9},{9,8},{10,11... | collective-permute-start | bytes 786440 | tf_op jit(solution)/shard_map/ppermute | solution.py:333
  19.6 0.7 %copy-start.2 = (f32[64]{0:T(128)S(1)}, f32[64]{0:T(128)}, u32[]{:S(2)}) copy-start(f32[64]{0:T(128)} %param.8) | copy-start | bytes 772
  19.6 0.7 %copy-start.3 = (f32[64]{0:T(128)S(1)}, f32[64]{0:T(128)}, u32[]{:S(2)}) copy-start(f32[64]{0:T(128)} %param.10) | copy-start | bytes 772

commit v6 on v5

--- a/solution.py
+++ b/solution.py
@@ -295,11 +295,12 @@
         share_cols = count // chunks
         window[k * share_cols : (k + 1) * share_cols] = finished.reshape(share_cols, class_rows, width)
 
-    for index, (a, b) in enumerate(class_order()):
+    classes = result.shape[0]
+    for index in range(classes):
         r, c = divmod(index, half_count)
         kept = window[pl.ds(half * CONVS + c * part_cols, part_cols)]
         kept = kept[:, r * part_rows : (r + 1) * part_rows]
-        result[a * DILATION_STEP + b] = kept.reshape(part, width)
+        result[classes - 1 - index] = kept.reshape(part, width)
 
 
 def class_chains(row_count, part_cols, own, other, *parameters):
@@ -333,13 +334,14 @@
     other = lax.ppermute(own, "col", [(i, i ^ 1) for i in range(col_count)])
     result = class_chains(row_count, part_cols, own, other, *chain_matrices(*raw))
 
-    half_count = col_count // HALVES
-    order = sorted(range(step * step), key=lambda index: class_order()[index])
+    half_count, classes = col_count // HALVES, step * step
     halves = [
-        [i // half_count * col_count + h * half_count + i % half_count for i in order]
+        [i // half_count * col_count + h * half_count + i % half_count for i in range(classes)][::-1]
         for h in range(HALVES)
     ]
     back = lax.all_to_all(result, both, 0, 0, axis_index_groups=halves, tiled=True)
+    order = sorted(range(classes), key=lambda index: class_order()[index])
+    back = jnp.concatenate([back[classes - 1 - i : classes - i] for i in order], 0)
     back = back.reshape(step, step, part_cols, part_rows, 2 * channels)
     back = jnp.transpose(back, (3, 0, 2, 1, 4)).reshape(tile_rows, tile_cols, 2 * channels)
     return back[..., :channels], back[..., channels:]

time: 32.5 us -> 31.4 us (0.966)
  blocking collectives: 26.3 us -> 25.1 us
    all_to_all x1, blocking collectives: 8.92 us -> 7.7 us  [by_classes(): lax.all_to_all(result, both, 0, 0, axis_index_groups=halves, tiled=True)]
    unnamed x8 -> x23, local copies, waits for them, and re-layouts: 0.67 us -> 0.79 us
where the time goes in v6:
time: 31.4 us; the launch traced here: 31.2 us
  blocking collectives  25.1 us (80%)
  Pallas kernels  1.98 us (6%)
  local copies, waits for them, and re-layouts  1.64 us (5%)
  other arithmetic  1.08 us (3%)
  between operations  0.73 us (2%)
  waiting for transfers between devices  0.38 us (1%)
    all_to_all x1, blocking collectives, by_classes(): own = lax.all_to_all(parts, both, 0, 0, tiled=True)  17.4 us
    all_to_all x1, blocking collectives, by_classes(): lax.all_to_all(result, both, 0, 0, axis_index_groups=halves, tiled=True)  7.7 us
    pallas_call x1, Pallas kernels, class_chains(): pl.pallas_call(functools.partial(class_kernel, row_count, part_cols), out...  1.65 us
    convert_element_type x1, other arithmetic, class_parts(): tile = jnp.concatenate([feature_map, cotangent], 2).astype(jnp.float32)  1.08 us
    unnamed x23, local copies, waits for them, and re-layouts  0.79 us
    slice x1, local copies, waits for them, and re-layouts, by_classes(): return (back[..., :channels], back[..., channels:])  0.77 us
  transfers between devices with their start and end apart: 1, of which 1 were waited for; matrix products, arithmetic and copies ran while one was open for 0% of the time, Pallas kernels for 1%

profile of v6, /device:TPU:0, one launch (start us, length us, event | category | flops | bytes accessed | tf_op | source)
XLA Modules:
  0.0 31.2 jit_solution(10864835993194547028)
XLA Ops:
  0.6 1.1 %maximum_convert_fusion.tile = f32[512,128]{1,0:T(8,128)S(1)} fusion(bf16[512,64]{1,0:T(8,128)(2,1)} %bitcast.14, bf16[512,64]{1,0:T(8,128)(2,1)} %bitcast.15), kind=kLoop, calls=%fused_computation | loop fusion | flops 262144 | bytes 393216 | tf_op jit(solution)/shard_map/convert_element_type | solution.py:183
  1.7 0.1 shard_map.77
  1.9 0.0 copy-start
  1.9 0.0 copy-start.1
  1.9 17.4 %all_to_all.10.own = bf16[32,32,128]{2,1,0:T(8,128)(2,1)S(1)} all-to-all(bf16[32,32,128]{2,1,0:T(8,128)(2,1)S(1)} %bitcast.9), channel_id=1, replica_groups=mesh['row'=2,'col'=16] {'row','col'}, dimensions={0} | all-to-all | bytes 524288 | tf_op jit(solution)/shard_map/all_to_all | solution.py:331
  19.3 0.3 collective-permute-start
  19.6 0.0 copy-start.2
  19.6 0.0 copy-start.3
  19.6 0.0 copy-done
  19.6 0.0 copy-done.1
  19.6 0.6 %copy-done.2 = f32[64]{0:T(128)S(1)} copy-done((f32[64]{0:T(128)S(1)}, f32[64]{0:T(128)}, u32[]{:S(2)}) %copy-start.2) | copy-done | bytes 280
  20.3 0.0 copy-done.3
  20.3 0.2 shard_map.78
  20.4 0.4 %collective-permute-done.other = bf16[32,32,128]{2,1,0:T(8,128)(2,1)S(1)} collective-permute-done((bf16[32,32,128]{2,1,0:T(8,128)(2,1)S(1)}, bf16[32,32,128]{2,1,0:T(8,128)(2,1)S(1)}, u32[]{:S(2)}, u32[]{:S(2)}) %collective-permute-start) | collective-permute-done | bytes 262176 | tf_op jit(solution)/shard_map/ppermute | solution.py:334
  20.8 1.7 %shard_map.79 = bf16[16,32,128]{2,1,0:T(8,128)(2,1)S(1)} custom-call(bf16[32,32,128]{2,1,0:T(8,128)(2,1)S(1)} %all_to_all.10.own, bf16[32,32,128]{2,1,0:T(8,128)(2,1)S(1)} %collective-permute-done.other, bf16[256,384]{1,0:T(8,128)(2,1)S(1)} %get-tuple-element.18.weight_first, bf16[384,384]{1,0:T(8,128)(2,1)S(1)} %get-tuple-element.19.weight_second, ...), custom_call_target="tpu_custom_call" | custom-call | tf_op jit(solution)/shard_map/pallas_call | solution.py:310
  22.5 7.7 %all_to_all.11 = bf16[16,32,128]{2,1,0:T(8,128)(2,1)S(1)} all-to-all(bf16[16,32,128]{2,1,0:T(8,128)(2,1)S(1)} %shard_map.79), channel_id=1, replica_groups={{23,22,21,20,19,18,17,16,7,6,5,4,3,2,1,0},{31,30,29,28,27,26,25,24,15,1..., dimensions={0} | all-to-all | bytes 262144 | tf_op jit(solution)/shard_map/all_to_all | solution.py:342
  30.4 0.1 copy.8
  30.4 0.8 %fusion = (bf16[64,8,64]{2,1,0:T(8,128)(2,1)}, bf16[64,8,64]{2,1,0:T(8,128)(2,1)}) fusion(bf16[64,8,128]{2,1,0:T(8,128)(2,1)S(1)} %bitcast.12), kind=kLoop, calls=%fused_computation.17 | loop fusion | bytes 262144 | tf_op jit(solution)/shard_map/slice | solution.py:347
  (16 shorter events, 0.1 us)
Async XLA Ops:
  1.9 17.7 %copy-start = (bf16[3,3,64,64]{3,2,1,0:T(8,128)(2,1)S(1)}, bf16[3,3,64,64]{3,2,1,0:T(8,128)(2,1)}, u32[]{:S(2)}) copy-start(bf16[3,3,64,64]{3,2,1,0:T(8,128)(2,1)} %weight_first) | copy-start | bytes 221188
  1.9 17.7 %copy-start.1 = (bf16[3,3,64,64]{3,2,1,0:T(8,128)(2,1)S(1)}, bf16[3,3,64,64]{3,2,1,0:T(8,128)(2,1)}, u32[]{:S(2)}) copy-start(bf16[3,3,64,64]{3,2,1,0:T(8,128)(2,1)} %weight_second) | copy-start | bytes 221188
  19.3 1.5 %collective-permute-start = (bf16[32,32,128]{2,1,0:T(8,128)(2,1)S(1)}, bf16[32,32,128]{2,1,0:T(8,128)(2,1)S(1)}, u32[]{:S(2)}, u32[]{:S(2)}) collective-permute-start(bf16[32,32,128]{2,1,0:T(8,128)(2,1)S(1)} %all_to_all.10.own), channel_id=1, source_target_pairs={{0,1},{1,0},{2,3},{3,2},{4,5},{5,4},{6,7},{7,6},{8,9},{9,8},{10,11... | collective-permute-start | bytes 786440 | tf_op jit(solution)/shard_map/ppermute | solution.py:334
  19.6 0.7 %copy-start.2 = (f32[64]{0:T(128)S(1)}, f32[64]{0:T(128)}, u32[]{:S(2)}) copy-start(f32[64]{0:T(128)} %param.8) | copy-start | bytes 772
  19.6 0.7 %copy-start.3 = (f32[64]{0:T(128)S(1)}, f32[64]{0:T(128)}, u32[]{:S(2)}) copy-start(f32[64]{0:T(128)} %param.10) | copy-start | bytes 772

commit v7 on v5

--- a/solution.py
+++ b/solution.py
@@ -156,14 +156,16 @@
 
 def class_order():
     step = range(DILATION_STEP)
-    uneven = [[(a, b), (b, a)] for a in step for b in step if a < b]
-    return sum(uneven, []) + [(a, a) for a in step]
-
-
-def part_kernel(tile_cols, tile, parts):
+    pairs = [((a, a), (a + 1, a + 1)) for a in step[::2]]
+    pairs += [((a, b), (b, a)) for a in step for b in step if a < b]
+    return [c for pair in sorted(pairs) for c in pair][::-1]
+
+
+def part_kernel(tile_cols, whole, parts, tile):
     step = DILATION_STEP
     part_cols = tile_cols // step
-    part_rows = tile.shape[0] // (tile_cols * step)
+    part_rows = whole.shape[0] // (tile_cols * step)
+    tile[: whole.shape[0]] = whole[...]
     for index, (a, b) in enumerate(class_order()):
         columns = [
             tile[pl.ds(a * tile_cols + k * step + b, part_rows, stride=step * tile_cols), :]
@@ -186,6 +188,7 @@
         out_shape=jax.ShapeDtypeStruct(shape, jnp.bfloat16),
         in_specs=[pl.BlockSpec(memory_space=pltpu.VMEM)],
         out_specs=pl.BlockSpec(memory_space=pltpu.VMEM),
+        scratch_shapes=[pltpu.VMEM((cells + DILATION_STEP * tile_cols, 2 * channels), jnp.float32)],
         compiler_params=pltpu.CompilerParams(vmem_limit_bytes=16 * 2**20),
     )(tile.reshape(cells, 2 * channels))
 
@@ -216,7 +219,8 @@
     column = lax.axis_index("col")
     half = lax.div(column, half_count)
     place = lax.axis_index("row") * half_count + lax.rem(column, half_count)
-    even = place >= len(class_order()) - DILATION_STEP
+    evens = [index for index, (a, b) in enumerate(class_order()) if a == b]
+    even = functools.reduce(jnp.logical_or, [place == index for index in evens])
     begin = half * (share - CONVS)
     cells = count * class_rows
     low = lax.broadcasted_iota(jnp.int32, (cells, width), 1) < channels
@@ -312,7 +316,7 @@
         in_specs=[pl.BlockSpec(memory_space=pltpu.VMEM)] * 8,
         out_specs=pl.BlockSpec(memory_space=pltpu.VMEM),
         scratch_shapes=[
-            pltpu.VMEM((class_cols * class_rows, width), jnp.float32),
+            pltpu.VMEM(((class_cols + 1) * class_rows, width), jnp.float32),
             pltpu.VMEM((count, class_rows, width), jnp.bfloat16),
         ],
         compiler_params=pltpu.CompilerParams(vmem_limit_bytes=32 * 2**20),

time: 32.5 us -> 31.2 us (0.960)
  blocking collectives: 26.3 us -> 25.1 us
    all_to_all x1, blocking collectives: 8.92 us -> 7.69 us  [by_classes(): lax.all_to_all(result, both, 0, 0, axis_index_groups=halves, tiled=True)]
where the time goes in v7:
time: 31.2 us; the launch traced here: 31 us
  blocking collectives  25.1 us (80%)
  Pallas kernels  1.99 us (6%)
  local copies, waits for them, and re-layouts  1.51 us (5%)
  other arithmetic  1.08 us (3%)
  between operations  0.68 us (2%)
  waiting for transfers between devices  0.38 us (1%)
    all_to_all x1, blocking collectives, by_classes(): own = lax.all_to_all(parts, both, 0, 0, tiled=True)  17.4 us
    all_to_all x1, blocking collectives, by_classes(): lax.all_to_all(result, both, 0, 0, axis_index_groups=halves, tiled=True)  7.69 us
    pallas_call x1, Pallas kernels, class_chains(): pl.pallas_call(functools.partial(class_kernel, row_count, part_cols), out...  1.64 us
    convert_element_type x1, other arithmetic, class_parts(): tile = jnp.concatenate([feature_map, cotangent], 2).astype(jnp.float32)  1.08 us
    slice x1, local copies, waits for them, and re-layouts, by_classes(): return (back[..., :channels], back[..., channels:])  0.77 us
    unnamed x8, local copies, waits for them, and re-layouts  0.67 us
  transfers between devices with their start and end apart: 1, of which 1 were waited for; matrix products, arithmetic and copies ran while one was open for 0% of the time, Pallas kernels for 1%

profile of v7, /device:TPU:0, one launch (start us, length us, event | category | flops | bytes accessed | tf_op | source)
XLA Modules:
  0.0 31.0 jit_solution(15987961793968712793)
XLA Ops:
  0.6 1.1 %maximum_convert_fusion.whole = f32[512,128]{1,0:T(8,128)S(1)} fusion(bf16[512,64]{1,0:T(8,128)(2,1)} %bitcast.14, bf16[512,64]{1,0:T(8,128)(2,1)} %bitcast.15), kind=kLoop, calls=%fused_computation | loop fusion | flops 262144 | bytes 393216 | tf_op jit(solution)/shard_map/convert_element_type | solution.py:185
  1.7 0.2 shard_map.77
  1.9 0.0 copy-start
  1.9 0.0 copy-start.1
  1.9 17.4 %all_to_all.10.own = bf16[32,32,128]{2,1,0:T(8,128)(2,1)S(1)} all-to-all(bf16[32,32,128]{2,1,0:T(8,128)(2,1)S(1)} %bitcast.9), channel_id=1, replica_groups=mesh['row'=2,'col'=16] {'row','col'}, dimensions={0} | all-to-all | bytes 524288 | tf_op jit(solution)/shard_map/all_to_all | solution.py:334
  19.3 0.3 collective-permute-start
  19.6 0.0 copy-start.2
  19.6 0.0 copy-start.3
  19.6 0.0 copy-done
  19.6 0.0 copy-done.1
  19.6 0.6 %copy-done.2 = f32[64]{0:T(128)S(1)} copy-done((f32[64]{0:T(128)S(1)}, f32[64]{0:T(128)}, u32[]{:S(2)}) %copy-start.2) | copy-done | bytes 280
  20.3 0.0 copy-done.3
  20.3 0.2 shard_map.78
  20.5 0.4 %collective-permute-done.other = bf16[32,32,128]{2,1,0:T(8,128)(2,1)S(1)} collective-permute-done((bf16[32,32,128]{2,1,0:T(8,128)(2,1)S(1)}, bf16[32,32,128]{2,1,0:T(8,128)(2,1)S(1)}, u32[]{:S(2)}, u32[]{:S(2)}) %collective-permute-start) | collective-permute-done | bytes 262176 | tf_op jit(solution)/shard_map/ppermute | solution.py:337
  20.8 1.6 %shard_map.79 = bf16[16,32,128]{2,1,0:T(8,128)(2,1)S(1)} custom-call(bf16[32,32,128]{2,1,0:T(8,128)(2,1)S(1)} %all_to_all.10.own, bf16[32,32,128]{2,1,0:T(8,128)(2,1)S(1)} %collective-permute-done.other, bf16[256,384]{1,0:T(8,128)(2,1)S(1)} %get-tuple-element.18.weight_first, bf16[384,384]{1,0:T(8,128)(2,1)S(1)} %get-tuple-element.19.weight_second, ...), custom_call_target="tpu_custom_call" | custom-call | tf_op jit(solution)/shard_map/pallas_call | solution.py:313
  22.5 7.7 %all_to_all.11 = bf16[16,32,128]{2,1,0:T(8,128)(2,1)S(1)} all-to-all(bf16[16,32,128]{2,1,0:T(8,128)(2,1)S(1)} %shard_map.79), channel_id=1, replica_groups={{23,21,19,17,20,22,7,5,18,6,3,1,16,4,0,2},{31,29,27,25,28,30,15,13,26,1..., dimensions={0} | all-to-all | bytes 262144 | tf_op jit(solution)/shard_map/all_to_all | solution.py:346
  30.2 0.1 copy.8
  30.3 0.8 %fusion = (bf16[64,8,64]{2,1,0:T(8,128)(2,1)}, bf16[64,8,64]{2,1,0:T(8,128)(2,1)}) fusion(bf16[64,8,128]{2,1,0:T(8,128)(2,1)S(1)} %bitcast.12), kind=kLoop, calls=%fused_computation.1 | loop fusion | bytes 262144 | tf_op jit(solution)/shard_map/slice | solution.py:349
Async XLA Ops:
  1.9 17.7 %copy-start = (bf16[3,3,64,64]{3,2,1,0:T(8,128)(2,1)S(1)}, bf16[3,3,64,64]{3,2,1,0:T(8,128)(2,1)}, u32[]{:S(2)}) copy-start(bf16[3,3,64,64]{3,2,1,0:T(8,128)(2,1)} %weight_first) | copy-start | bytes 221188
  1.9 17.7 %copy-start.1 = (bf16[3,3,64,64]{3,2,1,0:T(8,128)(2,1)S(1)}, bf16[3,3,64,64]{3,2,1,0:T(8,128)(2,1)}, u32[]{:S(2)}) copy-start(bf16[3,3,64,64]{3,2,1,0:T(8,128)(2,1)} %weight_second) | copy-start | bytes 221188
  19.3 1.5 %collective-permute-start = (bf16[32,32,128]{2,1,0:T(8,128)(2,1)S(1)}, bf16[32,32,128]{2,1,0:T(8,128)(2,1)S(1)}, u32[]{:S(2)}, u32[]{:S(2)}) collective-permute-start(bf16[32,32,128]{2,1,0:T(8,128)(2,1)S(1)} %all_to_all.10.own), channel_id=1, source_target_pairs={{0,1},{1,0},{2,3},{3,2},{4,5},{5,4},{6,7},{7,6},{8,9},{9,8},{10,11... | collective-permute-start | bytes 786440 | tf_op jit(solution)/shard_map/ppermute | solution.py:337
  19.6 0.7 %copy-start.2 = (f32[64]{0:T(128)S(1)}, f32[64]{0:T(128)}, u32[]{:S(2)}) copy-start(f32[64]{0:T(128)} %param.8) | copy-start | bytes 772
  19.6 0.7 %copy-start.3 = (f32[64]{0:T(128)S(1)}, f32[64]{0:T(128)}, u32[]{:S(2)}) copy-start(f32[64]{0:T(128)} %param.10) | copy-start | bytes 772

commit v8 on v7

--- a/solution.py
+++ b/solution.py
@@ -107,24 +107,26 @@
     return output, add_rounded(grad_sym, mirror(grad_sym))
 
 
-def matrix_kernel(weight_first, weight_second, bias_first, bias_second, *outputs):
+def matrix_kernel(half_count, weight_first, weight_second, bias_first, bias_second, *outputs):
     first, second, third, fourth, first_bias, second_bias = outputs
     taps, channels = weight_first.shape[0], weight_first.shape[2]
     gap = jnp.zeros(weight_first.shape[2:], weight_first.dtype)
+    half = lax.div(lax.axis_index("col"), half_count)
     for weight, ahead, behind in (
         (weight_first, first, fourth),
         (weight_second, second, third),
     ):
         for p in range(taps):
+            along = half * (taps - 1) + (1 - 2 * half) * p
             for q in range(taps):
-                upper = jnp.concatenate([weight[q, p], gap], 1)
-                lower = jnp.concatenate([gap, weight[p, q]], 1)
+                upper = jnp.concatenate([weight[q, along], gap], 1)
+                lower = jnp.concatenate([gap, weight[along, q]], 1)
                 block = jnp.concatenate([upper, lower], 0)
                 columns = pl.ds(2 * channels * q, 2 * channels)
                 if ahead is second:
                     ahead[pl.ds(2 * channels * p, 2 * channels), columns] = block
                 else:
-                    joint = jnp.concatenate([weight[q, p], weight[p, q]], 1)
+                    joint = jnp.concatenate([weight[q, along], weight[along, q]], 1)
                     ahead[pl.ds(channels * p, channels), columns] = joint
                 p_back, q_back = taps - 1 - p, taps - 1 - q
                 behind[
@@ -137,12 +139,12 @@
         wide[...] = jnp.concatenate([bias[...], bias[...]], 1)
 
 
-def chain_matrices(weight_first, weight_second, bias_first, bias_second):
+def chain_matrices(half_count, weight_first, weight_second, bias_first, bias_second):
     taps, channels = weight_first.shape[0], weight_first.shape[2]
     size = taps * 2 * channels
     vmem = pl.BlockSpec(memory_space=pltpu.VMEM)
     return pl.pallas_call(
-        matrix_kernel,
+        functools.partial(matrix_kernel, half_count),
         out_shape=[
             jax.ShapeDtypeStruct(((taps + 1) * channels, size), jnp.bfloat16),
             *[jax.ShapeDtypeStruct((size, size), jnp.bfloat16)] * 3,
@@ -221,16 +223,18 @@
     place = lax.axis_index("row") * half_count + lax.rem(column, half_count)
     evens = [index for index, (a, b) in enumerate(class_order()) if a == b]
     even = functools.reduce(jnp.logical_or, [place == index for index in evens])
-    begin = half * (share - CONVS)
-    cells = count * class_rows
-    low = lax.broadcasted_iota(jnp.int32, (cells, width), 1) < channels
     row = lax.broadcasted_iota(jnp.int32, (1, class_rows, width), 1)
 
+    def inward(index, total):
+        return half * (total - 1) + (1 - 2 * half) * index
+
     pieces = []
-    for r in range(row_count):
-        reach = pl.ds(r * col_count + half * ((share - CONVS) // part_cols), count // part_cols)
-        pieces.append(own[reach].reshape(count, part_rows, width))
-    straight = jnp.concatenate(pieces, 1).astype(jnp.float32).reshape(cells, width)
+    for n in range(count // part_cols):
+        blocks = [own[r * col_count + inward(n, col_count)] for r in range(row_count)]
+        for k in range(part_cols):
+            ends = [slice(m * part_rows, (m + 1) * part_rows) for m in (k, part_cols - 1 - k)]
+            pieces += [jnp.where(half == 0, block[ends[0]], block[ends[1]]) for block in blocks]
+    straight = jnp.concatenate(pieces, 0).astype(jnp.float32)
 
     for r in range(row_count):
         reach = slice(r * col_count, (r + 1) * col_count)
@@ -239,77 +243,101 @@
         for k in range(class_cols):
             turning[pl.ds(k * class_rows + r * part_rows, part_rows), :] = piece[k]
     turned = jnp.concatenate(
-        [turning[pl.ds(begin + i, class_cols, stride=class_rows), :] for i in range(count)], 0
+        [
+            turning[pl.ds(inward(n, class_cols), class_cols, stride=class_rows), :]
+            for n in range(count)
+        ],
+        0,
     )
+
+    def low(value):
+        return lax.broadcasted_iota(jnp.int32, value.shape, 1) < channels
 
     def swapped(value):
         return pltpu.roll(value, channels, 1)
 
-    chunks = 2
-    size = cells // chunks
-    rows = [slice(k * size, (k + 1) * size) for k in range(chunks)]
-    low = low[:size]
-
-    def tap_sum(images, k, matrix, dimension, doubled=False):
-        gap = jnp.zeros((class_rows, width), jnp.bfloat16)
-        image = images[k]
-        before = images[k - 1][-class_rows:] if k else gap
-        before = jnp.concatenate([before, image[:-class_rows]], 0)
-        after = images[k + 1][:class_rows] if k + 1 < chunks else gap
-        after = jnp.concatenate([image[class_rows:], after], 0)
-        columns = [jnp.where(low, before, image), after] if doubled else [before, image, after]
-        taps = lax.dot_general(
-            jnp.concatenate(columns, 1),
-            matrix[...],
-            (((1,), (dimension,)), ((), ())),
-            preferred_element_type=jnp.float32,
-        )
-        taps = taps.reshape(count // chunks, class_rows, 3 * width)
+    def tap_sum(image, begin, end, matrix, dimension, doubled=False):
+        first, last = begin * class_rows, end * class_rows
+        gap = [jnp.zeros((class_rows, width), image.dtype)] if begin == 0 else []
+        before = image[max(first - class_rows, 0) : last - class_rows]
+        before = jnp.concatenate(gap + [before], 0)
+        after = image[first + class_rows : last + class_rows]
+        image = image[first:last]
+        columns = [jnp.where(low(image), before, image), after]
+        def product(value, weights):
+            return lax.dot_general(
+                value, weights, (((1,), (dimension,)), ((), ())), preferred_element_type=jnp.float32
+            )
+
+        if doubled:
+            taps = product(jnp.concatenate(columns, 1), matrix[...])
+        elif dimension == 0:
+            taps = product(jnp.concatenate([image, after], 1), matrix[width:, :])
+            taps = taps + product(before, matrix[:width, :])
+        else:
+            taps = product(jnp.concatenate([image, after], 1), matrix[:, width:])
+            taps = taps + product(before, matrix[:, :width])
+        taps = taps.reshape(end - begin, class_rows, 3 * width)
         above = jnp.where(row == 0, 0.0, pltpu.roll(taps[:, :, :width], 1, 1))
         below = pltpu.roll(taps[:, :, 2 * width :], class_rows - 1, 1)
         below = jnp.where(row == class_rows - 1, 0.0, below)
-        return (above + taps[:, :, width : 2 * width] + below).reshape(size, width)
-
-    symmetric, gradient = [], []
-    for k in range(chunks):
-        total = straight[rows[k]] + turned[rows[k]]
-        symmetric.append(jnp.where(low, total, swapped(total)).astype(jnp.bfloat16))
-        gradient.append(jnp.where(low, swapped(straight[rows[k]]), turned[rows[k]]))
+        return (above + taps[:, :, width : 2 * width] + below).reshape(last - first, width)
+
+    def runs(total):
+        cut = (total + 1) // 2
+        return (0, cut), (cut, total)
+
+    def columns(value, begin, end):
+        return value[begin * class_rows : end * class_rows]
+
+    symmetric = straight + turned
+    symmetric = jnp.where(low(symmetric), symmetric, swapped(symmetric)).astype(jnp.bfloat16)
+    gradient = jnp.where(low(turned), swapped(straight), turned)
 
     hidden, slope_first = [], []
-    for k in range(chunks):
-        pre_first = tap_sum(symmetric, k, weight_first, 0, True) + bias_first[...]
+    for run in runs(count - 1):
+        pre_first = tap_sum(symmetric, *run, weight_first, 0, True) + bias_first[...]
         value, slope = gelu_pair(pre_first)
         hidden.append(value.astype(jnp.bfloat16))
         slope_first.append(slope)
+    hidden, slope_first = jnp.concatenate(hidden, 0), jnp.concatenate(slope_first, 0)
     output, grad_second = [], []
-    for k in range(chunks):
-        pre_second = tap_sum(hidden, k, weight_second, 0) + bias_second[...]
+    for run in runs(count - 2):
+        pre_second = tap_sum(hidden, *run, weight_second, 0) + bias_second[...]
         value, slope = gelu_pair(pre_second)
-        output.append(symmetric[k].astype(jnp.float32) + value)
-        grad_second.append((gradient[k] * slope).astype(jnp.bfloat16))
-    grad_first = [
-        (tap_sum(grad_second, k, weight_third, 1) * slope_first[k]).astype(jnp.bfloat16)
-        for k in range(chunks)
-    ]
-    for k in range(chunks):
-        grad_sym = (gradient[k] + tap_sum(grad_first, k, weight_fourth, 1)).astype(jnp.bfloat16)
-        grad_sym = grad_sym.astype(jnp.float32)
-        finished = jnp.where(low, output[k], grad_sym + swapped(grad_sym)).astype(jnp.bfloat16)
-        share_cols = count // chunks
-        window[k * share_cols : (k + 1) * share_cols] = finished.reshape(share_cols, class_rows, width)
+        output.append(columns(symmetric, *run).astype(jnp.float32) + value)
+        grad_second.append((columns(gradient, *run) * slope).astype(jnp.bfloat16))
+    output, grad_second = jnp.concatenate(output, 0), jnp.concatenate(grad_second, 0)
+    grad_first = jnp.concatenate(
+        [
+            (tap_sum(grad_second, *run, weight_third, 1) * columns(slope_first, *run)).astype(
+                jnp.bfloat16
+            )
+            for run in runs(count - 3)
+        ],
+        0,
+    )
+    for run in runs(share):
+        total_sum = columns(gradient, *run) + tap_sum(grad_first, *run, weight_fourth, 1)
+        grad_sym = total_sum.astype(jnp.bfloat16).astype(jnp.float32)
+        grad_input = grad_sym + swapped(grad_sym)
+        finished = jnp.where(low(grad_input), columns(output, *run), grad_input)
+        finished = finished.astype(jnp.bfloat16).reshape(run[1] - run[0], class_rows, width)
+        window[run[0] : run[1]] = finished
 
     for index, (a, b) in enumerate(class_order()):
         r, c = divmod(index, half_count)
-        kept = window[pl.ds(half * CONVS + c * part_cols, part_cols)]
-        kept = kept[:, r * part_rows : (r + 1) * part_rows]
-        result[a * DILATION_STEP + b] = kept.reshape(part, width)
+        kept = [
+            window[inward(c * part_cols + k, share), r * part_rows : (r + 1) * part_rows]
+            for k in range(part_cols)
+        ]
+        result[a * DILATION_STEP + b] = jnp.concatenate(kept, 0)
 
 
 def class_chains(row_count, part_cols, own, other, *parameters):
     blocks, part, width = own.shape
     class_cols, class_rows = blocks // row_count * part_cols, row_count * (part // part_cols)
-    count = class_cols // HALVES + CONVS
+    share = class_cols // HALVES
     return pl.pallas_call(
         functools.partial(class_kernel, row_count, part_cols),
         out_shape=jax.ShapeDtypeStruct((blocks // HALVES, part, width), jnp.bfloat16),
@@ -317,7 +345,7 @@
         out_specs=pl.BlockSpec(memory_space=pltpu.VMEM),
         scratch_shapes=[
             pltpu.VMEM(((class_cols + 1) * class_rows, width), jnp.float32),
-            pltpu.VMEM((count, class_rows, width), jnp.bfloat16),
+            pltpu.VMEM((share, class_rows, width), jnp.bfloat16),
         ],
         compiler_params=pltpu.CompilerParams(vmem_limit_bytes=32 * 2**20),
     )(own, other, *parameters)
@@ -332,12 +360,12 @@
     parts = class_parts(row_count, feature_map, cotangent)
     parts = parts.reshape(row_count * col_count, part_cols * part_rows, 2 * channels)
     own = lax.all_to_all(parts, both, 0, 0, tiled=True)
+    half_count = col_count // HALVES
     raw = (kernel_first, kernel_second, bias_first, bias_second)
     own, *raw = lax.optimization_barrier((own,) + raw)
     other = lax.ppermute(own, "col", [(i, i ^ 1) for i in range(col_count)])
-    result = class_chains(row_count, part_cols, own, other, *chain_matrices(*raw))
-
-    half_count = col_count // HALVES
+    result = class_chains(row_count, part_cols, own, other, *chain_matrices(half_count, *raw))
+
     order = sorted(range(step * step), key=lambda index: class_order()[index])
     halves = [
         [i // half_count * col_count + h * half_count + i % half_count for i in order]

time: 31.2 us -> 31.1 us (level)
  no operation moved by 1% of the time
where the time goes in v8:
time: 31.1 us; the launch traced here: 30.9 us
  blocking collectives  25.1 us (81%)
  Pallas kernels  1.87 us (6%)
  local copies, waits for them, and re-layouts  1.51 us (5%)
  other arithmetic  1.08 us (3%)
  between operations  0.68 us (2%)
  waiting for transfers between devices  0.39 us (1%)
    all_to_all x1, blocking collectives, by_classes(): own = lax.all_to_all(parts, both, 0, 0, tiled=True)  17.4 us
    all_to_all x1, blocking collectives, by_classes(): lax.all_to_all(result, both, 0, 0, axis_index_groups=halves, tiled=True)  7.69 us
    pallas_call x1, Pallas kernels, class_chains(): pl.pallas_call(functools.partial(class_kernel, row_count, part_cols), out...  1.54 us
    convert_element_type x1, other arithmetic, class_parts(): tile = jnp.concatenate([feature_map, cotangent], 2).astype(jnp.float32)  1.08 us
    slice x1, local copies, waits for them, and re-layouts, by_classes(): return (back[..., :channels], back[..., channels:])  0.77 us
    unnamed x8, local copies, waits for them, and re-layouts  0.67 us
  transfers between devices with their start and end apart: 1, of which 1 were waited for; matrix products, arithmetic and copies ran while one was open for 0% of the time, Pallas kernels for 1%

profile of v8, /device:TPU:0, one launch (start us, length us, event | category | flops | bytes accessed | tf_op | source)
XLA Modules:
  0.0 30.9 jit_solution(1456107781815553911)
XLA Ops:
  0.6 1.1 %maximum_convert_fusion.whole = f32[512,128]{1,0:T(8,128)S(1)} fusion(bf16[512,64]{1,0:T(8,128)(2,1)} %bitcast.14, bf16[512,64]{1,0:T(8,128)(2,1)} %bitcast.15), kind=kLoop, calls=%fused_computation | loop fusion | flops 262144 | bytes 393216 | tf_op jit(solution)/shard_map/convert_element_type | solution.py:187
  1.7 0.2 shard_map.77
  1.9 0.0 copy-start
  1.9 0.0 copy-start.1
  1.9 17.4 %all_to_all.10.own = bf16[32,32,128]{2,1,0:T(8,128)(2,1)S(1)} all-to-all(bf16[32,32,128]{2,1,0:T(8,128)(2,1)S(1)} %bitcast.9), channel_id=1, replica_groups=mesh['row'=2,'col'=16] {'row','col'}, dimensions={0} | all-to-all | bytes 524288 | tf_op jit(solution)/shard_map/all_to_all | solution.py:362
  19.3 0.3 collective-permute-start
  19.6 0.0 copy-start.2
  19.6 0.0 copy-start.3
  19.6 0.0 copy-done
  19.6 0.0 copy-done.1
  19.6 0.6 %copy-done.2 = f32[64]{0:T(128)S(1)} copy-done((f32[64]{0:T(128)S(1)}, f32[64]{0:T(128)}, u32[]{:S(2)}) %copy-start.2) | copy-done | bytes 280
  20.3 0.0 copy-done.3
  20.3 0.2 shard_map.78
  20.5 0.4 %collective-permute-done.other = bf16[32,32,128]{2,1,0:T(8,128)(2,1)S(1)} collective-permute-done((bf16[32,32,128]{2,1,0:T(8,128)(2,1)S(1)}, bf16[32,32,128]{2,1,0:T(8,128)(2,1)S(1)}, u32[]{:S(2)}, u32[]{:S(2)}) %collective-permute-start) | collective-permute-done | bytes 262176 | tf_op jit(solution)/shard_map/ppermute | solution.py:366
  20.8 1.5 %shard_map.79 = bf16[16,32,128]{2,1,0:T(8,128)(2,1)S(1)} custom-call(bf16[32,32,128]{2,1,0:T(8,128)(2,1)S(1)} %all_to_all.10.own, bf16[32,32,128]{2,1,0:T(8,128)(2,1)S(1)} %collective-permute-done.other, bf16[256,384]{1,0:T(8,128)(2,1)S(1)} %get-tuple-element.18.weight_first, bf16[384,384]{1,0:T(8,128)(2,1)S(1)} %get-tuple-element.19.weight_second, ...), custom_call_target="tpu_custom_call" | custom-call | tf_op jit(solution)/shard_map/pallas_call | solution.py:341
  22.4 7.7 %all_to_all.11 = bf16[16,32,128]{2,1,0:T(8,128)(2,1)S(1)} all-to-all(bf16[16,32,128]{2,1,0:T(8,128)(2,1)S(1)} %shard_map.79), channel_id=1, replica_groups={{23,21,19,17,20,22,7,5,18,6,3,1,16,4,0,2},{31,29,27,25,28,30,15,13,26,1..., dimensions={0} | all-to-all | bytes 262144 | tf_op jit(solution)/shard_map/all_to_all | solution.py:374
  30.1 0.1 copy.8
  30.2 0.8 %fusion = (bf16[64,8,64]{2,1,0:T(8,128)(2,1)}, bf16[64,8,64]{2,1,0:T(8,128)(2,1)}) fusion(bf16[64,8,128]{2,1,0:T(8,128)(2,1)S(1)} %bitcast.12), kind=kLoop, calls=%fused_computation.1 | loop fusion | bytes 262144 | tf_op jit(solution)/shard_map/slice | solution.py:377
Async XLA Ops:
  1.9 17.7 %copy-start = (bf16[3,3,64,64]{3,2,1,0:T(8,128)(2,1)S(1)}, bf16[3,3,64,64]{3,2,1,0:T(8,128)(2,1)}, u32[]{:S(2)}) copy-start(bf16[3,3,64,64]{3,2,1,0:T(8,128)(2,1)} %weight_first) | copy-start | bytes 221188
  1.9 17.7 %copy-start.1 = (bf16[3,3,64,64]{3,2,1,0:T(8,128)(2,1)S(1)}, bf16[3,3,64,64]{3,2,1,0:T(8,128)(2,1)}, u32[]{:S(2)}) copy-start(bf16[3,3,64,64]{3,2,1,0:T(8,128)(2,1)} %weight_second) | copy-start | bytes 221188
  19.3 1.5 %collective-permute-start = (bf16[32,32,128]{2,1,0:T(8,128)(2,1)S(1)}, bf16[32,32,128]{2,1,0:T(8,128)(2,1)S(1)}, u32[]{:S(2)}, u32[]{:S(2)}) collective-permute-start(bf16[32,32,128]{2,1,0:T(8,128)(2,1)S(1)} %all_to_all.10.own), channel_id=1, source_target_pairs={{0,1},{1,0},{2,3},{3,2},{4,5},{5,4},{6,7},{7,6},{8,9},{9,8},{10,11... | collective-permute-start | bytes 786440 | tf_op jit(solution)/shard_map/ppermute | solution.py:366
  19.6 0.7 %copy-start.2 = (f32[64]{0:T(128)S(1)}, f32[64]{0:T(128)}, u32[]{:S(2)}) copy-start(f32[64]{0:T(128)} %param.8) | copy-start | bytes 772
  19.6 0.7 %copy-start.3 = (f32[64]{0:T(128)S(1)}, f32[64]{0:T(128)}, u32[]{:S(2)}) copy-start(f32[64]{0:T(128)} %param.10) | copy-start | bytes 772

commit v9 on v7

--- a/solution.py
+++ b/solution.py
@@ -107,24 +107,26 @@
     return output, add_rounded(grad_sym, mirror(grad_sym))
 
 
-def matrix_kernel(weight_first, weight_second, bias_first, bias_second, *outputs):
+def matrix_kernel(half_count, weight_first, weight_second, bias_first, bias_second, *outputs):
     first, second, third, fourth, first_bias, second_bias = outputs
     taps, channels = weight_first.shape[0], weight_first.shape[2]
     gap = jnp.zeros(weight_first.shape[2:], weight_first.dtype)
+    half = lax.div(lax.axis_index("col"), half_count)
     for weight, ahead, behind in (
         (weight_first, first, fourth),
         (weight_second, second, third),
     ):
         for p in range(taps):
+            along = half * (taps - 1) + (1 - 2 * half) * p
             for q in range(taps):
-                upper = jnp.concatenate([weight[q, p], gap], 1)
-                lower = jnp.concatenate([gap, weight[p, q]], 1)
+                upper = jnp.concatenate([weight[q, along], gap], 1)
+                lower = jnp.concatenate([gap, weight[along, q]], 1)
                 block = jnp.concatenate([upper, lower], 0)
                 columns = pl.ds(2 * channels * q, 2 * channels)
                 if ahead is second:
                     ahead[pl.ds(2 * channels * p, 2 * channels), columns] = block
                 else:
-                    joint = jnp.concatenate([weight[q, p], weight[p, q]], 1)
+                    joint = jnp.concatenate([weight[q, along], weight[along, q]], 1)
                     ahead[pl.ds(channels * p, channels), columns] = joint
                 p_back, q_back = taps - 1 - p, taps - 1 - q
                 behind[
@@ -137,12 +139,12 @@
         wide[...] = jnp.concatenate([bias[...], bias[...]], 1)
 
 
-def chain_matrices(weight_first, weight_second, bias_first, bias_second):
+def chain_matrices(half_count, weight_first, weight_second, bias_first, bias_second):
     taps, channels = weight_first.shape[0], weight_first.shape[2]
     size = taps * 2 * channels
     vmem = pl.BlockSpec(memory_space=pltpu.VMEM)
     return pl.pallas_call(
-        matrix_kernel,
+        functools.partial(matrix_kernel, half_count),
         out_shape=[
             jax.ShapeDtypeStruct(((taps + 1) * channels, size), jnp.bfloat16),
             *[jax.ShapeDtypeStruct((size, size), jnp.bfloat16)] * 3,
@@ -221,95 +223,125 @@
     place = lax.axis_index("row") * half_count + lax.rem(column, half_count)
     evens = [index for index, (a, b) in enumerate(class_order()) if a == b]
     even = functools.reduce(jnp.logical_or, [place == index for index in evens])
-    begin = half * (share - CONVS)
-    cells = count * class_rows
-    low = lax.broadcasted_iota(jnp.int32, (cells, width), 1) < channels
     row = lax.broadcasted_iota(jnp.int32, (1, class_rows, width), 1)
 
-    pieces = []
-    for r in range(row_count):
-        reach = pl.ds(r * col_count + half * ((share - CONVS) // part_cols), count // part_cols)
-        pieces.append(own[reach].reshape(count, part_rows, width))
-    straight = jnp.concatenate(pieces, 1).astype(jnp.float32).reshape(cells, width)
-
-    for r in range(row_count):
-        reach = slice(r * col_count, (r + 1) * col_count)
-        piece = jnp.where(even, own[reach], other[reach]).astype(jnp.float32)
-        piece = piece.reshape(class_cols, part_rows, width)
-        for k in range(class_cols):
-            turning[pl.ds(k * class_rows + r * part_rows, part_rows), :] = piece[k]
-    turned = jnp.concatenate(
-        [turning[pl.ds(begin + i, class_cols, stride=class_rows), :] for i in range(count)], 0
-    )
-
-    def swapped(value):
-        return pltpu.roll(value, channels, 1)
-
-    chunks = 2
-    size = cells // chunks
-    rows = [slice(k * size, (k + 1) * size) for k in range(chunks)]
-    low = low[:size]
-
-    def tap_sum(images, k, matrix, dimension, doubled=False):
-        gap = jnp.zeros((class_rows, width), jnp.bfloat16)
-        image = images[k]
-        before = images[k - 1][-class_rows:] if k else gap
-        before = jnp.concatenate([before, image[:-class_rows]], 0)
-        after = images[k + 1][:class_rows] if k + 1 < chunks else gap
-        after = jnp.concatenate([image[class_rows:], after], 0)
-        columns = [jnp.where(low, before, image), after] if doubled else [before, image, after]
-        taps = lax.dot_general(
-            jnp.concatenate(columns, 1),
-            matrix[...],
-            (((1,), (dimension,)), ((), ())),
-            preferred_element_type=jnp.float32,
+    def chains(half):
+        def inward(index, total):
+            return total - 1 - index if half else index
+
+        pieces = []
+        for n in range(count // part_cols):
+            blocks = [own[r * col_count + inward(n, col_count)] for r in range(row_count)]
+            for k in range(part_cols):
+                ends = [slice(m * part_rows, (m + 1) * part_rows) for m in (k, part_cols - 1 - k)]
+                pieces += [block[ends[half]] for block in blocks]
+        straight = jnp.concatenate(pieces, 0).astype(jnp.float32)
+
+        for r in range(row_count):
+            reach = slice(r * col_count, (r + 1) * col_count)
+            piece = jnp.where(even, own[reach], other[reach]).astype(jnp.float32)
+            piece = piece.reshape(class_cols, part_rows, width)
+            for k in range(class_cols):
+                turning[pl.ds(k * class_rows + r * part_rows, part_rows), :] = piece[k]
+        turned = jnp.concatenate(
+            [
+                turning[pl.ds(inward(n, class_cols), class_cols, stride=class_rows), :]
+                for n in range(count)
+            ],
+            0,
         )
-        taps = taps.reshape(count // chunks, class_rows, 3 * width)
-        above = jnp.where(row == 0, 0.0, pltpu.roll(taps[:, :, :width], 1, 1))
-        below = pltpu.roll(taps[:, :, 2 * width :], class_rows - 1, 1)
-        below = jnp.where(row == class_rows - 1, 0.0, below)
-        return (above + taps[:, :, width : 2 * width] + below).reshape(size, width)
-
-    symmetric, gradient = [], []
-    for k in range(chunks):
-        total = straight[rows[k]] + turned[rows[k]]
-        symmetric.append(jnp.where(low, total, swapped(total)).astype(jnp.bfloat16))
-        gradient.append(jnp.where(low, swapped(straight[rows[k]]), turned[rows[k]]))
-
-    hidden, slope_first = [], []
-    for k in range(chunks):
-        pre_first = tap_sum(symmetric, k, weight_first, 0, True) + bias_first[...]
-        value, slope = gelu_pair(pre_first)
-        hidden.append(value.astype(jnp.bfloat16))
-        slope_first.append(slope)
-    output, grad_second = [], []
-    for k in range(chunks):
-        pre_second = tap_sum(hidden, k, weight_second, 0) + bias_second[...]
-        value, slope = gelu_pair(pre_second)
-        output.append(symmetric[k].astype(jnp.float32) + value)
-        grad_second.append((gradient[k] * slope).astype(jnp.bfloat16))
-    grad_first = [
-        (tap_sum(grad_second, k, weight_third, 1) * slope_first[k]).astype(jnp.bfloat16)
-        for k in range(chunks)
-    ]
-    for k in range(chunks):
-        grad_sym = (gradient[k] + tap_sum(grad_first, k, weight_fourth, 1)).astype(jnp.bfloat16)
-        grad_sym = grad_sym.astype(jnp.float32)
-        finished = jnp.where(low, output[k], grad_sym + swapped(grad_sym)).astype(jnp.bfloat16)
-        share_cols = count // chunks
-        window[k * share_cols : (k + 1) * share_cols] = finished.reshape(share_cols, class_rows, width)
-
-    for index, (a, b) in enumerate(class_order()):
-        r, c = divmod(index, half_count)
-        kept = window[pl.ds(half * CONVS + c * part_cols, part_cols)]
-        kept = kept[:, r * part_rows : (r + 1) * part_rows]
-        result[a * DILATION_STEP + b] = kept.reshape(part, width)
+
+        def low(value):
+            return lax.broadcasted_iota(jnp.int32, value.shape, 1) < channels
+
+        def swapped(value):
+            return pltpu.roll(value, channels, 1)
+
+        def tap_sum(image, begin, end, matrix, dimension, doubled=False):
+            first, last = begin * class_rows, end * class_rows
+            gap = [jnp.zeros((class_rows, width), image.dtype)] if begin == 0 else []
+            before = image[max(first - class_rows, 0) : last - class_rows]
+            before = jnp.concatenate(gap + [before], 0)
+            after = image[first + class_rows : last + class_rows]
+            image = image[first:last]
+            columns = [jnp.where(low(image), before, image), after]
+            def product(value, weights):
+                return lax.dot_general(
+                    value, weights, (((1,), (dimension,)), ((), ())), preferred_element_type=jnp.float32
+                )
+
+            if doubled:
+                taps = product(jnp.concatenate(columns, 1), matrix[...])
+            elif dimension == 0:
+                taps = product(jnp.concatenate([image, after], 1), matrix[width:, :])
+                taps = taps + product(before, matrix[:width, :])
+            else:
+                taps = product(jnp.concatenate([image, after], 1), matrix[:, width:])
+                taps = taps + product(before, matrix[:, :width])
+            taps = taps.reshape(end - begin, class_rows, 3 * width)
+            above = jnp.where(row == 0, 0.0, pltpu.roll(taps[:, :, :width], 1, 1))
+            below = pltpu.roll(taps[:, :, 2 * width :], class_rows - 1, 1)
+            below = jnp.where(row == class_rows - 1, 0.0, below)
+            return (above + taps[:, :, width : 2 * width] + below).reshape(last - first, width)
+
+        def runs(total):
+            cut = (total + 1) // 2
+            return (0, cut), (cut, total)
+
+        def columns(value, begin, end):
+            return value[begin * class_rows : end * class_rows]
+
+        symmetric = straight + turned
+        symmetric = jnp.where(low(symmetric), symmetric, swapped(symmetric)).astype(jnp.bfloat16)
+        gradient = jnp.where(low(turned), swapped(straight), turned)
+
+        hidden, slope_first = [], []
+        for run in runs(count - 1):
+            pre_first = tap_sum(symmetric, *run, weight_first, 0, True) + bias_first[...]
+            value, slope = gelu_pair(pre_first)
+            hidden.append(value.astype(jnp.bfloat16))
+            slope_first.append(slope)
+        hidden, slope_first = jnp.concatenate(hidden, 0), jnp.concatenate(slope_first, 0)
+        output, grad_second = [], []
+        for run in runs(count - 2):
+            pre_second = tap_sum(hidden, *run, weight_second, 0) + bias_second[...]
+            value, slope = gelu_pair(pre_second)
+            output.append(columns(symmetric, *run).astype(jnp.float32) + value)
+            grad_second.append((columns(gradient, *run) * slope).astype(jnp.bfloat16))
+        output, grad_second = jnp.concatenate(output, 0), jnp.concatenate(grad_second, 0)
+        grad_first = jnp.concatenate(
+            [
+                (tap_sum(grad_second, *run, weight_third, 1) * columns(slope_first, *run)).astype(
+                    jnp.bfloat16
+                )
+                for run in runs(count - 3)
+            ],
+            0,
+        )
+        for run in runs(share):
+            total_sum = columns(gradient, *run) + tap_sum(grad_first, *run, weight_fourth, 1)
+            grad_sym = total_sum.astype(jnp.bfloat16).astype(jnp.float32)
+            grad_input = grad_sym + swapped(grad_sym)
+            finished = jnp.where(low(grad_input), columns(output, *run), grad_input)
+            finished = finished.astype(jnp.bfloat16).reshape(run[1] - run[0], class_rows, width)
+            window[run[0] : run[1]] = finished
+
+        for index, (a, b) in enumerate(class_order()):
+            r, c = divmod(index, half_count)
+            kept = [
+                window[inward(c * part_cols + k, share), r * part_rows : (r + 1) * part_rows]
+                for k in range(part_cols)
+            ]
+            result[a * DILATION_STEP + b] = jnp.concatenate(kept, 0)
+
+    for index in range(HALVES):
+        pl.when(half == index)(functools.partial(chains, index))
 
 
 def class_chains(row_count, part_cols, own, other, *parameters):
     blocks, part, width = own.shape
     class_cols, class_rows = blocks // row_count * part_cols, row_count * (part // part_cols)
-    count = class_cols // HALVES + CONVS
+    share = class_cols // HALVES
     return pl.pallas_call(
         functools.partial(class_kernel, row_count, part_cols),
         out_shape=jax.ShapeDtypeStruct((blocks // HALVES, part, width), jnp.bfloat16),
@@ -317,7 +349,7 @@
         out_specs=pl.BlockSpec(memory_space=pltpu.VMEM),
         scratch_shapes=[
             pltpu.VMEM(((class_cols + 1) * class_rows, width), jnp.float32),
-            pltpu.VMEM((count, class_rows, width), jnp.bfloat16),
+            pltpu.VMEM((share, class_rows, width), jnp.bfloat16),
         ],
         compiler_params=pltpu.CompilerParams(vmem_limit_bytes=32 * 2**20),
     )(own, other, *parameters)
@@ -332,12 +364,12 @@
     parts = class_parts(row_count, feature_map, cotangent)
     parts = parts.reshape(row_count * col_count, part_cols * part_rows, 2 * channels)
     own = lax.all_to_all(parts, both, 0, 0, tiled=True)
+    half_count = col_count // HALVES
     raw = (kernel_first, kernel_second, bias_first, bias_second)
     own, *raw = lax.optimization_barrier((own,) + raw)
     other = lax.ppermute(own, "col", [(i, i ^ 1) for i in range(col_count)])
-    result = class_chains(row_count, part_cols, own, other, *chain_matrices(*raw))
-
-    half_count = col_count // HALVES
+    result = class_chains(row_count, part_cols, own, other, *chain_matrices(half_count, *raw))
+
     order = sorted(range(step * step), key=lambda index: class_order()[index])
     halves = [
         [i // half_count * col_count + h * half_count + i % half_count for i in order]

time: 31.2 us -> 31 us (level)
  no operation moved by 1% of the time
where the time goes in v9:
time: 31 us; the launch traced here: 30.8 us
  blocking collectives  25.1 us (81%)
  Pallas kernels  1.77 us (6%)
  local copies, waits for them, and re-layouts  1.51 us (5%)
  other arithmetic  1.08 us (3%)
  between operations  0.67 us (2%)
  waiting for transfers between devices  0.39 us (1%)
    all_to_all x1, blocking collectives, by_classes(): own = lax.all_to_all(parts, both, 0, 0, tiled=True)  17.4 us
    all_to_all x1, blocking collectives, by_classes(): lax.all_to_all(result, both, 0, 0, axis_index_groups=halves, tiled=True)  7.69 us
    pallas_call x1, Pallas kernels, class_chains(): pl.pallas_call(functools.partial(class_kernel, row_count, part_cols), out...  1.44 us
    convert_element_type x1, other arithmetic, class_parts(): tile = jnp.concatenate([feature_map, cotangent], 2).astype(jnp.float32)  1.08 us
    slice x1, local copies, waits for them, and re-layouts, by_classes(): return (back[..., :channels], back[..., channels:])  0.77 us
    unnamed x8, local copies, waits for them, and re-layouts  0.67 us
  transfers between devices with their start and end apart: 1, of which 1 were waited for; matrix products, arithmetic and copies ran while one was open for 0% of the time, Pallas kernels for 1%

profile of v9, /device:TPU:0, one launch (start us, length us, event | category | flops | bytes accessed | tf_op | source)
XLA Modules:
  0.0 30.8 jit_solution(12258595987955284333)
XLA Ops:
  0.6 1.1 %maximum_convert_fusion.whole = f32[512,128]{1,0:T(8,128)S(1)} fusion(bf16[512,64]{1,0:T(8,128)(2,1)} %bitcast.14, bf16[512,64]{1,0:T(8,128)(2,1)} %bitcast.15), kind=kLoop, calls=%fused_computation | loop fusion | flops 262144 | bytes 393216 | tf_op jit(solution)/shard_map/convert_element_type | solution.py:187
  1.7 0.2 shard_map.77
  1.9 0.0 copy-start
  1.9 0.0 copy-start.1
  1.9 17.4 %all_to_all.10.own = bf16[32,32,128]{2,1,0:T(8,128)(2,1)S(1)} all-to-all(bf16[32,32,128]{2,1,0:T(8,128)(2,1)S(1)} %bitcast.9), channel_id=1, replica_groups=mesh['row'=2,'col'=16] {'row','col'}, dimensions={0} | all-to-all | bytes 524288 | tf_op jit(solution)/shard_map/all_to_all | solution.py:366
  19.3 0.3 collective-permute-start
  19.6 0.0 copy-start.2
  19.6 0.0 copy-start.3
  19.6 0.0 copy-done
  19.6 0.0 copy-done.1
  19.6 0.6 %copy-done.2 = f32[64]{0:T(128)S(1)} copy-done((f32[64]{0:T(128)S(1)}, f32[64]{0:T(128)}, u32[]{:S(2)}) %copy-start.2) | copy-done | bytes 280
  20.3 0.0 copy-done.3
  20.3 0.2 shard_map.78
  20.5 0.4 %collective-permute-done.other = bf16[32,32,128]{2,1,0:T(8,128)(2,1)S(1)} collective-permute-done((bf16[32,32,128]{2,1,0:T(8,128)(2,1)S(1)}, bf16[32,32,128]{2,1,0:T(8,128)(2,1)S(1)}, u32[]{:S(2)}, u32[]{:S(2)}) %collective-permute-start) | collective-permute-done | bytes 262176 | tf_op jit(solution)/shard_map/ppermute | solution.py:370
  20.8 1.4 %shard_map.79 = bf16[16,32,128]{2,1,0:T(8,128)(2,1)S(1)} custom-call(bf16[32,32,128]{2,1,0:T(8,128)(2,1)S(1)} %all_to_all.10.own, bf16[32,32,128]{2,1,0:T(8,128)(2,1)S(1)} %collective-permute-done.other, bf16[256,384]{1,0:T(8,128)(2,1)S(1)} %get-tuple-element.18.weight_first, bf16[384,384]{1,0:T(8,128)(2,1)S(1)} %get-tuple-element.19.weight_second, ...), custom_call_target="tpu_custom_call" | custom-call | tf_op jit(solution)/shard_map/pallas_call | solution.py:345
  22.3 7.7 %all_to_all.11 = bf16[16,32,128]{2,1,0:T(8,128)(2,1)S(1)} all-to-all(bf16[16,32,128]{2,1,0:T(8,128)(2,1)S(1)} %shard_map.79), channel_id=1, replica_groups={{23,21,19,17,20,22,7,5,18,6,3,1,16,4,0,2},{31,29,27,25,28,30,15,13,26,1..., dimensions={0} | all-to-all | bytes 262144 | tf_op jit(solution)/shard_map/all_to_all | solution.py:378
  30.0 0.1 copy.8
  30.1 0.8 %fusion = (bf16[64,8,64]{2,1,0:T(8,128)(2,1)}, bf16[64,8,64]{2,1,0:T(8,128)(2,1)}) fusion(bf16[64,8,128]{2,1,0:T(8,128)(2,1)S(1)} %bitcast.12), kind=kLoop, calls=%fused_computation.1 | loop fusion | bytes 262144 | tf_op jit(solution)/shard_map/slice | solution.py:381
Async XLA Ops:
  1.9 17.7 %copy-start = (bf16[3,3,64,64]{3,2,1,0:T(8,128)(2,1)S(1)}, bf16[3,3,64,64]{3,2,1,0:T(8,128)(2,1)}, u32[]{:S(2)}) copy-start(bf16[3,3,64,64]{3,2,1,0:T(8,128)(2,1)} %weight_first) | copy-start | bytes 221188
  1.9 17.7 %copy-start.1 = (bf16[3,3,64,64]{3,2,1,0:T(8,128)(2,1)S(1)}, bf16[3,3,64,64]{3,2,1,0:T(8,128)(2,1)}, u32[]{:S(2)}) copy-start(bf16[3,3,64,64]{3,2,1,0:T(8,128)(2,1)} %weight_second) | copy-start | bytes 221188
  19.3 1.5 %collective-permute-start = (bf16[32,32,128]{2,1,0:T(8,128)(2,1)S(1)}, bf16[32,32,128]{2,1,0:T(8,128)(2,1)S(1)}, u32[]{:S(2)}, u32[]{:S(2)}) collective-permute-start(bf16[32,32,128]{2,1,0:T(8,128)(2,1)S(1)} %all_to_all.10.own), channel_id=1, source_target_pairs={{0,1},{1,0},{2,3},{3,2},{4,5},{5,4},{6,7},{7,6},{8,9},{9,8},{10,11... | collective-permute-start | bytes 786440 | tf_op jit(solution)/shard_map/ppermute | solution.py:370
  19.6 0.7 %copy-start.2 = (f32[64]{0:T(128)S(1)}, f32[64]{0:T(128)}, u32[]{:S(2)}) copy-start(f32[64]{0:T(128)} %param.8) | copy-start | bytes 772
  19.6 0.7 %copy-start.3 = (f32[64]{0:T(128)S(1)}, f32[64]{0:T(128)}, u32[]{:S(2)}) copy-start(f32[64]{0:T(128)} %param.10) | copy-start | bytes 772

commit v10 on v9

--- a/solution.py
+++ b/solution.py
@@ -241,8 +241,12 @@
             reach = slice(r * col_count, (r + 1) * col_count)
             piece = jnp.where(even, own[reach], other[reach]).astype(jnp.float32)
             piece = piece.reshape(class_cols, part_rows, width)
+            read = [inward(n, class_cols) - r * part_rows for n in range(count)]
+            read = [n for n in read if 0 <= n < part_rows]
+            low_row, high_row = min(read) // 8 * 8, (max(read) // 8 + 1) * 8
             for k in range(class_cols):
-                turning[pl.ds(k * class_rows + r * part_rows, part_rows), :] = piece[k]
+                rows = pl.ds(k * class_rows + r * part_rows + low_row, high_row - low_row)
+                turning[rows, :] = piece[k, low_row:high_row]
         turned = jnp.concatenate(
             [
                 turning[pl.ds(inward(n, class_cols), class_cols, stride=class_rows), :]

time: 31 us -> 31 us (level)
  no operation moved by 1% of the time
where the time goes in v10:
time: 31 us; the launch traced here: 30.8 us
  blocking collectives  25.1 us (81%)
  Pallas kernels  1.75 us (6%)
  local copies, waits for them, and re-layouts  1.51 us (5%)
  other arithmetic  1.08 us (3%)
  between operations  0.67 us (2%)
  waiting for transfers between devices  0.39 us (1%)
    all_to_all x1, blocking collectives, by_classes(): own = lax.all_to_all(parts, both, 0, 0, tiled=True)  17.4 us
    all_to_all x1, blocking collectives, by_classes(): lax.all_to_all(result, both, 0, 0, axis_index_groups=halves, tiled=True)  7.7 us
    pallas_call x1, Pallas kernels, class_chains(): pl.pallas_call(functools.partial(class_kernel, row_count, part_cols), out...  1.42 us
    convert_element_type x1, other arithmetic, class_parts(): tile = jnp.concatenate([feature_map, cotangent], 2).astype(jnp.float32)  1.08 us
    slice x1, local copies, waits for them, and re-layouts, by_classes(): return (back[..., :channels], back[..., channels:])  0.77 us
    unnamed x8, local copies, waits for them, and re-layouts  0.67 us
  transfers between devices with their start and end apart: 1, of which 1 were waited for; matrix products, arithmetic and copies ran while one was open for 0% of the time, Pallas kernels for 1%

profile of v10, /device:TPU:0, one launch (start us, length us, event | category | flops | bytes accessed | tf_op | source)
XLA Modules:
  0.0 30.8 jit_solution(10246866949579757208)
XLA Ops:
  0.6 1.1 %maximum_convert_fusion.whole = f32[512,128]{1,0:T(8,128)S(1)} fusion(bf16[512,64]{1,0:T(8,128)(2,1)} %bitcast.14, bf16[512,64]{1,0:T(8,128)(2,1)} %bitcast.15), kind=kLoop, calls=%fused_computation | loop fusion | flops 262144 | bytes 393216 | tf_op jit(solution)/shard_map/convert_element_type | solution.py:187
  1.7 0.2 shard_map.77
  1.9 0.0 copy-start
  1.9 0.0 copy-start.1
  1.9 17.4 %all_to_all.10.own = bf16[32,32,128]{2,1,0:T(8,128)(2,1)S(1)} all-to-all(bf16[32,32,128]{2,1,0:T(8,128)(2,1)S(1)} %bitcast.9), channel_id=1, replica_groups=mesh['row'=2,'col'=16] {'row','col'}, dimensions={0} | all-to-all | bytes 524288 | tf_op jit(solution)/shard_map/all_to_all | solution.py:370
  19.3 0.3 collective-permute-start
  19.6 0.0 copy-start.2
  19.6 0.0 copy-start.3
  19.6 0.0 copy-done
  19.6 0.0 copy-done.1
  19.6 0.6 %copy-done.2 = f32[64]{0:T(128)S(1)} copy-done((f32[64]{0:T(128)S(1)}, f32[64]{0:T(128)}, u32[]{:S(2)}) %copy-start.2) | copy-done | bytes 280
  20.3 0.0 copy-done.3
  20.3 0.2 shard_map.78
  20.5 0.4 %collective-permute-done.other = bf16[32,32,128]{2,1,0:T(8,128)(2,1)S(1)} collective-permute-done((bf16[32,32,128]{2,1,0:T(8,128)(2,1)S(1)}, bf16[32,32,128]{2,1,0:T(8,128)(2,1)S(1)}, u32[]{:S(2)}, u32[]{:S(2)}) %collective-permute-start) | collective-permute-done | bytes 262176 | tf_op jit(solution)/shard_map/ppermute | solution.py:374
  20.8 1.4 %shard_map.79 = bf16[16,32,128]{2,1,0:T(8,128)(2,1)S(1)} custom-call(bf16[32,32,128]{2,1,0:T(8,128)(2,1)S(1)} %all_to_all.10.own, bf16[32,32,128]{2,1,0:T(8,128)(2,1)S(1)} %collective-permute-done.other, bf16[256,384]{1,0:T(8,128)(2,1)S(1)} %get-tuple-element.18.weight_first, bf16[384,384]{1,0:T(8,128)(2,1)S(1)} %get-tuple-element.19.weight_second, ...), custom_call_target="tpu_custom_call" | custom-call | tf_op jit(solution)/shard_map/pallas_call | solution.py:349
  22.3 7.7 %all_to_all.11 = bf16[16,32,128]{2,1,0:T(8,128)(2,1)S(1)} all-to-all(bf16[16,32,128]{2,1,0:T(8,128)(2,1)S(1)} %shard_map.79), channel_id=1, replica_groups={{23,21,19,17,20,22,7,5,18,6,3,1,16,4,0,2},{31,29,27,25,28,30,15,13,26,1..., dimensions={0} | all-to-all | bytes 262144 | tf_op jit(solution)/shard_map/all_to_all | solution.py:382
  30.0 0.1 copy.8
  30.0 0.8 %fusion = (bf16[64,8,64]{2,1,0:T(8,128)(2,1)}, bf16[64,8,64]{2,1,0:T(8,128)(2,1)}) fusion(bf16[64,8,128]{2,1,0:T(8,128)(2,1)S(1)} %bitcast.12), kind=kLoop, calls=%fused_computation.1 | loop fusion | bytes 262144 | tf_op jit(solution)/shard_map/slice | solution.py:385
Async XLA Ops:
  1.9 17.7 %copy-start = (bf16[3,3,64,64]{3,2,1,0:T(8,128)(2,1)S(1)}, bf16[3,3,64,64]{3,2,1,0:T(8,128)(2,1)}, u32[]{:S(2)}) copy-start(bf16[3,3,64,64]{3,2,1,0:T(8,128)(2,1)} %weight_first) | copy-start | bytes 221188
  1.9 17.7 %copy-start.1 = (bf16[3,3,64,64]{3,2,1,0:T(8,128)(2,1)S(1)}, bf16[3,3,64,64]{3,2,1,0:T(8,128)(2,1)}, u32[]{:S(2)}) copy-start(bf16[3,3,64,64]{3,2,1,0:T(8,128)(2,1)} %weight_second) | copy-start | bytes 221188
  19.3 1.5 %collective-permute-start = (bf16[32,32,128]{2,1,0:T(8,128)(2,1)S(1)}, bf16[32,32,128]{2,1,0:T(8,128)(2,1)S(1)}, u32[]{:S(2)}, u32[]{:S(2)}) collective-permute-start(bf16[32,32,128]{2,1,0:T(8,128)(2,1)S(1)} %all_to_all.10.own), channel_id=1, source_target_pairs={{0,1},{1,0},{2,3},{3,2},{4,5},{5,4},{6,7},{7,6},{8,9},{9,8},{10,11... | collective-permute-start | bytes 786440 | tf_op jit(solution)/shard_map/ppermute | solution.py:374
  19.6 0.7 %copy-start.2 = (f32[64]{0:T(128)S(1)}, f32[64]{0:T(128)}, u32[]{:S(2)}) copy-start(f32[64]{0:T(128)} %param.8) | copy-start | bytes 772
  19.6 0.7 %copy-start.3 = (f32[64]{0:T(128)S(1)}, f32[64]{0:T(128)}, u32[]{:S(2)}) copy-start(f32[64]{0:T(128)} %param.10) | copy-start | bytes 772

commit v11 on v10

--- a/solution.py
+++ b/solution.py
@@ -225,7 +225,7 @@
     even = functools.reduce(jnp.logical_or, [place == index for index in evens])
     row = lax.broadcasted_iota(jnp.int32, (1, class_rows, width), 1)
 
-    def chains(half):
+    def chains(half, mirrored):
         def inward(index, total):
             return total - 1 - index if half else index
 
@@ -239,7 +239,7 @@
 
         for r in range(row_count):
             reach = slice(r * col_count, (r + 1) * col_count)
-            piece = jnp.where(even, own[reach], other[reach]).astype(jnp.float32)
+            piece = mirrored[reach].astype(jnp.float32)
             piece = piece.reshape(class_cols, part_rows, width)
             read = [inward(n, class_cols) - r * part_rows for n in range(count)]
             read = [n for n in read if 0 <= n < part_rows]
@@ -339,7 +339,11 @@
             result[a * DILATION_STEP + b] = jnp.concatenate(kept, 0)
 
     for index in range(HALVES):
-        pl.when(half == index)(functools.partial(chains, index))
+        here = half == index
+        pl.when(jnp.logical_and(here, even))(functools.partial(chains, index, own))
+        pl.when(jnp.logical_and(here, jnp.logical_not(even)))(
+            functools.partial(chains, index, other)
+        )
 
 
 def class_chains(row_count, part_cols, own, other, *parameters):

time: 31 us -> 31 us (level)
  no operation moved by 1% of the time
where the time goes in v11:
time: 31 us; the launch traced here: 30.8 us
  blocking collectives  25.1 us (81%)
  Pallas kernels  1.72 us (6%)
  local copies, waits for them, and re-layouts  1.51 us (5%)
  other arithmetic  1.08 us (3%)
  between operations  0.68 us (2%)
  waiting for transfers between devices  0.39 us (1%)
    all_to_all x1, blocking collectives, by_classes(): own = lax.all_to_all(parts, both, 0, 0, tiled=True)  17.4 us
    all_to_all x1, blocking collectives, by_classes(): lax.all_to_all(result, both, 0, 0, axis_index_groups=halves, tiled=True)  7.7 us
    pallas_call x1, Pallas kernels, class_chains(): pl.pallas_call(functools.partial(class_kernel, row_count, part_cols), out...  1.39 us
    convert_element_type x1, other arithmetic, class_parts(): tile = jnp.concatenate([feature_map, cotangent], 2).astype(jnp.float32)  1.08 us
    slice x1, local copies, waits for them, and re-layouts, by_classes(): return (back[..., :channels], back[..., channels:])  0.77 us
    unnamed x8, local copies, waits for them, and re-layouts  0.67 us
  transfers between devices with their start and end apart: 1, of which 1 were waited for; matrix products, arithmetic and copies ran while one was open for 0% of the time, Pallas kernels for 1%

profile of v11, /device:TPU:0, one launch (start us, length us, event | category | flops | bytes accessed | tf_op | source)
XLA Modules:
  0.0 30.8 jit_solution(4481805495860283632)
XLA Ops:
  0.6 1.1 %maximum_convert_fusion.whole = f32[512,128]{1,0:T(8,128)S(1)} fusion(bf16[512,64]{1,0:T(8,128)(2,1)} %bitcast.14, bf16[512,64]{1,0:T(8,128)(2,1)} %bitcast.15), kind=kLoop, calls=%fused_computation | loop fusion | flops 262144 | bytes 393216 | tf_op jit(solution)/shard_map/convert_element_type | solution.py:187
  1.7 0.2 shard_map.77
  1.9 0.0 copy-start
  1.9 0.0 copy-start.1
  1.9 17.4 %all_to_all.10.own = bf16[32,32,128]{2,1,0:T(8,128)(2,1)S(1)} all-to-all(bf16[32,32,128]{2,1,0:T(8,128)(2,1)S(1)} %bitcast.9), channel_id=1, replica_groups=mesh['row'=2,'col'=16] {'row','col'}, dimensions={0} | all-to-all | bytes 524288 | tf_op jit(solution)/shard_map/all_to_all | solution.py:374
  19.3 0.3 collective-permute-start
  19.6 0.0 copy-start.2
  19.6 0.0 copy-start.3
  19.6 0.0 copy-done
  19.6 0.0 copy-done.1
  19.6 0.6 %copy-done.2 = f32[64]{0:T(128)S(1)} copy-done((f32[64]{0:T(128)S(1)}, f32[64]{0:T(128)}, u32[]{:S(2)}) %copy-start.2) | copy-done | bytes 280
  20.3 0.0 copy-done.3
  20.3 0.2 shard_map.78
  20.5 0.4 %collective-permute-done.other = bf16[32,32,128]{2,1,0:T(8,128)(2,1)S(1)} collective-permute-done((bf16[32,32,128]{2,1,0:T(8,128)(2,1)S(1)}, bf16[32,32,128]{2,1,0:T(8,128)(2,1)S(1)}, u32[]{:S(2)}, u32[]{:S(2)}) %collective-permute-start) | collective-permute-done | bytes 262176 | tf_op jit(solution)/shard_map/ppermute | solution.py:378
  20.8 1.4 %shard_map.79 = bf16[16,32,128]{2,1,0:T(8,128)(2,1)S(1)} custom-call(bf16[32,32,128]{2,1,0:T(8,128)(2,1)S(1)} %all_to_all.10.own, bf16[32,32,128]{2,1,0:T(8,128)(2,1)S(1)} %collective-permute-done.other, bf16[256,384]{1,0:T(8,128)(2,1)S(1)} %get-tuple-element.18.weight_first, bf16[384,384]{1,0:T(8,128)(2,1)S(1)} %get-tuple-element.19.weight_second, ...), custom_call_target="tpu_custom_call" | custom-call | tf_op jit(solution)/shard_map/pallas_call | solution.py:353
  22.2 7.7 %all_to_all.11 = bf16[16,32,128]{2,1,0:T(8,128)(2,1)S(1)} all-to-all(bf16[16,32,128]{2,1,0:T(8,128)(2,1)S(1)} %shard_map.79), channel_id=1, replica_groups={{23,21,19,17,20,22,7,5,18,6,3,1,16,4,0,2},{31,29,27,25,28,30,15,13,26,1..., dimensions={0} | all-to-all | bytes 262144 | tf_op jit(solution)/shard_map/all_to_all | solution.py:386
  29.9 0.1 copy.8
  30.0 0.8 %fusion = (bf16[64,8,64]{2,1,0:T(8,128)(2,1)}, bf16[64,8,64]{2,1,0:T(8,128)(2,1)}) fusion(bf16[64,8,128]{2,1,0:T(8,128)(2,1)S(1)} %bitcast.12), kind=kLoop, calls=%fused_computation.1 | loop fusion | bytes 262144 | tf_op jit(solution)/shard_map/slice | solution.py:389
Async XLA Ops:
  1.9 17.7 %copy-start = (bf16[3,3,64,64]{3,2,1,0:T(8,128)(2,1)S(1)}, bf16[3,3,64,64]{3,2,1,0:T(8,128)(2,1)}, u32[]{:S(2)}) copy-start(bf16[3,3,64,64]{3,2,1,0:T(8,128)(2,1)} %weight_first) | copy-start | bytes 221188
  1.9 17.7 %copy-start.1 = (bf16[3,3,64,64]{3,2,1,0:T(8,128)(2,1)S(1)}, bf16[3,3,64,64]{3,2,1,0:T(8,128)(2,1)}, u32[]{:S(2)}) copy-start(bf16[3,3,64,64]{3,2,1,0:T(8,128)(2,1)} %weight_second) | copy-start | bytes 221188
  19.3 1.5 %collective-permute-start = (bf16[32,32,128]{2,1,0:T(8,128)(2,1)S(1)}, bf16[32,32,128]{2,1,0:T(8,128)(2,1)S(1)}, u32[]{:S(2)}, u32[]{:S(2)}) collective-permute-start(bf16[32,32,128]{2,1,0:T(8,128)(2,1)S(1)} %all_to_all.10.own), channel_id=1, source_target_pairs={{0,1},{1,0},{2,3},{3,2},{4,5},{5,4},{6,7},{7,6},{8,9},{9,8},{10,11... | collective-permute-start | bytes 786440 | tf_op jit(solution)/shard_map/ppermute | solution.py:378
  19.6 0.7 %copy-start.2 = (f32[64]{0:T(128)S(1)}, f32[64]{0:T(128)}, u32[]{:S(2)}) copy-start(f32[64]{0:T(128)} %param.8) | copy-start | bytes 772
  19.6 0.7 %copy-start.3 = (f32[64]{0:T(128)S(1)}, f32[64]{0:T(128)}, u32[]{:S(2)}) copy-start(f32[64]{0:T(128)} %param.10) | copy-start | bytes 772

commit v12 on v11

--- a/solution.py
+++ b/solution.py
@@ -289,7 +289,7 @@
             return (above + taps[:, :, width : 2 * width] + below).reshape(last - first, width)
 
         def runs(total):
-            cut = (total + 1) // 2
+            cut = total * 3 // 5
             return (0, cut), (cut, total)
 
         def columns(value, begin, end):

time: 31 us -> 31 us (level)
  no operation moved by 1% of the time
where the time goes in v12:
time: 31 us; the launch traced here: 30.8 us
  blocking collectives  25.1 us (81%)
  Pallas kernels  1.73 us (6%)
  local copies, waits for them, and re-layouts  1.51 us (5%)
  other arithmetic  1.08 us (3%)
  between operations  0.68 us (2%)
  waiting for transfers between devices  0.39 us (1%)
    all_to_all x1, blocking collectives, by_classes(): own = lax.all_to_all(parts, both, 0, 0, tiled=True)  17.4 us
    all_to_all x1, blocking collectives, by_classes(): lax.all_to_all(result, both, 0, 0, axis_index_groups=halves, tiled=True)  7.72 us
    pallas_call x1, Pallas kernels, class_chains(): pl.pallas_call(functools.partial(class_kernel, row_count, part_cols), out...  1.4 us
    convert_element_type x1, other arithmetic, class_parts(): tile = jnp.concatenate([feature_map, cotangent], 2).astype(jnp.float32)  1.08 us
    slice x1, local copies, waits for them, and re-layouts, by_classes(): return (back[..., :channels], back[..., channels:])  0.77 us
    unnamed x8, local copies, waits for them, and re-layouts  0.67 us
  transfers between devices with their start and end apart: 1, of which 1 were waited for; matrix products, arithmetic and copies ran while one was open for 0% of the time, Pallas kernels for 1%

profile of v12, /device:TPU:0, one launch (start us, length us, event | category | flops | bytes accessed | tf_op | source)
XLA Modules:
  0.0 30.8 jit_solution(13009154681952136024)
XLA Ops:
  0.6 1.1 %maximum_convert_fusion.whole = f32[512,128]{1,0:T(8,128)S(1)} fusion(bf16[512,64]{1,0:T(8,128)(2,1)} %bitcast.14, bf16[512,64]{1,0:T(8,128)(2,1)} %bitcast.15), kind=kLoop, calls=%fused_computation | loop fusion | flops 262144 | bytes 393216 | tf_op jit(solution)/shard_map/convert_element_type | solution.py:187
  1.7 0.2 shard_map.77
  1.9 0.0 copy-start
  1.9 0.0 copy-start.1
  1.9 17.4 %all_to_all.10.own = bf16[32,32,128]{2,1,0:T(8,128)(2,1)S(1)} all-to-all(bf16[32,32,128]{2,1,0:T(8,128)(2,1)S(1)} %bitcast.9), channel_id=1, replica_groups=mesh['row'=2,'col'=16] {'row','col'}, dimensions={0} | all-to-all | bytes 524288 | tf_op jit(solution)/shard_map/all_to_all | solution.py:374
  19.3 0.3 collective-permute-start
  19.6 0.0 copy-start.2
  19.6 0.0 copy-start.3
  19.6 0.0 copy-done
  19.6 0.0 copy-done.1
  19.6 0.6 %copy-done.2 = f32[64]{0:T(128)S(1)} copy-done((f32[64]{0:T(128)S(1)}, f32[64]{0:T(128)}, u32[]{:S(2)}) %copy-start.2) | copy-done | bytes 280
  20.3 0.0 copy-done.3
  20.3 0.2 shard_map.78
  20.5 0.4 %collective-permute-done.other = bf16[32,32,128]{2,1,0:T(8,128)(2,1)S(1)} collective-permute-done((bf16[32,32,128]{2,1,0:T(8,128)(2,1)S(1)}, bf16[32,32,128]{2,1,0:T(8,128)(2,1)S(1)}, u32[]{:S(2)}, u32[]{:S(2)}) %collective-permute-start) | collective-permute-done | bytes 262176 | tf_op jit(solution)/shard_map/ppermute | solution.py:378
  20.8 1.4 %shard_map.79 = bf16[16,32,128]{2,1,0:T(8,128)(2,1)S(1)} custom-call(bf16[32,32,128]{2,1,0:T(8,128)(2,1)S(1)} %all_to_all.10.own, bf16[32,32,128]{2,1,0:T(8,128)(2,1)S(1)} %collective-permute-done.other, bf16[256,384]{1,0:T(8,128)(2,1)S(1)} %get-tuple-element.18.weight_first, bf16[384,384]{1,0:T(8,128)(2,1)S(1)} %get-tuple-element.19.weight_second, ...), custom_call_target="tpu_custom_call" | custom-call | tf_op jit(solution)/shard_map/pallas_call | solution.py:353
  22.2 7.7 %all_to_all.11 = bf16[16,32,128]{2,1,0:T(8,128)(2,1)S(1)} all-to-all(bf16[16,32,128]{2,1,0:T(8,128)(2,1)S(1)} %shard_map.79), channel_id=1, replica_groups={{23,21,19,17,20,22,7,5,18,6,3,1,16,4,0,2},{31,29,27,25,28,30,15,13,26,1..., dimensions={0} | all-to-all | bytes 262144 | tf_op jit(solution)/shard_map/all_to_all | solution.py:386
  30.0 0.1 copy.8
  30.0 0.8 %fusion = (bf16[64,8,64]{2,1,0:T(8,128)(2,1)}, bf16[64,8,64]{2,1,0:T(8,128)(2,1)}) fusion(bf16[64,8,128]{2,1,0:T(8,128)(2,1)S(1)} %bitcast.12), kind=kLoop, calls=%fused_computation.1 | loop fusion | bytes 262144 | tf_op jit(solution)/shard_map/slice | solution.py:389
Async XLA Ops:
  1.9 17.7 %copy-start = (bf16[3,3,64,64]{3,2,1,0:T(8,128)(2,1)S(1)}, bf16[3,3,64,64]{3,2,1,0:T(8,128)(2,1)}, u32[]{:S(2)}) copy-start(bf16[3,3,64,64]{3,2,1,0:T(8,128)(2,1)} %weight_first) | copy-start | bytes 221188
  1.9 17.7 %copy-start.1 = (bf16[3,3,64,64]{3,2,1,0:T(8,128)(2,1)S(1)}, bf16[3,3,64,64]{3,2,1,0:T(8,128)(2,1)}, u32[]{:S(2)}) copy-start(bf16[3,3,64,64]{3,2,1,0:T(8,128)(2,1)} %weight_second) | copy-start | bytes 221188
  19.3 1.5 %collective-permute-start = (bf16[32,32,128]{2,1,0:T(8,128)(2,1)S(1)}, bf16[32,32,128]{2,1,0:T(8,128)(2,1)S(1)}, u32[]{:S(2)}, u32[]{:S(2)}) collective-permute-start(bf16[32,32,128]{2,1,0:T(8,128)(2,1)S(1)} %all_to_all.10.own), channel_id=1, source_target_pairs={{0,1},{1,0},{2,3},{3,2},{4,5},{5,4},{6,7},{7,6},{8,9},{9,8},{10,11... | collective-permute-start | bytes 786440 | tf_op jit(solution)/shard_map/ppermute | solution.py:378
  19.6 0.7 %copy-start.2 = (f32[64]{0:T(128)S(1)}, f32[64]{0:T(128)}, u32[]{:S(2)}) copy-start(f32[64]{0:T(128)} %param.8) | copy-start | bytes 772
  19.6 0.7 %copy-start.3 = (f32[64]{0:T(128)S(1)}, f32[64]{0:T(128)}, u32[]{:S(2)}) copy-start(f32[64]{0:T(128)} %param.10) | copy-start | bytes 772

commit v13 on v9

--- a/solution.py
+++ b/solution.py
@@ -285,7 +285,7 @@
             return (above + taps[:, :, width : 2 * width] + below).reshape(last - first, width)
 
         def runs(total):
-            cut = (total + 1) // 2
+            cut = total // 2
             return (0, cut), (cut, total)
 
         def columns(value, begin, end):

time: 31 us -> 31 us (level)
  no operation moved by 1% of the time
where the time goes in v13:
time: 31 us; the launch traced here: 30.8 us
  blocking collectives  25.1 us (81%)
  Pallas kernels  1.77 us (6%)
  local copies, waits for them, and re-layouts  1.51 us (5%)
  other arithmetic  1.08 us (3%)
  between operations  0.67 us (2%)
  waiting for transfers between devices  0.39 us (1%)
    all_to_all x1, blocking collectives, by_classes(): own = lax.all_to_all(parts, both, 0, 0, tiled=True)  17.4 us
    all_to_all x1, blocking collectives, by_classes(): lax.all_to_all(result, both, 0, 0, axis_index_groups=halves, tiled=True)  7.7 us
    pallas_call x1, Pallas kernels, class_chains(): pl.pallas_call(functools.partial(class_kernel, row_count, part_cols), out...  1.44 us
    convert_element_type x1, other arithmetic, class_parts(): tile = jnp.concatenate([feature_map, cotangent], 2).astype(jnp.float32)  1.08 us
    slice x1, local copies, waits for them, and re-layouts, by_classes(): return (back[..., :channels], back[..., channels:])  0.77 us
    unnamed x8, local copies, waits for them, and re-layouts  0.67 us
  transfers between devices with their start and end apart: 1, of which 1 were waited for; matrix products, arithmetic and copies ran while one was open for 0% of the time, Pallas kernels for 1%

profile of v13, /device:TPU:0, one launch (start us, length us, event | category | flops | bytes accessed | tf_op | source)
XLA Modules:
  0.0 30.8 jit_solution(10992378905943691110)
XLA Ops:
  0.6 1.1 %maximum_convert_fusion.whole = f32[512,128]{1,0:T(8,128)S(1)} fusion(bf16[512,64]{1,0:T(8,128)(2,1)} %bitcast.14, bf16[512,64]{1,0:T(8,128)(2,1)} %bitcast.15), kind=kLoop, calls=%fused_computation | loop fusion | flops 262144 | bytes 393216 | tf_op jit(solution)/shard_map/convert_element_type | solution.py:187
  1.7 0.2 shard_map.77
  1.9 0.0 copy-start
  1.9 0.0 copy-start.1
  1.9 17.4 %all_to_all.10.own = bf16[32,32,128]{2,1,0:T(8,128)(2,1)S(1)} all-to-all(bf16[32,32,128]{2,1,0:T(8,128)(2,1)S(1)} %bitcast.9), channel_id=1, replica_groups=mesh['row'=2,'col'=16] {'row','col'}, dimensions={0} | all-to-all | bytes 524288 | tf_op jit(solution)/shard_map/all_to_all | solution.py:366
  19.3 0.3 collective-permute-start
  19.6 0.0 copy-start.2
  19.6 0.0 copy-start.3
  19.6 0.0 copy-done
  19.6 0.0 copy-done.1
  19.6 0.6 %copy-done.2 = f32[64]{0:T(128)S(1)} copy-done((f32[64]{0:T(128)S(1)}, f32[64]{0:T(128)}, u32[]{:S(2)}) %copy-start.2) | copy-done | bytes 280
  20.3 0.0 copy-done.3
  20.3 0.2 shard_map.78
  20.5 0.4 %collective-permute-done.other = bf16[32,32,128]{2,1,0:T(8,128)(2,1)S(1)} collective-permute-done((bf16[32,32,128]{2,1,0:T(8,128)(2,1)S(1)}, bf16[32,32,128]{2,1,0:T(8,128)(2,1)S(1)}, u32[]{:S(2)}, u32[]{:S(2)}) %collective-permute-start) | collective-permute-done | bytes 262176 | tf_op jit(solution)/shard_map/ppermute | solution.py:370
  20.8 1.4 %shard_map.79 = bf16[16,32,128]{2,1,0:T(8,128)(2,1)S(1)} custom-call(bf16[32,32,128]{2,1,0:T(8,128)(2,1)S(1)} %all_to_all.10.own, bf16[32,32,128]{2,1,0:T(8,128)(2,1)S(1)} %collective-permute-done.other, bf16[256,384]{1,0:T(8,128)(2,1)S(1)} %get-tuple-element.18.weight_first, bf16[384,384]{1,0:T(8,128)(2,1)S(1)} %get-tuple-element.19.weight_second, ...), custom_call_target="tpu_custom_call" | custom-call | tf_op jit(solution)/shard_map/pallas_call | solution.py:345
  22.3 7.7 %all_to_all.11 = bf16[16,32,128]{2,1,0:T(8,128)(2,1)S(1)} all-to-all(bf16[16,32,128]{2,1,0:T(8,128)(2,1)S(1)} %shard_map.79), channel_id=1, replica_groups={{23,21,19,17,20,22,7,5,18,6,3,1,16,4,0,2},{31,29,27,25,28,30,15,13,26,1..., dimensions={0} | all-to-all | bytes 262144 | tf_op jit(solution)/shard_map/all_to_all | solution.py:378
  30.0 0.1 copy.8
  30.1 0.8 %fusion = (bf16[64,8,64]{2,1,0:T(8,128)(2,1)}, bf16[64,8,64]{2,1,0:T(8,128)(2,1)}) fusion(bf16[64,8,128]{2,1,0:T(8,128)(2,1)S(1)} %bitcast.12), kind=kLoop, calls=%fused_computation.1 | loop fusion | bytes 262144 | tf_op jit(solution)/shard_map/slice | solution.py:381
Async XLA Ops:
  1.9 17.7 %copy-start = (bf16[3,3,64,64]{3,2,1,0:T(8,128)(2,1)S(1)}, bf16[3,3,64,64]{3,2,1,0:T(8,128)(2,1)}, u32[]{:S(2)}) copy-start(bf16[3,3,64,64]{3,2,1,0:T(8,128)(2,1)} %weight_first) | copy-start | bytes 221188
  1.9 17.7 %copy-start.1 = (bf16[3,3,64,64]{3,2,1,0:T(8,128)(2,1)S(1)}, bf16[3,3,64,64]{3,2,1,0:T(8,128)(2,1)}, u32[]{:S(2)}) copy-start(bf16[3,3,64,64]{3,2,1,0:T(8,128)(2,1)} %weight_second) | copy-start | bytes 221188
  19.3 1.5 %collective-permute-start = (bf16[32,32,128]{2,1,0:T(8,128)(2,1)S(1)}, bf16[32,32,128]{2,1,0:T(8,128)(2,1)S(1)}, u32[]{:S(2)}, u32[]{:S(2)}) collective-permute-start(bf16[32,32,128]{2,1,0:T(8,128)(2,1)S(1)} %all_to_all.10.own), channel_id=1, source_target_pairs={{0,1},{1,0},{2,3},{3,2},{4,5},{5,4},{6,7},{7,6},{8,9},{9,8},{10,11... | collective-permute-start | bytes 786440 | tf_op jit(solution)/shard_map/ppermute | solution.py:370
  19.6 0.7 %copy-start.2 = (f32[64]{0:T(128)S(1)}, f32[64]{0:T(128)}, u32[]{:S(2)}) copy-start(f32[64]{0:T(128)} %param.8) | copy-start | bytes 772
  19.6 0.7 %copy-start.3 = (f32[64]{0:T(128)S(1)}, f32[64]{0:T(128)}, u32[]{:S(2)}) copy-start(f32[64]{0:T(128)} %param.10) | copy-start | bytes 772
